TPU v7x, 32 devices: a whole 2x2x4 slice. The times are simulated.
32 devices in a mesh: rep: 2 (over x), seq: 8 (over z, y), chan: 2 (over core).
Axes of the slice: x: 2, y: 2, z: 4, core: 2. Of those that a mesh axis runs over, the one named last changes fastest.
Arguments:
- inputs: float32 [32768, 256], P(('rep', 'seq'), 'chan'), parts along dimension 0, may hold values from -6 to 6
- gate_in: float32 [32768, 256], P(('rep', 'seq'), 'chan'), parts along dimension 0, may hold values from -6 to 6
- out_grad: float32 [32768, 256], P(('rep', 'seq'), 'chan'), parts along dimension 0, may hold values from -6 to 6
- w_first: float32 [1024, 1024], P(('seq', 'chan')), may hold values from -0.1875 to 0.1875
- w_second: float32 [16, 16], replicated, may hold values from -1.5 to 1.5
- w_out: float32 [256, 256], replicated, may hold values from -0.375 to 0.375
Outputs:
- input_grad: float32 [32768, 256], P(('rep', 'seq'), 'chan'), parts along dimension 0
- gate_grad: float32 [32768, 256], P(('rep', 'seq'), 'chan'), parts along dimension 0
- first_grad: float32 [2048, 1024], P(('rep', 'seq', 'chan')), parts along dimension 0
- second_grad: float32 [32, 16], P('rep'), parts along dimension 0
There are 2 independent parts, one for each index of `rep`. A program takes and returns all parts, laid end to end along the dimension named above; an argument that names none is the same for every part. Nothing has to cross between parts.
All inputs are finite; a program needn't handle non-finite values.
Results may differ from a plain program's by a relative error of at most 0.00013.
Values sent between devices are 32-bit elements; how exact they have to be, the bound alone decides.
No kernel may reach another device: no remote copies, remote signals or barrier semaphores. Data moves between devices by JAX's collectives and lax.ppermute only.
A program may use at most 64 MiB of HBM per device.

v0:
```python
import math

import jax
import jax.numpy as jnp
from jax import lax
from jax.sharding import PartitionSpec as P

B = 1024
C = 256


def body(inputs, gate_in, out_grad, w_first, w_second, w_out):
    highest = lax.Precision.HIGHEST
    chan_width = inputs.shape[1]
    block_count = inputs.shape[0] // B
    total_blocks = w_second.shape[0]
    blocks = inputs.reshape(block_count, B, chan_width)
    gate_vals = gate_in.reshape(block_count, B, chan_width)
    whole_first = lax.all_gather(w_first, ("seq", "chan"), axis=0, tiled=True)
    tile_vals = jnp.einsum("kj,ijc->ikc", whole_first, blocks, precision=highest)
    own_start = lax.axis_index("chan") * chan_width
    own_rows = lax.dynamic_slice_in_dim(w_out, own_start, chan_width, 0)
    hidden_flat = jnp.dot(
        lax.all_gather(out_grad, "chan", axis=1, tiled=True), own_rows.T, precision=highest
    )
    hidden_grad = hidden_flat.reshape(block_count, B, chan_width)

    def mix_second(matrix, columns):
        flattened = columns.reshape(total_blocks, -1)
        return jnp.dot(matrix, flattened, precision=highest).reshape(columns.shape)

    tile_cols = lax.all_to_all(tile_vals, "seq", split_axis=1, concat_axis=0, tiled=True)
    mixed_cols = mix_second(w_second, tile_cols)
    mixed_vals = lax.all_to_all(mixed_cols, "seq", split_axis=0, concat_axis=1, tiled=True)
    squash = jax.nn.sigmoid(gate_vals)
    mixed_grad = hidden_grad * gate_vals * squash
    gate_grad = hidden_grad * mixed_vals * squash * (1.0 + gate_vals * (1.0 - squash))
    mixed_grad, gate_grad = (mixed_grad, gate_grad)
    grad_cols = lax.all_to_all(mixed_grad, "seq", split_axis=1, concat_axis=0, tiled=True)
    tile_grad_cols = mix_second(w_second.T, grad_cols)
    tile_grad = lax.all_to_all(tile_grad_cols, "seq", split_axis=0, concat_axis=1, tiled=True)
    second_term = jnp.dot(
        grad_cols.reshape(total_blocks, -1),
        tile_cols.reshape(total_blocks, -1).T,
        precision=highest,
    ) * (1.0 / math.sqrt(B * C))
    second_grad = lax.psum(second_term, ("seq", "chan"))
    input_grad = jnp.einsum("kj,ikc->ijc", whole_first, tile_grad, precision=highest).reshape(
        inputs.shape
    )
    first_scale = 1.0 / math.sqrt(total_blocks * C)
    first_grad = lax.psum_scatter(
        jnp.einsum("ikc,ijc->kj", tile_grad, blocks, precision=highest) * first_scale,
        ("seq", "chan"),
        scatter_dimension=0,
        tiled=True,
    )
    return (input_grad, gate_grad.reshape(inputs.shape), first_grad, second_grad)


def solution(mesh):
    return jax.shard_map(
        body,
        mesh=mesh,
        in_specs=(
            P(("rep", "seq"), "chan"),
            P(("rep", "seq"), "chan"),
            P(("rep", "seq"), "chan"),
            P(("seq", "chan"), None),
            P(),
            P(),
        ),
        out_specs=(
            P(("rep", "seq"), "chan"),
            P(("rep", "seq"), "chan"),
            P(("rep", "seq", "chan"), None),
            P("rep", None),
        ),
        check_vma=False,
    )
```

profile of v0, /device:TPU:0, one launch (start us, length us, event | category | flops | bytes accessed | tf_op | source)
XLA Modules:
  0.0 302.4 jit_solution(9653559817584949188)
XLA Ops:
  8.0 0.0 copy-start
  8.0 0.0 all-gather.5.cloned.1.call-start
  8.1 0.7 all-gather.5.cloned.1.call-update
  8.7 55.6 %all-gather.5.cloned.1.call-done = f32[1024,1024]{1,0:T(8,128)} async-done(((f32[64,1024]{1,0:T(8,128)}), f32[1024,1024]{1,0:T(8,128)}) %all-gather.5.cloned.1.call-update) | async-done | bytes 4194320 | tf_op jit(solution)/shard_map/all_gather | solution.py:19
  64.3 0.0 copy-done
  64.3 8.7 %fusion.7 = f32[2,1024,128]{1,2,0:T(8,128)S(1)} fusion(f32[2,1024,128]{2,1,0:T(8,128)S(1)} %bitcast.74, f32[1024,1024]{1,0:T(8,128)} %all-gather.5.cloned.1.call-done), kind=kOutput, calls=%fused_computation.7 | convolution fusion | flops 3221225472 | bytes 6291456 | tf_op jit(solution)/shard_map/kj,ijc->ikc/dot_general | solution.py:20
  73.0 0.0 copy-start.1
  73.0 1.3 copy.47
  74.3 3.6 %all-to-all-start.2 = ((f32[2,1024,128]{2,0,1:T(2,128)}), f32[2,1024,128]{2,0,1:T(2,128)S(1)}, u32[]{:S(2)}, u32[]{:S(2)}) async-start(f32[2,1024,128]{2,0,1:T(2,128)} %copy.47), calls=%async_computation.2 | async-start | bytes 2097152 | tf_op jit(solution)/shard_map/all_to_all | solution.py:32
  77.9 0.0 all-gather.3.cloned.1.call-start
  77.9 0.5 all-gather.3.cloned.1.call-update
  78.5 25.8 %all-to-all-done.2 = f32[2,1024,128]{2,0,1:T(2,128)S(1)} async-done(((f32[2,1024,128]{2,0,1:T(2,128)}), f32[2,1024,128]{2,0,1:T(2,128)S(1)}, u32[]{:S(2)}, u32[]{:S(2)}) %all-to-all-start.2) | async-done | bytes 1048608 | tf_op jit(solution)/shard_map/all_to_all | solution.py:32
  104.3 0.1 copy.48
  104.4 0.0 copy-done.1
  104.4 1.6 convolution_bitcast_fusion.1
  106.0 0.0 copy-start.2
  106.0 1.2 copy.58
  107.2 3.6 %all-to-all-start.3 = ((f32[16,128,128]{2,1,0:T(8,128)}), f32[16,128,128]{2,1,0:T(8,128)S(1)}, u32[]{:S(2)}, u32[]{:S(2)}) async-start(f32[16,128,128]{2,1,0:T(8,128)} %bitcast.81), calls=%async_computation.3 | async-start | bytes 2097152 | tf_op jit(solution)/shard_map/all_to_all | solution.py:34
  110.8 0.0 reduce-scatter.2.cloned.1.call-start
  110.9 2.5 copy.39
  113.4 23.4 %all-to-all-done.3 = f32[16,128,128]{2,1,0:T(8,128)S(1)} async-done(((f32[16,128,128]{2,1,0:T(8,128)}), f32[16,128,128]{2,1,0:T(8,128)S(1)}, u32[]{:S(2)}, u32[]{:S(2)}) %all-to-all-start.3) | async-done | bytes 1048608 | tf_op jit(solution)/shard_map/all_to_all | solution.py:34
  136.8 1.4 copy.49
  138.2 0.0 all-gather.3.cloned.1.call-done
  138.2 0.0 copy-done.2
  138.2 6.1 %fusion.11 = (f32[2048,128]{0,1:T(8,128)}, f32[2048,128]{0,1:T(8,128)}) fusion(f32[16,8,16,128]{3,2,1,0:T(8,128)} %bitcast.88, f32[2048,128]{0,1:T(8,128)} %copy.39, f32[2048,256]{1,0:T(8,128)} %all-gather.3.cloned.1.call-done, f32[256,256]{1,0:T(8,128)S(1)} %copy-done.2, s32[]{:T(128)S(6)} %select_n.3), kind=kOutput, calls=%fused_computation.13 | convolution fusion | flops 808189952 | bytes 6422532 | tf_op jit(solution)/shard_map/dot_general | solution.py:23
  144.3 2.1 reshape.50
  146.4 2.0 copy.41
  148.3 29.5 %all_to_all.66 = f32[2,1024,128]{2,0,1:T(2,128)S(1)} all-to-all(f32[2,1024,128]{2,0,1:T(2,128)} %copy.41), channel_id=1, replica_groups=mesh['rep'=2,'seq'=8,'chan'=2] {'seq'}, dimensions={1} | all-to-all | bytes 2097152 | tf_op jit(solution)/shard_map/all_to_all | solution.py:39
  177.9 0.1 copy.42
  177.9 0.1 copy.43
  178.0 1.6 convolution_bitcast_fusion.2
  179.6 0.2 copy.56
  179.9 29.0 %all_to_all.67 = f32[16,128,128]{2,1,0:T(8,128)} all-to-all(f32[16,128,128]{2,1,0:T(8,128)S(1)} %bitcast.84), channel_id=1, replica_groups=mesh['rep'=2,'seq'=8,'chan'=2] {'seq'}, dimensions={0} | all-to-all | bytes 2097152 | tf_op jit(solution)/shard_map/all_to_all | solution.py:41
  208.9 2.5 copy.44
  211.4 2.4 all_to_all.54
  213.8 9.5 %bitcast_multiply_fusion = f32[1024,1024]{1,0:T(8,128)} fusion(f32[2,1024,128]{1,2,0:T(8,128)} %all_to_all.54, f32[2,1024,128]{2,1,0:T(8,128)S(1)} %bitcast.75), kind=kOutput, calls=%fused_computation | convolution fusion | flops 3222274048 | bytes 6291456 | tf_op jit(solution)/shard_map/ikc,ijc->kj/dot_general | solution.py:53
  223.3 0.0 reduce-scatter.2.cloned.1.call-update
  223.3 2.5 copy.52
  225.9 2.5 convolution_multiply_fusion
  228.3 32.2 %psum.7 = f32[16,16]{1,0:T(8,128)} all-reduce(f32[16,16]{1,0:T(8,128)S(1)} %convolution_multiply_fusion), channel_id=1, replica_groups=mesh['rep'=2,'seq'=8,'chan'=2] {'seq','chan'}, use_global_device_ids=true, to_apply=%region_1.0 | all-reduce | flops 256 | bytes 2048 | tf_op jit(solution)/shard_map/psum | solution.py:47
  260.5 6.0 %fusion.4 = f32[2,1024,128]{1,2,0:T(8,128)S(1)} fusion(f32[2,1024,128]{1,2,0:T(8,128)} %all_to_all.54, f32[1024,1024]{1,0:T(8,128)} %all-gather.5.cloned.1.call-done), kind=kOutput, calls=%fused_computation.6 | convolution fusion | flops 3221225472 | bytes 6291456 | tf_op jit(solution)/shard_map/kj,ikc->ijc/dot_general | solution.py:48
  266.5 1.3 copy.45
  267.8 27.1 %reduce-scatter.2.cloned.1.call-done = f32[64,1024]{1,0:T(8,128)} async-done(((f32[1024,1024]{1,0:T(8,128)}), f32[64,1024]{1,0:T(8,128)}) %reduce-scatter.2.cloned.1.call-update) | async-done | bytes 262160 | tf_op jit(solution)/shard_map/reduce_scatter | solution.py:52
Async XLA Ops:
  8.0 56.3 %copy-start = (f32[2048,128]{1,0:T(8,128)S(1)}, f32[2048,128]{1,0:T(8,128)}, u32[]{:S(2)}) copy-start(f32[2048,128]{1,0:T(8,128)} %param.6) | copy-start | bytes 3145732
  8.0 56.3 %all-gather.5.cloned.1.call-start = ((), (), s32[]{:S(2)}) async-start(), calls=%async_computation.6 | async-start | bytes 4456448 | tf_op jit(solution)/shard_map/all_gather | solution.py:19
  73.0 31.4 %copy-start.1 = (f32[16,16]{1,0:T(8,128)S(1)}, f32[16,16]{1,0:T(8,128)}, u32[]{:S(2)}) copy-start(f32[16,16]{1,0:T(8,128)} %param.10) | copy-start | bytes 3076
  74.3 29.9 %all-to-all-start.2 = ((f32[2,1024,128]{2,0,1:T(2,128)}), f32[2,1024,128]{2,0,1:T(2,128)S(1)}, u32[]{:S(2)}, u32[]{:S(2)}) async-start(f32[2,1024,128]{2,0,1:T(2,128)} %copy.47), calls=%async_computation.2 | async-start | bytes 2097152 | tf_op jit(solution)/shard_map/all_to_all | solution.py:32
  77.9 60.3 %all-gather.3.cloned.1.call-start = ((), (), s32[]{:S(2)}) async-start(), calls=%async_computation.5 | async-start | bytes 3145728 | tf_op jit(solution)/shard_map/all_gather | solution.py:24
  106.0 32.2 %copy-start.2 = (f32[256,256]{1,0:T(8,128)S(1)}, f32[256,256]{1,0:T(8,128)}, u32[]{:S(2)}) copy-start(f32[256,256]{1,0:T(8,128)} %param.11) | copy-start | bytes 786436
  107.2 29.6 %all-to-all-start.3 = ((f32[16,128,128]{2,1,0:T(8,128)}), f32[16,128,128]{2,1,0:T(8,128)S(1)}, u32[]{:S(2)}, u32[]{:S(2)}) async-start(f32[16,128,128]{2,1,0:T(8,128)} %bitcast.81), calls=%async_computation.3 | async-start | bytes 2097152 | tf_op jit(solution)/shard_map/all_to_all | solution.py:34
  110.8 184.1 %reduce-scatter.2.cloned.1.call-start = ((), (), s32[]{:S(2)}) async-start(), calls=%async_computation.7 | async-start | bytes 4456448 | tf_op jit(solution)/shard_map/reduce_scatter | solution.py:52
Sparse Core Ops, SparseCore 0:
  11.0 53.2 all-gather.4
  223.5 71.4 reduce-scatter.1
Sparse Core Ops, SparseCore 1:
  79.9 11.5 all-gather.2
where the time goes:
time: 303 us; the launch traced here: 302 us
  waiting for transfers between devices  133 us (44%)
  blocking collectives  90.7 us (30%)
  matrix products  35.9 us (12%)
  local copies, waits for them, and re-layouts  19.7 us (7%)
  between operations  15.6 us (5%)
  starting transfers between devices  7.3 us (2%)
    all_gather x1, waiting for transfers between devices, body(): whole_first = lax.all_gather(w_first, ('seq', 'chan'), axis=0, tiled=True)  55.6 us
    psum x1, blocking collectives, body(): second_grad = lax.psum(second_term, ('seq', 'chan'))  32.2 us
    all_to_all x1, blocking collectives, body(): lax.all_to_all(mixed_grad, 'seq', split_axis=1, concat_axis=0, tiled=True)  29.5 us
    all_to_all x1, blocking collectives, body(): lax.all_to_all(tile_grad_cols, 'seq', split_axis=0, concat_axis=1, tiled=...  29 us
    reduce_scatter x1, waiting for transfers between devices, body(): lax.psum_scatter(jnp.einsum('ikc,ijc->kj', tile_grad, blocks, precision=h...  27.1 us
    all_to_all x1, waiting for transfers between devices, body(): lax.all_to_all(tile_vals, 'seq', split_axis=1, concat_axis=0, tiled=True)  25.8 us
    all_to_all x1, waiting for transfers between devices, body(): lax.all_to_all(mixed_cols, 'seq', split_axis=0, concat_axis=1, tiled=True)  23.4 us
    dot_general x1, matrix products, body(): jnp.einsum('ikc,ijc->kj', tile_grad, blocks, precision=highest)  9.47 us
  transfers between devices with their start and end apart: 5, of which 4 were waited for; matrix products, arithmetic and copies ran while one was open for 6% of the time, Pallas kernels for 0%

commit v1 on v0

v1 whole, which is shorter than its diff:
```python
import functools
import math

import jax
import jax.numpy as jnp
from jax import lax
from jax.experimental import pallas as pl
from jax.experimental.pallas import tpu as pltpu
from jax.sharding import PartitionSpec as P

F32 = jnp.float32
BF16 = jnp.bfloat16
NN = (((1,), (0,)), ((), ()))
NT = (((1,), (1,)), ((), ()))
TN = (((0,), (0,)), ((), ()))
VMEM_LIMIT = 48 * 1024 * 1024


def split(x):
    hi = x.astype(BF16)
    return hi, (x - hi.astype(F32)).astype(BF16)


def dot3(a, b, dims):
    (ah, al), (bh, bl) = a, b

    def d(u, v):
        return lax.dot_general(u, v, dims, preferred_element_type=F32)

    return d(ah, bh) + (d(ah, bl) + d(al, bh))


def params():
    return pltpu.CompilerParams(vmem_limit_bytes=VMEM_LIMIT)


def cost(flops, size):
    return pl.CostEstimate(flops=flops, bytes_accessed=size, transcendentals=0)


def gate_kernel(own_ref, other_ref, gate_ref, w_ref, grad_ref, factor_ref):
    cot = jnp.concatenate([own_ref[...], other_ref[...]], axis=1)
    hidden = dot3(split(cot), split(w_ref[...]), NT)
    g = gate_ref[...]
    s = jax.nn.sigmoid(g)
    hs = hidden * s
    grad_ref[...] = hs * g
    factor_ref[...] = hs * (1.0 + g * (1.0 - s))


def gate_call(own, other, gate, w):
    rows, width = own.shape
    tile = rows // 4
    row = pl.BlockSpec((tile, width), lambda i: (i, 0))
    shape = jax.ShapeDtypeStruct(own.shape, F32)
    return pl.pallas_call(
        gate_kernel,
        grid=(4,),
        in_specs=[row, row, row, pl.BlockSpec(w.shape, lambda i: (0, 0))],
        out_specs=[row, row],
        out_shape=[shape, shape],
        compiler_params=params(),
        cost_estimate=cost(6 * rows * width * 2 * width, 5 * 4 * rows * width),
        name="gate",
    )(own, other, gate, w)


def grouped(ref, group):
    n, span, width = ref.shape
    return jnp.concatenate(
        [ref[:, g * group : (g + 1) * group, :].reshape(n * group, width) for g in range(span // group)], axis=1
    )


def scatter_groups(ref, group, val):
    n, span, width = ref.shape
    for g in range(span // group):
        ref[:, g * group : (g + 1) * group, :] = val[:, g * width : (g + 1) * width].reshape(n, group, width)


def mix_kernel(group, k_ref, x_ref, o_ref):
    x = grouped(x_ref, group)
    scatter_groups(o_ref, group, dot3(split(k_ref[...]), split(x), NN))


def mix_second_kernel(group, scale, k_ref, u_ref, b_ref, o_ref, s_ref, acc):
    step = pl.program_id(0)
    u = split(grouped(u_ref, group))
    b = split(grouped(b_ref, group))
    scatter_groups(o_ref, group, dot3(split(k_ref[...]), u, NN))

    @pl.when(step == 0)
    def _():
        acc[...] = jnp.zeros_like(acc)

    acc[...] += dot3(u, b, NT)

    @pl.when(step == pl.num_programs(0) - 1)
    def _():
        size = acc.shape[0]
        n = size // group
        r = lax.broadcasted_iota(jnp.int32, (size, size), 0)
        c = lax.broadcasted_iota(jnp.int32, (size, size), 1)
        diag = jnp.where(lax.rem(r, group) == lax.rem(c, group), acc[...], 0.0)
        rows = jnp.sum(diag.reshape(n, group, size), axis=1)
        pick_r = lax.broadcasted_iota(jnp.int32, (size, n), 0)
        pick_c = lax.broadcasted_iota(jnp.int32, (size, n), 1)
        pick = (lax.div(pick_r, group) == pick_c).astype(F32)
        s_ref[...] = jnp.dot(rows, pick, precision=lax.Precision.HIGHEST, preferred_element_type=F32) * scale


def mix_call(kron, x, group):
    n, width, chan = x.shape
    span = min(width, 2 * group)
    block = pl.BlockSpec((n, span, chan), lambda i: (0, i, 0))
    size = kron.shape[0]
    return pl.pallas_call(
        functools.partial(mix_kernel, group),
        grid=(width // span,),
        in_specs=[pl.BlockSpec(kron.shape, lambda i: (0, 0)), block],
        out_specs=block,
        out_shape=jax.ShapeDtypeStruct(x.shape, F32),
        compiler_params=params(),
        cost_estimate=cost(6 * size * n * width * chan, 8 * n * width * chan),
        name="mix",
    )(kron, x)


def mix_second_call(kron, u, b, group, scale):
    n, width, chan = u.shape
    span = min(width, 2 * group)
    block = pl.BlockSpec((n, span, chan), lambda i: (0, i, 0))
    size = kron.shape[0]
    return pl.pallas_call(
        functools.partial(mix_second_kernel, group, scale),
        grid=(width // span,),
        in_specs=[pl.BlockSpec(kron.shape, lambda i: (0, 0)), block, block],
        out_specs=[block, pl.BlockSpec((n, n), lambda i: (0, 0))],
        out_shape=[jax.ShapeDtypeStruct(u.shape, F32), jax.ShapeDtypeStruct((n, n), F32)],
        scratch_shapes=[pltpu.VMEM((size, size), F32)],
        compiler_params=params(),
        cost_estimate=cost(12 * size * n * width * chan, 12 * n * width * chan),
        name="mix_second",
    )(kron, u, b)


def place_kernel(offsets, s_ref, h_ref, *refs):
    pieces = refs[: 2 * len(offsets)]
    hi_ref, lo_ref, whole, sem = refs[2 * len(offsets) :]
    unit = pieces[0].shape[1]
    copies = []
    for side in range(2):
        for piece, rels in zip(pieces[side * len(offsets) :], offsets):
            for u, rel in enumerate(rels):
                place = 2 * lax.bitwise_xor(s_ref[0], rel) + lax.bitwise_xor(h_ref[0], side)
                start = pl.multiple_of(place * unit, unit)
                copies.append(
                    pltpu.make_async_copy(piece.at[u], whole.at[pl.ds(start, unit)], sem.at[len(copies)])
                )
    for c in copies:
        c.start()
    for c in copies:
        c.wait()
    rows = whole.shape[0]
    tile = 256
    for t in range(rows // tile):
        hi, lo = split(whole[t * tile : (t + 1) * tile, :])
        hi_ref[t * tile : (t + 1) * tile, :] = hi
        lo_ref[t * tile : (t + 1) * tile, :] = lo


def place_call(seq_id, chan_id, pieces, offsets, rows, columns):
    shape = jax.ShapeDtypeStruct((rows, columns), BF16)
    smem = pl.BlockSpec(memory_space=pltpu.SMEM)
    vmem = pl.BlockSpec(memory_space=pltpu.VMEM)
    return pl.pallas_call(
        functools.partial(place_kernel, offsets),
        in_specs=[smem, smem] + [pl.BlockSpec(memory_space=pl.ANY)] * len(pieces),
        out_specs=[vmem, vmem],
        out_shape=[shape, shape],
        scratch_shapes=[pltpu.VMEM((rows, columns), F32), pltpu.SemaphoreType.DMA((2 * sum(map(len, offsets)),))],
        compiler_params=params(),
        cost_estimate=cost(rows * columns, 8 * rows * columns),
        name="place",
    )(seq_id, chan_id, *pieces)


def up_kernel(hi_ref, lo_ref, g_ref, o_ref, gh, gl):
    @pl.when(pl.program_id(0) == 0)
    def _():
        both = jnp.concatenate([g_ref[m] for m in range(g_ref.shape[0])], axis=1)
        gh[...], gl[...] = split(both)

    res = dot3((hi_ref[...], lo_ref[...]), (gh[...], gl[...]), TN)
    slices, blocks, width, chan = o_ref.shape
    for t in range(slices):
        for m in range(blocks):
            o_ref[t, m] = res[t * width : (t + 1) * width, m * chan : (m + 1) * chan]


def up_call(hi, lo, grad, slices):
    blocks, rows, chan = grad.shape
    tile = 256
    width = rows // slices
    per = tile // width
    wspec = pl.BlockSpec((rows, tile), lambda i: (0, i))
    return pl.pallas_call(
        up_kernel,
        grid=(rows // tile,),
        in_specs=[wspec, wspec, pl.BlockSpec(grad.shape, lambda i: (0, 0, 0))],
        out_specs=pl.BlockSpec((per, blocks, width, chan), lambda i: (i, 0, 0, 0)),
        out_shape=jax.ShapeDtypeStruct((slices, blocks, width, chan), F32),
        scratch_shapes=[pltpu.VMEM((rows, blocks * chan), BF16)] * 2,
        compiler_params=params(),
        cost_estimate=cost(6 * rows * rows * blocks * chan, 4 * rows * rows + 8 * rows * blocks * chan),
        name="up",
    )(hi, lo, grad)


def join(ref):
    slices, blocks = ref.shape[0], ref.shape[1]
    return jnp.concatenate(
        [jnp.concatenate([ref[t, m] for m in range(blocks)], axis=1) for t in range(slices)], axis=0
    )


def mixed_kernel(hi_ref, lo_ref, v_ref, f_ref, o_ref, vh, vl):
    @pl.when(pl.program_id(0) == 0)
    def _():
        vh[...], vl[...] = split(join(v_ref))

    res = dot3((hi_ref[...], lo_ref[...]), (vh[...], vl[...]), NN)
    chan = o_ref.shape[2]
    for m in range(o_ref.shape[0]):
        o_ref[m] = res[:, m * chan : (m + 1) * chan] * f_ref[m]


def mixed_call(hi, lo, v, factor):
    blocks, rows, chan = factor.shape
    tile = 256
    wspec = pl.BlockSpec((tile, rows), lambda i: (i, 0))
    ospec = pl.BlockSpec((blocks, tile, chan), lambda i: (0, i, 0))
    return pl.pallas_call(
        mixed_kernel,
        grid=(rows // tile,),
        in_specs=[wspec, wspec, pl.BlockSpec(v.shape, lambda i: (0, 0, 0, 0)), ospec],
        out_specs=ospec,
        out_shape=jax.ShapeDtypeStruct(factor.shape, F32),
        scratch_shapes=[pltpu.VMEM((rows, blocks * chan), BF16)] * 2,
        compiler_params=params(),
        cost_estimate=cost(6 * rows * rows * blocks * chan, 4 * rows * rows + 12 * rows * blocks * chan),
        name="mixed",
    )(hi, lo, v, factor)


def flip_bits(q, bits):
    r = 0
    for b in range(bits):
        r |= ((q >> b) & 1) << (bits - 1 - b)
    return r


def first_kernel(bits, s_ref, ga_ref, gb_ref, va_ref, vb_ref, keep_ref, send_ref, lh, ll):
    count, unit = ga_ref.shape[1], ga_ref.shape[2]
    blocks = ga_ref.shape[0]

    @pl.when(pl.program_id(0) == 0)
    def _():
        for q in range(count):
            src = lax.bitwise_xor(s_ref[0], flip_bits(q, bits))
            row = jnp.concatenate([r[m, src] for m in range(blocks) for r in (ga_ref, gb_ref)], axis=1)
            lh[q * unit : (q + 1) * unit, :], ll[q * unit : (q + 1) * unit, :] = split(row)

    v = jnp.concatenate(
        [
            jnp.concatenate([r[t, m] for m in range(blocks) for r in (va_ref, vb_ref)], axis=1)
            for t in range(va_ref.shape[0])
        ],
        axis=0,
    )
    res = dot3((lh[...], ll[...]), split(v), NT)
    half = count // 2
    for q in range(half):
        keep_ref[q] = res[q * unit : (q + 1) * unit, :]
        send_ref[q] = res[(half + q) * unit : (half + q + 1) * unit, :]


def first_call(seq_id, grad_own, grad_other, v_own, v_other):
    blocks, count, unit, chan = grad_own.shape
    slices, _, width, _ = v_own.shape
    rows = slices * width
    tile = 256
    per = tile // width
    bits = count.bit_length() - 1
    gspec = pl.BlockSpec(grad_own.shape, lambda i: (0, 0, 0, 0))
    vspec = pl.BlockSpec((per, blocks, width, chan), lambda i: (i, 0, 0, 0))
    ospec = pl.BlockSpec((count // 2, unit, tile), lambda i: (0, 0, i))
    shape = jax.ShapeDtypeStruct((count // 2, unit, rows), F32)
    depth = 2 * blocks * chan
    return pl.pallas_call(
        functools.partial(first_kernel, bits),
        grid=(rows // tile,),
        in_specs=[pl.BlockSpec(memory_space=pltpu.SMEM), gspec, gspec, vspec, vspec],
        out_specs=[ospec, ospec],
        out_shape=[shape, shape],
        scratch_shapes=[pltpu.VMEM((count * unit, depth), BF16)] * 2,
        compiler_params=params(),
        cost_estimate=cost(6 * rows * count * unit * depth, 4 * (rows * count * unit + 2 * rows * depth)),
        name="first",
    )(seq_id, grad_own, grad_other, v_own, v_other)


def body(seq_count, inputs, gate_in, out_grad, w_first, w_second, w_out):
    total = w_second.shape[0]
    own = total // seq_count
    rows = inputs.shape[0] // own
    chan = inputs.shape[1]
    width = rows // seq_count
    unit, columns = w_first.shape
    bits = seq_count.bit_length() - 1
    s = lax.axis_index("seq").astype(jnp.int32)
    h = lax.axis_index("chan").astype(jnp.int32)
    seq_id, chan_id = s.reshape(1), h.reshape(1)
    group = 16 if total * 16 <= 256 else 8

    def swap_core(x):
        return lax.ppermute(x, "chan", [(0, 1), (1, 0)])

    def swap_seq(x, bit):
        return lax.ppermute(x, "seq", [(i, i ^ bit) for i in range(seq_count)])

    def exchange(x):
        return lax.all_to_all(x, "seq", split_axis=0, concat_axis=0, tiled=True)

    other_cot = swap_core(out_grad)
    eye = jnp.eye(group, dtype=F32)
    kron = (w_second[:, None, :, None] * eye[None, :, None, :]).reshape(total * group, total * group)
    kron_t = (w_second.T[:, None, :, None] * eye[None, :, None, :]).reshape(total * group, total * group)

    sliced = inputs.reshape(own, seq_count, width, chan).transpose(1, 0, 2, 3)
    block_cols = exchange(sliced).reshape(total, width, chan)
    v_cols = mix_call(kron, block_cols, group)
    v = exchange(v_cols.reshape(seq_count, own, width, chan))

    pieces, offsets = [w_first.reshape(1, unit, columns)], [(0,)]
    for b in reversed(range(bits)):
        held = pieces[0] if len(pieces) == 1 else jnp.concatenate(pieces, axis=0)
        pieces.append(swap_seq(held, 1 << b))
        offsets.append(tuple(r ^ (1 << b) for r in sum(offsets, ())))

    own_rows = lax.dynamic_slice_in_dim(w_out, h * chan, chan, 0)
    w_cat = jnp.concatenate(
        [
            lax.dynamic_slice_in_dim(own_rows, h * chan, chan, 1),
            lax.dynamic_slice_in_dim(own_rows, (1 - h) * chan, chan, 1),
        ],
        axis=1,
    )
    grad, factor = gate_call(out_grad, other_cot, gate_in, w_cat)
    by_core = grad.reshape(own, seq_count, 2, unit, chan)
    grad_own = lax.dynamic_index_in_dim(by_core, h, 2, keepdims=False)
    grad_other = swap_core(lax.dynamic_index_in_dim(by_core, 1 - h, 2, keepdims=False))

    far = [swap_core(p) for p in pieces]
    hi, lo = place_call(seq_id, chan_id, pieces + far, tuple(offsets), rows, columns)
    u = up_call(hi, lo, grad.reshape(own, rows, chan), seq_count)
    u_cols = exchange(u).reshape(total, width, chan)
    in_cols, second = mix_second_call(kron_t, u_cols, block_cols, group, 1.0 / math.sqrt(rows * 2 * chan))
    back = exchange(in_cols.reshape(seq_count, own, width, chan))
    input_grad = back.transpose(1, 0, 2, 3).reshape(inputs.shape)
    second = second + swap_core(second)
    for b in range(bits):
        second = second + swap_seq(second, 1 << b)

    gate_grad = mixed_call(hi, lo, v, factor.reshape(own, rows, chan)).reshape(inputs.shape)
    keep, send = first_call(seq_id, grad_own, grad_other, v, swap_core(v))
    for b in range(bits):
        keep = keep + swap_seq(send, 1 << b)
        if b + 1 < bits:
            half = keep.shape[0] // 2
            keep, send = keep[:half], keep[half:]
    first_grad = keep.reshape(unit, columns) * (1.0 / math.sqrt(total * 2 * chan))
    return input_grad, gate_grad, first_grad, second


def solution(mesh):
    return jax.shard_map(
        functools.partial(body, mesh.shape["seq"]),
        mesh=mesh,
        in_specs=(
            P(("rep", "seq"), "chan"),
            P(("rep", "seq"), "chan"),
            P(("rep", "seq"), "chan"),
            P(("seq", "chan"), None),
            P(),
            P(),
        ),
        out_specs=(
            P(("rep", "seq"), "chan"),
            P(("rep", "seq"), "chan"),
            P(("rep", "seq", "chan"), None),
            P("rep", None),
        ),
        check_vma=False,
    )
```

time: 303 us -> 211 us (0.70)
  blocking collectives: 90.7 us -> 0 us
  matrix products: 35.9 us -> 0 us
  starting transfers between devices: 7.3 us -> 39.7 us
  Pallas kernels: 0 us -> 29.3 us
  waiting for transfers between devices: 133 us -> 115 us
  between operations: 15.6 us -> 0.89 us
  other arithmetic: 0 us -> 8.27 us
    ppermute x0 -> x17, waiting for transfers between devices: none -> 102 us  [the longest x9 97.7 us: swap_seq(): return lax.ppermute(x, 'seq', [(i, i ^ bit) for i in range(seq_count)])]
    all_to_all x2 -> x0, blocking collectives: 58.5 us -> none  [the longest x1 29.5 us: body(): lax.all_to_all(mixed_grad, 'seq', split_axis=1, concat_axis=0, tiled=True)]
    all_gather x2 -> x0, waiting for transfers between devices: 55.6 us -> none  [the longest x1 55.6 us: body(): whole_first = lax.all_gather(w_first, ('seq', 'chan'), axis=0, tiled=True)]
    dot_general x7 -> x0, matrix products: 35.9 us -> none  [the longest x1 9.47 us: body(): jnp.einsum('ikc,ijc->kj', tile_grad, blocks, precision=highest)]
    all_to_all x2 -> x4, waiting for transfers between devices: 49.2 us -> 13.4 us  [exchange(): return lax.all_to_all(x, 'seq', split_axis=0, concat_axis=0, tiled=True)]
    psum x1 -> x0, blocking collectives: 32.2 us -> none  [body(): second_grad = lax.psum(second_term, ('seq', 'chan'))]
    pallas_call x0 -> x7, Pallas kernels: none -> 29.3 us  [the longest x1 5.09 us: up_call(): pl.pallas_call(up_kernel, grid=(rows // tile,), in_specs=[wspec, wspec, p...]
    reduce_scatter x1 -> x0, waiting for transfers between devices: 27.1 us -> none  [body(): lax.psum_scatter(jnp.einsum('ikc,ijc->kj', tile_grad, blocks, precision=h...]
  transfers between devices with their start and end apart: 5 -> 21, of which waited for: 4 -> 10; matrix products, arithmetic and copies ran while one was open for 6% -> 8% of each run, Pallas kernels for 0% -> 14%
where the time goes in v1:
time: 211 us; the launch traced here: 210 us
  waiting for transfers between devices  115 us (55%)
  starting transfers between devices  39.7 us (19%)
  Pallas kernels  29.3 us (14%)
  local copies, waits for them, and re-layouts  16.8 us (8%)
  other arithmetic  8.27 us (4%)
    ppermute x9, waiting for transfers between devices, swap_seq(): return lax.ppermute(x, 'seq', [(i, i ^ bit) for i in range(seq_count)])  97.7 us
    all_to_all x4, starting transfers between devices, exchange(): return lax.all_to_all(x, 'seq', split_axis=0, concat_axis=0, tiled=True)  21.1 us
    ppermute x9, starting transfers between devices, swap_seq(): return lax.ppermute(x, 'seq', [(i, i ^ bit) for i in range(seq_count)])  17 us
    all_to_all x4, waiting for transfers between devices, exchange(): return lax.all_to_all(x, 'seq', split_axis=0, concat_axis=0, tiled=True)  13.4 us
    unnamed x20, local copies, waits for them, and re-layouts  5.98 us
    pallas_call x1, Pallas kernels, up_call(): pl.pallas_call(up_kernel, grid=(rows // tile,), in_specs=[wspec, wspec, p...  5.09 us
    pallas_call x1, Pallas kernels, mixed_call(): pl.pallas_call(mixed_kernel, grid=(rows // tile,), in_specs=[wspec, wspec...  4.85 us
    pallas_call x1, Pallas kernels, first_call(): pl.pallas_call(functools.partial(first_kernel, bits), grid=(rows // tile,...  4.74 us
  transfers between devices with their start and end apart: 21, of which 10 were waited for; matrix products, arithmetic and copies ran while one was open for 8% of the time, Pallas kernels for 14%

profile of v1, /device:TPU:0, one launch (start us, length us, event | category | flops | bytes accessed | tf_op | source)
XLA Modules:
  0.0 210.0 jit_solution(169212281209249151)
XLA Ops:
  0.6 2.3 %copy.18 = f32[2,8,128,128]{3,2,0,1:T(8,128)} copy(f32[2,8,128,128]{3,2,1,0:T(8,128)} %bitcast.44) | data formatting | bytes 2097152 | tf_op jit(solution)/shard_map/reshape | solution.py:340
  3.0 7.3 %all-to-all-start.1 = ((f32[8,2,128,128]{3,2,1,0:T(8,128)}), f32[8,2,128,128]{3,2,1,0:T(8,128)S(1)}, u32[]{:S(2)}, u32[]{:S(2)}) async-start(f32[8,2,128,128]{3,2,1,0:T(8,128)} %bitcast.31), calls=%async_computation.1 | async-start | bytes 2097152 | tf_op jit(solution)/shard_map/all_to_all | solution.py:333
  10.3 3.0 %collective-permute-start = (f32[1,64,1024]{2,1,0:T(8,128)S(1)}, f32[1,64,1024]{2,1,0:T(8,128)}, u32[]{:S(2)}, u32[]{:S(2)}) collective-permute-start(f32[1,64,1024]{2,1,0:T(8,128)S(1)} %bitcast.36), channel_id=1, source_target_pairs={{0,8},{2,10},{4,12},{6,14},{8,0},{10,2},{12,4},{14,6},{1,9},{3,11}... | collective-permute-start | bytes 786440 | tf_op jit(solution)/shard_map/ppermute | solution.py:330
  13.2 34.1 %collective-permute-done.refs_1_ = f32[1,64,1024]{2,1,0:T(8,128)} collective-permute-done((f32[1,64,1024]{2,1,0:T(8,128)S(1)}, f32[1,64,1024]{2,1,0:T(8,128)}, u32[]{:S(2)}, u32[]{:S(2)}) %collective-permute-start) | collective-permute-done | bytes 262176 | tf_op jit(solution)/shard_map/ppermute | solution.py:330
  47.4 1.0 pad_maximum_fusion.1
  48.4 0.1 collective-permute-start.1
  48.4 12.6 %collective-permute-done.1.refs_2_ = f32[2,64,1024]{2,1,0:T(8,128)} collective-permute-done((f32[2,64,1024]{2,1,0:T(8,128)S(1)}, f32[2,64,1024]{2,1,0:T(8,128)}, u32[]{:S(2)}, u32[]{:S(2)}) %collective-permute-start.1) | collective-permute-done | bytes 524320 | tf_op jit(solution)/shard_map/ppermute | solution.py:330
  61.0 2.2 %pad_maximum_fusion = f32[4,64,1024]{2,1,0:T(8,128)} fusion(f32[2,64,1024]{2,1,0:T(8,128)} %collective-permute-done.1.refs_2_, f32[1,64,1024]{2,1,0:T(8,128)} %collective-permute-done.refs_1_, f32[1,64,1024]{2,1,0:T(8,128)S(1)} %bitcast.38), kind=kLoop, calls=%fused_computation | loop fusion | flops 524288 | bytes 2097152 | tf_op jit(solution)/shard_map/concatenate | solution.py:347
  63.2 1.8 collective-permute-start.2
  65.0 0.1 copy.10
  65.1 2.3 %broadcast_multiply_fusion = (f32[16,16,16,16]{3,2,1,0:T(8,128)}, f32[16,16,16,16]{3,2,1,0:T(8,128)}) fusion(f32[16,16]{1,0:T(8,128)S(1)} %copy-done.9, f32[16,16]{1,0:T(8,128)S(1)} %fusion.2, f32[16,16]{1,0:T(8,128)S(1)} %copy.10), kind=kLoop, calls=%fused_computation.2 | loop fusion | flops 131072 | bytes 527360 | tf_op jit(solution)/shard_map/mul | solution.py:337
  67.4 2.4 %mul.58.k_ref = f32[256,256]{1,0:T(8,128)S(1)} reshape(f32[16,16,16,16]{3,2,1,0:T(8,128)} %get-tuple-element.24) | data formatting | bytes 524288 | tf_op jit(solution)/shard_map/mul | solution.py:337
  69.9 0.0 all-to-all-done.1
  69.9 0.0 copy-start.3
  69.9 2.3 %mix.1 = f32[16,128,128]{2,1,0:T(8,128)} custom-call(f32[256,256]{1,0:T(8,128)S(1)} %mul.58.k_ref, f32[16,128,128]{2,1,0:T(8,128)S(1)} %bitcast.32), custom_call_target="tpu_custom_call" | custom-call | flops 402653184 | bytes 2097152 | tf_op jit(solution)/shard_map/mix/pallas_call | solution.py:117
  72.2 3.7 %all-to-all-start.3 = ((f32[8,2,128,128]{3,2,1,0:T(8,128)}), f32[8,2,128,128]{3,2,1,0:T(8,128)S(1)}, u32[]{:S(2)}, u32[]{:S(2)}) async-start(f32[8,2,128,128]{3,2,1,0:T(8,128)} %bitcast.12), calls=%async_computation.3 | async-start | bytes 2097152 | tf_op jit(solution)/shard_map/all_to_all | solution.py:333
  75.9 0.1 collective-permute-start.7
  76.0 20.6 %collective-permute-done.2.refs_3_ = f32[4,64,1024]{2,1,0:T(8,128)} collective-permute-done((f32[4,64,1024]{2,1,0:T(8,128)}, f32[4,64,1024]{2,1,0:T(8,128)}, u32[]{:S(2)}, u32[]{:S(2)}) %collective-permute-start.2) | collective-permute-done | bytes 1048608 | tf_op jit(solution)/shard_map/ppermute | solution.py:330
  96.6 0.0 collective-permute-start.6
  96.6 0.5 collective-permute-start.5
  97.1 0.0 collective-permute-start.3
  97.1 0.5 collective-permute-start.4
  97.6 1.1 fusion.3
  98.7 0.0 collective-permute-done.7.other_ref
  98.7 0.0 copy-start.4
  98.7 1.2 copy-done.4
  100.0 1.2 copy-done.5
  101.2 3.1 %gate.1 = (f32[2048,128]{1,0:T(8,128)S(1)}, f32[2048,128]{1,0:T(8,128)S(1)}) custom-call(f32[2048,128]{1,0:T(8,128)S(1)} %copy-done.4, f32[2048,128]{1,0:T(8,128)} %collective-permute-done.7.other_ref, f32[2048,128]{1,0:T(8,128)S(1)} %copy-done.5, f32[128,256]{1,0:T(8,128)S(1)} %pad_maximum_fusion.2.w_ref), custom_call_target="tpu_custom_call" | custom-call | flops 402653184 | bytes 5242880 | tf_op jit(solution)/shard_map/gate/pallas_call | solution.py:56
  104.3 1.0 copy-done.6
  105.2 0.0 collective-permute-done.3.refs_4_
  105.3 0.0 collective-permute-done.4.refs_5_
  105.3 0.0 collective-permute-done.6.refs_7_
  105.3 4.6 %place.1 = (bf16[1024,1024]{1,0:T(8,128)(2,1)}, bf16[1024,1024]{1,0:T(8,128)(2,1)}) custom-call(s32[1]{0:T(128)} %bitcast.1.s_ref, s32[1]{0:T(128)} %bitcast.2.h_ref, f32[1,64,1024]{2,1,0:T(8,128)S(1)} %bitcast.40, f32[1,64,1024]{2,1,0:T(8,128)} %collective-permute-done.refs_1_, f32[2,64,1024]{2,1,0:T(8,128)} %collective-permute-done.1.refs_2_, ...), custom_call_target="tpu_custom_call" | custom-call | flops 1048576 | bytes 8388608 | tf_op jit(solution)/shard_map/place/pallas_call | solution.py:176
  109.9 1.6 copy-done
  111.5 5.1 %up.1 = f32[8,2,128,128]{3,2,1,0:T(8,128)} custom-call(bf16[1024,1024]{1,0:T(8,128)(2,1)S(1)} %copy-done, bf16[1024,1024]{1,0:T(8,128)(2,1)} %get-tuple-element.13.lo_ref, f32[2,1024,128]{2,1,0:T(8,128)S(1)} %bitcast.34), custom_call_target="tpu_custom_call" | custom-call | flops 1610612736 | bytes 6291456 | tf_op jit(solution)/shard_map/up/pallas_call | solution.py:207
  116.6 5.9 %all-to-all-start = ((f32[8,2,128,128]{3,2,1,0:T(8,128)}), f32[8,2,128,128]{3,2,1,0:T(8,128)}, u32[]{:S(2)}, u32[]{:S(2)}) async-start(f32[8,2,128,128]{3,2,1,0:T(8,128)} %up.1), calls=%async_computation | async-start | bytes 2097152 | tf_op jit(solution)/shard_map/all_to_all | solution.py:333
  122.5 0.1 dynamic-slice_bitcast_fusion
  122.6 0.6 collective-permute-start.8
  123.1 2.8 %collective-permute-done.8.gb_ref = f32[2,8,64,128]{3,2,1,0:T(8,128)S(1)} collective-permute-done((f32[2,8,64,128]{3,2,1,0:T(8,128)S(1)}, f32[2,8,64,128]{3,2,1,0:T(8,128)S(1)}, u32[]{:S(2)}, u32[]{:S(2)}) %collective-permute-start.8) | collective-permute-done | bytes 524320 | tf_op jit(solution)/shard_map/ppermute | solution.py:327
  125.9 4.7 %first.1 = (f32[4,64,1024]{2,1,0:T(8,128)S(1)}, f32[4,64,1024]{2,1,0:T(8,128)}) custom-call(s32[1]{0:T(128)} %bitcast.1.s_ref, f32[2,8,64,128]{3,2,1,0:T(8,128)S(1)} %get-tuple-element.21.ga_ref, f32[2,8,64,128]{3,2,1,0:T(8,128)S(1)} %collective-permute-done.8.gb_ref, f32[8,2,128,128]{3,2,1,0:T(8,128)S(1)} %all-to-all-done.3.v_ref.va_ref, ...), custom_call_target="tpu_custom_call" | custom-call | flops 1610612736 | bytes 6291456 | tf_op jit(solution)/shard_map/first/pallas_call | solution.py:300
  130.6 2.0 collective-permute-start.10
  132.7 2.4 %mul.53.k_ref = f32[256,256]{1,0:T(8,128)S(1)} reshape(f32[16,16,16,16]{3,2,1,0:T(8,128)} %get-tuple-element.25) | data formatting | bytes 524288 | tf_op jit(solution)/shard_map/mul | solution.py:338
  135.1 13.4 %all-to-all-done = f32[8,2,128,128]{3,2,1,0:T(8,128)} async-done(((f32[8,2,128,128]{3,2,1,0:T(8,128)}), f32[8,2,128,128]{3,2,1,0:T(8,128)}, u32[]{:S(2)}, u32[]{:S(2)}) %all-to-all-start) | async-done | bytes 1048608 | tf_op jit(solution)/shard_map/all_to_all | solution.py:333
  148.6 4.6 %mix_second.1 = (f32[16,128,128]{2,1,0:T(8,128)S(1)}, f32[16,16]{1,0:T(8,128)S(1)}) custom-call(f32[256,256]{1,0:T(8,128)S(1)} %mul.53.k_ref, f32[16,128,128]{2,1,0:T(8,128)} %bitcast.5.u_ref, f32[16,128,128]{2,1,0:T(8,128)S(1)} %bitcast.33), custom_call_target="tpu_custom_call" | custom-call | flops 805306368 | bytes 3145728 | tf_op jit(solution)/shard_map/mix_second/pallas_call | solution.py:134
  153.2 0.0 copy-start.8
  153.2 1.0 copy-done.8
  154.1 4.2 %all-to-all-start.2 = ((f32[8,2,128,128]{3,2,1,0:T(8,128)}), f32[8,2,128,128]{3,2,1,0:T(8,128)}, u32[]{:S(2)}, u32[]{:S(2)}) async-start(f32[8,2,128,128]{3,2,1,0:T(8,128)} %bitcast.42), calls=%async_computation.2 | async-start | bytes 2097152 | tf_op jit(solution)/shard_map/all_to_all | solution.py:333
  158.4 2.2 %collective-permute-done.10 = f32[4,64,1024]{2,1,0:T(8,128)} collective-permute-done((f32[4,64,1024]{2,1,0:T(8,128)}, f32[4,64,1024]{2,1,0:T(8,128)}, u32[]{:S(2)}, u32[]{:S(2)}) %collective-permute-start.10) | collective-permute-done | bytes 1048608 | tf_op jit(solution)/shard_map/ppermute | solution.py:330
  160.6 1.4 add.44
  162.1 6.0 %collective-permute-start.11 = (f32[2,64,1024]{2,1,0:T(8,128)S(1)}, f32[2,64,1024]{2,1,0:T(8,128)S(1)}, u32[]{:S(2)}, u32[]{:S(2)}) collective-permute-start(f32[2,64,1024]{2,1,0:T(8,128)S(1)} %slice.17), channel_id=1, source_target_pairs={{0,4},{2,6},{4,0},{6,2},{8,12},{10,14},{12,8},{14,10},{1,5},{3,7},... | collective-permute-start | bytes 1572872 | tf_op jit(solution)/shard_map/ppermute | solution.py:330
  168.1 20.4 %collective-permute-done.11 = f32[2,64,1024]{2,1,0:T(8,128)S(1)} collective-permute-done((f32[2,64,1024]{2,1,0:T(8,128)S(1)}, f32[2,64,1024]{2,1,0:T(8,128)S(1)}, u32[]{:S(2)}, u32[]{:S(2)}) %collective-permute-start.11) | collective-permute-done | bytes 524320 | tf_op jit(solution)/shard_map/ppermute | solution.py:330
  188.5 0.1 slice_add_fusion
  188.6 2.5 %collective-permute-start.12 = (f32[1,64,1024]{2,1,0:T(8,128)S(1)}, f32[1,64,1024]{2,1,0:T(8,128)S(1)}, u32[]{:S(2)}, u32[]{:S(2)}) collective-permute-start(f32[1,64,1024]{2,1,0:T(8,128)S(1)} %slice.19), channel_id=1, source_target_pairs={{0,8},{2,10},{4,12},{6,14},{8,0},{10,2},{12,4},{14,6},{1,9},{3,11}... | collective-permute-start | bytes 786440 | tf_op jit(solution)/shard_map/ppermute | solution.py:330
  191.1 1.2 collective-permute-done.13
  192.3 1.4 collective-permute-start.14
  193.7 2.3 %collective-permute-done.14 = f32[16,16]{1,0:T(8,128)S(1)} collective-permute-done((f32[16,16]{1,0:T(8,128)S(1)}, f32[16,16]{1,0:T(8,128)S(1)}, u32[]{:S(2)}, u32[]{:S(2)}) %collective-permute-start.14) | collective-permute-done | bytes 1056 | tf_op jit(solution)/shard_map/ppermute | solution.py:330
  195.9 0.2 collective-permute-start.15
  196.1 5.4 %collective-permute-done.15 = f32[16,16]{1,0:T(8,128)S(1)} collective-permute-done((f32[16,16]{1,0:T(8,128)S(1)}, f32[16,16]{1,0:T(8,128)S(1)}, u32[]{:S(2)}, u32[]{:S(2)}) %collective-permute-start.15) | collective-permute-done | bytes 1056 | tf_op jit(solution)/shard_map/ppermute | solution.py:330
  201.5 0.0 collective-permute-start.16
  201.5 4.9 %mixed.1 = f32[2,1024,128]{2,1,0:T(8,128)} custom-call(bf16[1024,1024]{1,0:T(8,128)(2,1)S(1)} %copy-done.1, bf16[1024,1024]{1,0:T(8,128)(2,1)} %get-tuple-element.13.lo_ref, f32[8,2,128,128]{3,2,1,0:T(8,128)S(1)} %all-to-all-done.3.v_ref.va_ref, f32[2,1024,128]{2,1,0:T(8,128)S(1)} %bitcast.41), custom_call_target="tpu_custom_call" | custom-call | flops 1610612736 | bytes 7340032 | tf_op jit(solution)/shard_map/mixed/pallas_call | solution.py:243
  206.4 0.0 collective-permute-done.16
  206.4 0.6 add.50
  207.0 2.3 %copy.12 = f32[2,8,128,128]{3,2,1,0:T(8,128)} copy(f32[2,8,128,128]{3,2,0,1:T(8,128)} %bitcast.10) | data formatting | bytes 2097152 | tf_op jit(solution)/shard_map/transpose | solution.py:370
  209.3 0.7 fusion.1
  (26 shorter events, 0.1 us)
Async XLA Ops:
  0.6 9.6 %copy-start.2 = (f32[64,1024]{1,0:T(8,128)S(1)}, f32[64,1024]{1,0:T(8,128)}, u32[]{:S(2)}) copy-start(f32[64,1024]{1,0:T(8,128)} %param.9) | copy-start | bytes 786436
  3.0 66.9 %all-to-all-start.1 = ((f32[8,2,128,128]{3,2,1,0:T(8,128)}), f32[8,2,128,128]{3,2,1,0:T(8,128)S(1)}, u32[]{:S(2)}, u32[]{:S(2)}) async-start(f32[8,2,128,128]{3,2,1,0:T(8,128)} %bitcast.31), calls=%async_computation.1 | async-start | bytes 2097152 | tf_op jit(solution)/shard_map/all_to_all | solution.py:333
  10.3 54.8 %copy-start.9 = (f32[16,16]{1,0:T(8,128)S(1)}, f32[16,16]{1,0:T(8,128)}, u32[]{:S(2)}) copy-start(f32[16,16]{1,0:T(8,128)} %param.10) | copy-start | bytes 3076
  10.3 37.1 %collective-permute-start = (f32[1,64,1024]{2,1,0:T(8,128)S(1)}, f32[1,64,1024]{2,1,0:T(8,128)}, u32[]{:S(2)}, u32[]{:S(2)}) collective-permute-start(f32[1,64,1024]{2,1,0:T(8,128)S(1)} %bitcast.36), channel_id=1, source_target_pairs={{0,8},{2,10},{4,12},{6,14},{8,0},{10,2},{12,4},{14,6},{1,9},{3,11}... | collective-permute-start | bytes 786440 | tf_op jit(solution)/shard_map/ppermute | solution.py:330
  48.4 12.7 %collective-permute-start.1 = (f32[2,64,1024]{2,1,0:T(8,128)S(1)}, f32[2,64,1024]{2,1,0:T(8,128)}, u32[]{:S(2)}, u32[]{:S(2)}) collective-permute-start(f32[2,64,1024]{2,1,0:T(8,128)S(1)} %pad_maximum_fusion.1), channel_id=1, source_target_pairs={{0,4},{2,6},{4,0},{6,2},{8,12},{10,14},{12,8},{14,10},{1,5},{3,7},... | collective-permute-start | bytes 1572872 | tf_op jit(solution)/shard_map/ppermute | solution.py:330
  63.2 33.4 %collective-permute-start.2 = (f32[4,64,1024]{2,1,0:T(8,128)}, f32[4,64,1024]{2,1,0:T(8,128)}, u32[]{:S(2)}, u32[]{:S(2)}) collective-permute-start(f32[4,64,1024]{2,1,0:T(8,128)} %pad_maximum_fusion), channel_id=1, source_target_pairs={{0,2},{2,0},{4,6},{6,4},{8,10},{10,8},{12,14},{14,12},{1,3},{3,1},... | collective-permute-start | bytes 3145736 | tf_op jit(solution)/shard_map/ppermute | solution.py:330
  69.9 6.0 %copy-start.3 = (f32[2048,128]{1,0:T(8,128)S(1)}, f32[2048,128]{1,0:T(8,128)}, u32[]{:S(2)}) copy-start(f32[2048,128]{1,0:T(8,128)} %own_ref.1) | copy-start | bytes 3145732
  72.2 44.4 %all-to-all-start.3 = ((f32[8,2,128,128]{3,2,1,0:T(8,128)}), f32[8,2,128,128]{3,2,1,0:T(8,128)S(1)}, u32[]{:S(2)}, u32[]{:S(2)}) async-start(f32[8,2,128,128]{3,2,1,0:T(8,128)} %bitcast.12), calls=%async_computation.3 | async-start | bytes 2097152 | tf_op jit(solution)/shard_map/all_to_all | solution.py:333
  75.9 22.8 %collective-permute-start.7 = (f32[2048,128]{1,0:T(8,128)S(1)}, f32[2048,128]{1,0:T(8,128)}, u32[]{:S(2)}, u32[]{:S(2)}) collective-permute-start(f32[2048,128]{1,0:T(8,128)S(1)} %copy-done.3), channel_id=1, source_target_pairs={{0,1},{1,0},{2,3},{3,2},{4,5},{5,4},{6,7},{7,6},{8,9},{9,8},{10,11... | collective-permute-start | bytes 3145736 | tf_op jit(solution)/shard_map/ppermute | solution.py:327
  96.6 8.6 %collective-permute-start.6 = (f32[4,64,1024]{2,1,0:T(8,128)}, f32[4,64,1024]{2,1,0:T(8,128)}, u32[]{:S(2)}, u32[]{:S(2)}) collective-permute-start(f32[4,64,1024]{2,1,0:T(8,128)} %collective-permute-done.2.refs_3_), channel_id=1, source_target_pairs={{0,1},{1,0},{2,3},{3,2},{4,5},{5,4},{6,7},{7,6},{8,9},{9,8},{10,11... | collective-permute-start | bytes 3145736 | tf_op jit(solution)/shard_map/ppermute | solution.py:327
  96.6 8.6 %collective-permute-start.5 = (f32[2,64,1024]{2,1,0:T(8,128)}, f32[2,64,1024]{2,1,0:T(8,128)}, u32[]{:S(2)}, u32[]{:S(2)}) collective-permute-start(f32[2,64,1024]{2,1,0:T(8,128)} %collective-permute-done.1.refs_2_), channel_id=1, source_target_pairs={{0,1},{1,0},{2,3},{3,2},{4,5},{5,4},{6,7},{7,6},{8,9},{9,8},{10,11... | collective-permute-start | bytes 1572872 | tf_op jit(solution)/shard_map/ppermute | solution.py:327
  97.1 8.1 %collective-permute-start.3 = (f32[1,64,1024]{2,1,0:T(8,128)S(1)}, f32[1,64,1024]{2,1,0:T(8,128)}, u32[]{:S(2)}, u32[]{:S(2)}) collective-permute-start(f32[1,64,1024]{2,1,0:T(8,128)S(1)} %bitcast.39), channel_id=1, source_target_pairs={{0,1},{1,0},{2,3},{3,2},{4,5},{5,4},{6,7},{7,6},{8,9},{9,8},{10,11... | collective-permute-start | bytes 786440 | tf_op jit(solution)/shard_map/ppermute | solution.py:327
  97.1 8.1 %collective-permute-start.4 = (f32[1,64,1024]{2,1,0:T(8,128)}, f32[1,64,1024]{2,1,0:T(8,128)S(1)}, u32[]{:S(2)}, u32[]{:S(2)}) collective-permute-start(f32[1,64,1024]{2,1,0:T(8,128)} %collective-permute-done.refs_1_), channel_id=1, source_target_pairs={{0,1},{1,0},{2,3},{3,2},{4,5},{5,4},{6,7},{7,6},{8,9},{9,8},{10,11... | collective-permute-start | bytes 786440 | tf_op jit(solution)/shard_map/ppermute | solution.py:327
  98.7 1.2 copy-start.4
  100.0 1.2 copy-start.5
  104.3 1.0 copy-start.6
  109.9 1.6 copy-start
  116.6 32.0 %all-to-all-start = ((f32[8,2,128,128]{3,2,1,0:T(8,128)}), f32[8,2,128,128]{3,2,1,0:T(8,128)}, u32[]{:S(2)}, u32[]{:S(2)}) async-start(f32[8,2,128,128]{3,2,1,0:T(8,128)} %up.1), calls=%async_computation | async-start | bytes 2097152 | tf_op jit(solution)/shard_map/all_to_all | solution.py:333
  122.5 3.4 %collective-permute-start.9 = (f32[8,2,128,128]{3,2,1,0:T(8,128)S(1)}, f32[8,2,128,128]{3,2,1,0:T(8,128)}, u32[]{:S(2)}, u32[]{:S(2)}) collective-permute-start(f32[8,2,128,128]{3,2,1,0:T(8,128)S(1)} %all-to-all-done.3.v_ref.va_ref), channel_id=1, source_target_pairs={{0,1},{1,0},{2,3},{3,2},{4,5},{5,4},{6,7},{7,6},{8,9},{9,8},{10,11... | collective-permute-start | bytes 3145736 | tf_op jit(solution)/shard_map/ppermute | solution.py:327
  122.6 3.3 %collective-permute-start.8 = (f32[2,8,64,128]{3,2,1,0:T(8,128)S(1)}, f32[2,8,64,128]{3,2,1,0:T(8,128)S(1)}, u32[]{:S(2)}, u32[]{:S(2)}) collective-permute-start(f32[2,8,64,128]{3,2,1,0:T(8,128)S(1)} %get-tuple-element.20), channel_id=1, source_target_pairs={{0,1},{1,0},{2,3},{3,2},{4,5},{5,4},{6,7},{7,6},{8,9},{9,8},{10,11... | collective-permute-start | bytes 1572872 | tf_op jit(solution)/shard_map/ppermute | solution.py:327
  130.6 30.0 %collective-permute-start.10 = (f32[4,64,1024]{2,1,0:T(8,128)}, f32[4,64,1024]{2,1,0:T(8,128)}, u32[]{:S(2)}, u32[]{:S(2)}) collective-permute-start(f32[4,64,1024]{2,1,0:T(8,128)} %get-tuple-element.18), channel_id=1, source_target_pairs={{0,2},{2,0},{4,6},{6,4},{8,10},{10,8},{12,14},{14,12},{1,3},{3,1},... | collective-permute-start | bytes 3145736 | tf_op jit(solution)/shard_map/ppermute | solution.py:330
  153.2 1.0 copy-start.8
  154.1 52.8 %all-to-all-start.2 = ((f32[8,2,128,128]{3,2,1,0:T(8,128)}), f32[8,2,128,128]{3,2,1,0:T(8,128)}, u32[]{:S(2)}, u32[]{:S(2)}) async-start(f32[8,2,128,128]{3,2,1,0:T(8,128)} %bitcast.42), calls=%async_computation.2 | async-start | bytes 2097152 | tf_op jit(solution)/shard_map/all_to_all | solution.py:333
  162.0 39.5 %copy-start.1 = (bf16[1024,1024]{1,0:T(8,128)(2,1)S(1)}, bf16[1024,1024]{1,0:T(8,128)(2,1)}, u32[]{:S(2)}) copy-start(bf16[1024,1024]{1,0:T(8,128)(2,1)} %get-tuple-element.12.hi_ref) | copy-start | bytes 6291460
  162.0 39.5 %copy-start.7 = (f32[2048,128]{1,0:T(8,128)S(1)}, f32[2048,128]{1,0:T(8,128)}, u32[]{:S(2)}) copy-start(f32[2048,128]{1,0:T(8,128)} %copy-done.6) | copy-start | bytes 3145732
  162.1 26.4 %collective-permute-start.11 = (f32[2,64,1024]{2,1,0:T(8,128)S(1)}, f32[2,64,1024]{2,1,0:T(8,128)S(1)}, u32[]{:S(2)}, u32[]{:S(2)}) collective-permute-start(f32[2,64,1024]{2,1,0:T(8,128)S(1)} %slice.17), channel_id=1, source_target_pairs={{0,4},{2,6},{4,0},{6,2},{8,12},{10,14},{12,8},{14,10},{1,5},{3,7},... | collective-permute-start | bytes 1572872 | tf_op jit(solution)/shard_map/ppermute | solution.py:330
  188.6 20.7 %collective-permute-start.12 = (f32[1,64,1024]{2,1,0:T(8,128)S(1)}, f32[1,64,1024]{2,1,0:T(8,128)S(1)}, u32[]{:S(2)}, u32[]{:S(2)}) collective-permute-start(f32[1,64,1024]{2,1,0:T(8,128)S(1)} %slice.19), channel_id=1, source_target_pairs={{0,8},{2,10},{4,12},{6,14},{8,0},{10,2},{12,4},{14,6},{1,9},{3,11}... | collective-permute-start | bytes 786440 | tf_op jit(solution)/shard_map/ppermute | solution.py:330
  191.1 1.2 collective-permute-start.13
  192.3 3.7 %collective-permute-start.14 = (f32[16,16]{1,0:T(8,128)S(1)}, f32[16,16]{1,0:T(8,128)S(1)}, u32[]{:S(2)}, u32[]{:S(2)}) collective-permute-start(f32[16,16]{1,0:T(8,128)S(1)} %add.47), channel_id=1, source_target_pairs={{0,2},{2,0},{4,6},{6,4},{8,10},{10,8},{12,14},{14,12},{1,3},{3,1},... | collective-permute-start | bytes 3080 | tf_op jit(solution)/shard_map/ppermute | solution.py:330
  195.9 5.6 %collective-permute-start.15 = (f32[16,16]{1,0:T(8,128)S(1)}, f32[16,16]{1,0:T(8,128)S(1)}, u32[]{:S(2)}, u32[]{:S(2)}) collective-permute-start(f32[16,16]{1,0:T(8,128)S(1)} %add.48), channel_id=1, source_target_pairs={{0,4},{2,6},{4,0},{6,2},{8,12},{10,14},{12,8},{14,10},{1,5},{3,7},... | collective-permute-start | bytes 3080 | tf_op jit(solution)/shard_map/ppermute | solution.py:330
  201.5 4.9 %collective-permute-start.16 = (f32[16,16]{1,0:T(8,128)S(1)}, f32[16,16]{1,0:T(8,128)S(1)}, u32[]{:S(2)}, u32[]{:S(2)}) collective-permute-start(f32[16,16]{1,0:T(8,128)S(1)} %add.49), channel_id=1, source_target_pairs={{0,8},{2,10},{4,12},{6,14},{8,0},{10,2},{12,4},{14,6},{1,9},{3,11}... | collective-permute-start | bytes 3080 | tf_op jit(solution)/shard_map/ppermute | solution.py:330

commit v2 on v1

v2 whole, which is shorter than its diff:
```python
import functools
import math

import jax
import jax.numpy as jnp
from jax import lax
from jax.experimental import pallas as pl
from jax.experimental.pallas import tpu as pltpu
from jax.sharding import PartitionSpec as P

F32 = jnp.float32
BF16 = jnp.bfloat16
NN = (((1,), (0,)), ((), ()))
NT = (((1,), (1,)), ((), ()))
TN = (((0,), (0,)), ((), ()))
VMEM_LIMIT = 16 * 1024 * 1024


def split(x):
    hi = x.astype(BF16)
    return hi, (x - hi.astype(F32)).astype(BF16)


def dot3(a, b, dims):
    (ah, al), (bh, bl) = a, b

    def d(u, v):
        return lax.dot_general(u, v, dims, preferred_element_type=F32)

    return d(ah, bh) + (d(ah, bl) + d(al, bh))


def params():
    return pltpu.CompilerParams(vmem_limit_bytes=VMEM_LIMIT)


def cost(flops, size):
    return pl.CostEstimate(flops=flops, bytes_accessed=size, transcendentals=0)


def gate_kernel(ids_ref, own_ref, other_ref, gate_ref, w_ref, grad_ref, factor_ref, mine_ref, send_ref):
    cot = jnp.concatenate([own_ref[...], other_ref[...]], axis=1)
    hidden = dot3(split(cot), split(w_ref[...]), NT)
    g = gate_ref[...]
    s = jax.nn.sigmoid(g)
    hs = hidden * s
    grad = hs * g
    grad_ref[...] = grad
    _, count, unit, width = mine_ref.shape
    pairs = grad.reshape(count, 2, unit, width)
    low = ids_ref[1] == 0
    mine_ref[0] = jnp.where(low, pairs[:, 0], pairs[:, 1])
    send_ref[0] = jnp.where(low, pairs[:, 1], pairs[:, 0])
    factor_ref[...] = hs * (1.0 + g * (1.0 - s))


def gate_call(ids, own, other, gate, w, blocks, unit):
    rows, width = own.shape
    per = 2
    tile = rows // blocks // per
    count = tile // (2 * unit)
    row = pl.BlockSpec((tile, width), lambda i: (i, 0))
    part = pl.BlockSpec((1, count, unit, width), lambda i: (i // per, i % per, 0, 0))
    shape = jax.ShapeDtypeStruct(own.shape, F32)
    part_shape = jax.ShapeDtypeStruct((blocks, per * count, unit, width), F32)
    return pl.pallas_call(
        gate_kernel,
        grid=(blocks * per,),
        in_specs=[
            pl.BlockSpec(memory_space=pltpu.SMEM),
            row,
            row,
            row,
            pl.BlockSpec(w.shape, lambda i: (0, 0)),
        ],
        out_specs=[row, row, part, part],
        out_shape=[shape, shape, part_shape, part_shape],
        compiler_params=params(),
        cost_estimate=cost(6 * rows * width * 2 * width, 6 * 4 * rows * width),
        name="gate",
    )(ids, own, other, gate, w)


def grouped(ref, group):
    n, span, width = ref.shape
    return jnp.concatenate(
        [ref[:, g * group : (g + 1) * group, :].reshape(n * group, width) for g in range(span // group)], axis=1
    )


def scatter_groups(ref, group, val):
    n, span, width = ref.shape
    for g in range(span // group):
        ref[:, g * group : (g + 1) * group, :] = val[:, g * width : (g + 1) * width].reshape(n, group, width)


def spread(w, group):
    n = w.shape[0]
    size = n * group
    pick = (
        lax.div(lax.broadcasted_iota(jnp.int32, (size, n), 0), group)
        == lax.broadcasted_iota(jnp.int32, (size, n), 1)
    ).astype(F32)

    def d(a, b, dims):
        return lax.dot_general(a, b, dims, precision=lax.Precision.HIGHEST, preferred_element_type=F32)

    full = d(d(pick, w, NN), pick, NT)
    r = lax.broadcasted_iota(jnp.int32, (size, size), 0)
    c = lax.broadcasted_iota(jnp.int32, (size, size), 1)
    return jnp.where(lax.rem(r, group) == lax.rem(c, group), full, 0.0)


def spread_kernel(group, w_ref, kh, kl, th, tl):
    w = w_ref[...]
    kh[...], kl[...] = split(spread(w, group))
    th[...], tl[...] = split(spread(w.T, group))


def spread_call(w, group):
    size = w.shape[0] * group
    return pl.pallas_call(
        functools.partial(spread_kernel, group),
        out_shape=[jax.ShapeDtypeStruct((size, size), BF16)] * 4,
        compiler_params=params(),
        cost_estimate=cost(8 * size * size * w.shape[0], 8 * size * size),
        name="spread",
    )(w)


def spans(width, group):
    step = min(width, 2 * group)
    return [(a, step) for a in range(0, width, step)]


def mix_kernel(group, kh, kl, x_ref, o_ref):
    k = kh[...], kl[...]
    for a, step in spans(x_ref.shape[1], group):
        x = grouped(x_ref.at[:, a : a + step], group)
        scatter_groups(o_ref.at[:, a : a + step], group, dot3(k, split(x), NN))


def mix_second_kernel(group, scale, own, kh, kl, u_ref, b_ref, o_ref, acc):
    k = kh[...], kl[...]
    n, width, _ = u_ref.shape
    for a, step in spans(width, group):
        u = split(grouped(u_ref.at[:, a : a + step], group))
        b = split(grouped(b_ref.at[:, a : a + step], group))
        scatter_groups(o_ref.at[:, a : a + step], group, dot3(k, u, NN))
        term = dot3(u, b, NT)
        acc[...] = term if a == 0 else acc[...] + term
    size = n * group
    r = lax.broadcasted_iota(jnp.int32, (size, size), 0)
    c = lax.broadcasted_iota(jnp.int32, (size, size), 1)
    diag = jnp.where(lax.rem(r, group) == lax.rem(c, group), acc[...], 0.0)
    rows = jnp.sum(diag.reshape(n, group, size), axis=1)
    lanes = o_ref.shape[2]
    pick = (
        lax.div(lax.broadcasted_iota(jnp.int32, (size, lanes), 0), group)
        == lax.broadcasted_iota(jnp.int32, (size, lanes), 1)
    ).astype(F32)
    second = scale * jnp.dot(rows, pick, precision=lax.Precision.HIGHEST, preferred_element_type=F32)
    part = n // own
    for m in range(n):
        start = (m % own) * part
        o_ref[m, width:, :] = second[start : start + part, :]


def mix_call(k, x, group):
    n, width, chan = x.shape
    return pl.pallas_call(
        functools.partial(mix_kernel, group),
        out_shape=jax.ShapeDtypeStruct(x.shape, F32),
        compiler_params=params(),
        cost_estimate=cost(6 * group * n * n * width * chan, 8 * n * width * chan),
        name="mix",
    )(*k, x)


def mix_second_call(k, u, b, group, own, scale):
    n, width, chan = u.shape
    size = n * group
    return pl.pallas_call(
        functools.partial(mix_second_kernel, group, scale, own),
        out_shape=jax.ShapeDtypeStruct((n, width + n // own, chan), F32),
        scratch_shapes=[pltpu.VMEM((size, size), F32)],
        compiler_params=params(),
        cost_estimate=cost(12 * size * n * width * chan, 12 * n * width * chan),
        name="mix_second",
    )(*k, u, b)


def place_kernel(offsets, ids_ref, *refs):
    pieces = refs[: len(offsets)]
    hi_ref, lo_ref, whole, sem = refs[len(offsets) :]
    half = pieces[0].shape[1]
    copies = []
    for piece, rels in zip(pieces, offsets):
        for u, (rel, side, flip) in enumerate(rels):
            place = 2 * lax.bitwise_xor(ids_ref[0], rel) + lax.bitwise_xor(ids_ref[1], side)
            place = 2 * place + lax.bitwise_xor(ids_ref[2], flip)
            start = pl.multiple_of(place * half, half)
            copies.append(pltpu.make_async_copy(piece.at[u], whole.at[pl.ds(start, half)], sem.at[len(copies)]))
    for c in copies:
        c.start()
    for c in copies:
        c.wait()
    rows = whole.shape[0]
    tile = 256
    for t in range(rows // tile):
        hi, lo = split(whole[t * tile : (t + 1) * tile, :])
        hi_ref[t * tile : (t + 1) * tile, :] = hi
        lo_ref[t * tile : (t + 1) * tile, :] = lo


def place_call(ids, pieces, offsets, rows, columns):
    shape = jax.ShapeDtypeStruct((rows, columns), BF16)
    vmem = pl.BlockSpec(memory_space=pltpu.VMEM)
    return pl.pallas_call(
        functools.partial(place_kernel, offsets),
        in_specs=[pl.BlockSpec(memory_space=pltpu.SMEM)] + [pl.BlockSpec(memory_space=pltpu.HBM)] * len(pieces),
        out_specs=[vmem, vmem],
        out_shape=[shape, shape],
        scratch_shapes=[pltpu.VMEM((rows, columns), F32), pltpu.SemaphoreType.DMA((sum(map(len, offsets)),))],
        compiler_params=params(),
        cost_estimate=cost(rows * columns, 8 * rows * columns),
        name="place",
    )(ids, *pieces)


def up_kernel(hi_ref, lo_ref, g_ref, o_ref, gh, gl):
    @pl.when(pl.program_id(0) == 0)
    def _():
        both = jnp.concatenate([g_ref[m] for m in range(g_ref.shape[0])], axis=1)
        gh[...], gl[...] = split(both)

    res = dot3((hi_ref[...], lo_ref[...]), (gh[...], gl[...]), TN)
    slices, blocks, width, chan = o_ref.shape
    for t in range(slices):
        for m in range(blocks):
            o_ref[t, m] = res[t * width : (t + 1) * width, m * chan : (m + 1) * chan]


def up_call(hi, lo, grad, slices):
    blocks, rows, chan = grad.shape
    tile = 256
    width = rows // slices
    per = tile // width
    wspec = pl.BlockSpec((rows, tile), lambda i: (0, i))
    return pl.pallas_call(
        up_kernel,
        grid=(rows // tile,),
        in_specs=[wspec, wspec, pl.BlockSpec(grad.shape, lambda i: (0, 0, 0))],
        out_specs=pl.BlockSpec((per, blocks, width, chan), lambda i: (i, 0, 0, 0)),
        out_shape=jax.ShapeDtypeStruct((slices, blocks, width, chan), F32),
        scratch_shapes=[pltpu.VMEM((rows, blocks * chan), BF16)] * 2,
        compiler_params=params(),
        cost_estimate=cost(6 * rows * rows * blocks * chan, 4 * rows * rows + 8 * rows * blocks * chan),
        name="up",
    )(hi, lo, grad)


def join(ref):
    slices, blocks = ref.shape[0], ref.shape[1]
    return jnp.concatenate(
        [jnp.concatenate([ref[t, m] for m in range(blocks)], axis=1) for t in range(slices)], axis=0
    )


def mixed_kernel(hi_ref, lo_ref, v_ref, f_ref, o_ref, vh, vl):
    @pl.when(pl.program_id(0) == 0)
    def _():
        vh[...], vl[...] = split(join(v_ref))

    res = dot3((hi_ref[...], lo_ref[...]), (vh[...], vl[...]), NN)
    chan = o_ref.shape[2]
    for m in range(o_ref.shape[0]):
        o_ref[m] = res[:, m * chan : (m + 1) * chan] * f_ref[m]


def mixed_call(hi, lo, v, factor):
    blocks, rows, chan = factor.shape
    tile = 256
    wspec = pl.BlockSpec((tile, rows), lambda i: (i, 0))
    ospec = pl.BlockSpec((blocks, tile, chan), lambda i: (0, i, 0))
    return pl.pallas_call(
        mixed_kernel,
        grid=(rows // tile,),
        in_specs=[wspec, wspec, pl.BlockSpec(v.shape, lambda i: (0, 0, 0, 0)), ospec],
        out_specs=ospec,
        out_shape=jax.ShapeDtypeStruct(factor.shape, F32),
        scratch_shapes=[pltpu.VMEM((rows, blocks * chan), BF16)] * 2,
        compiler_params=params(),
        cost_estimate=cost(6 * rows * rows * blocks * chan, 4 * rows * rows + 12 * rows * blocks * chan),
        name="mixed",
    )(hi, lo, v, factor)


def flip_bits(q, bits):
    r = 0
    for b in range(bits):
        r |= ((q >> b) & 1) << (bits - 1 - b)
    return r


def first_kernel(bits, ids_ref, ga_ref, gb_ref, va_ref, vb_ref, ka_ref, sa_ref, kb_ref, sb_ref, lh, ll):
    count, unit = ga_ref.shape[1], ga_ref.shape[2]
    blocks = ga_ref.shape[0]

    @pl.when(pl.program_id(0) == 0)
    def _():
        for q in range(count):
            src = lax.bitwise_xor(ids_ref[0], flip_bits(q, bits))
            row = jnp.concatenate([r[m, src] for m in range(blocks) for r in (ga_ref, gb_ref)], axis=1)
            lh[q * unit : (q + 1) * unit, :], ll[q * unit : (q + 1) * unit, :] = split(row)

    v = jnp.concatenate(
        [
            jnp.concatenate([r[t, m] for m in range(blocks) for r in (va_ref, vb_ref)], axis=1)
            for t in range(va_ref.shape[0])
        ],
        axis=0,
    )
    res = dot3((lh[...], ll[...]), split(v), NT)
    quarter, half = count // 4, unit // 2
    for q in range(count):
        r0, r1, rest = q // (2 * quarter), (q // quarter) % 2, q % quarter
        (sa_ref if r0 else ka_ref)[r1 * quarter + rest] = res[q * unit : q * unit + half, :]
        (sb_ref if r1 else kb_ref)[r0 * quarter + rest] = res[q * unit + half : (q + 1) * unit, :]


def first_call(ids, grad_own, grad_other, v_own, v_other):
    blocks, count, unit, chan = grad_own.shape
    slices, _, width, _ = v_own.shape
    rows = slices * width
    tile = 256
    per = tile // width
    bits = count.bit_length() - 1
    gspec = pl.BlockSpec(grad_own.shape, lambda i: (0, 0, 0, 0))
    vspec = pl.BlockSpec((per, blocks, width, chan), lambda i: (i, 0, 0, 0))
    ospec = pl.BlockSpec((count // 2, unit // 2, tile), lambda i: (0, 0, i))
    shape = jax.ShapeDtypeStruct((count // 2, unit // 2, rows), F32)
    depth = 2 * blocks * chan
    return pl.pallas_call(
        functools.partial(first_kernel, bits),
        grid=(rows // tile,),
        in_specs=[pl.BlockSpec(memory_space=pltpu.SMEM), gspec, gspec, vspec, vspec],
        out_specs=[ospec] * 4,
        out_shape=[shape] * 4,
        scratch_shapes=[pltpu.VMEM((count * unit, depth), BF16)] * 2,
        compiler_params=params(),
        cost_estimate=cost(6 * rows * count * unit * depth, 4 * (rows * count * unit + 2 * rows * depth)),
        name="first",
    )(ids, grad_own, grad_other, v_own, v_other)


def body(seq_count, rep_count, inputs, gate_in, out_grad, w_first, w_second, w_out):
    total = w_second.shape[0]
    own = total // seq_count
    rows = inputs.shape[0] // own
    chan = inputs.shape[1]
    width = rows // seq_count
    unit, columns = w_first.shape
    bits = seq_count.bit_length() - 1
    s = lax.axis_index("seq").astype(jnp.int32)
    h = lax.axis_index("chan").astype(jnp.int32)
    side = lax.rem(lax.axis_index("rep").astype(jnp.int32), 2)
    ids = jnp.stack([s, h, side])
    group = 16 if total * 16 <= 256 else 8

    def swap_core(x):
        return lax.ppermute(x, "chan", [(0, 1), (1, 0)])

    def swap_rep(x):
        return lax.ppermute(x, "rep", [(i, i ^ 1) for i in range(rep_count)])

    def swap_seq(x, bit):
        return lax.ppermute(x, "seq", [(i, i ^ bit) for i in range(seq_count)])

    def exchange(x):
        return lax.all_to_all(x, "seq", split_axis=0, concat_axis=0, tiled=True)

    def after(x, *deps):
        return lax.optimization_barrier((x, *deps))[0]

    other_cot = swap_core(out_grad)
    half = lax.dynamic_slice_in_dim(w_first, side * (unit // 2), unit // 2, 0).reshape(1, unit // 2, columns)
    far_bits = range(2, seq_count, 2)
    z_all = jnp.concatenate([half] + [swap_seq(half, b) for b in far_bits], axis=0)
    z_rel = (0, *far_bits)

    own_rows = lax.dynamic_slice_in_dim(w_out, h * chan, chan, 0)
    w_cat = jnp.concatenate(
        [
            lax.dynamic_slice_in_dim(own_rows, h * chan, chan, 1),
            lax.dynamic_slice_in_dim(own_rows, (1 - h) * chan, chan, 1),
        ],
        axis=1,
    )
    grad, factor, grad_own, grad_send = gate_call(ids, out_grad, other_cot, gate_in, w_cat, own, unit)
    grad_other = swap_core(grad_send)
    mixers = spread_call(w_second, group)

    sliced = inputs.reshape(own, seq_count, width, chan).transpose(1, 0, 2, 3)
    block_cols = exchange(after(sliced, grad, z_all)).reshape(total, width, chan)

    n = len(z_rel)
    y_all = swap_seq(z_all, 1)
    x_all = swap_rep(z_all)
    yx_a = swap_seq(x_all[: n // 2], 1)
    yx_b = swap_rep(y_all[n // 2 :])
    pieces = [z_all, y_all, x_all, yx_a, yx_b]
    offsets = [
        [(r, 0, 0) for r in z_rel],
        [(r ^ 1, 0, 0) for r in z_rel],
        [(r, 0, 1) for r in z_rel],
        [(r ^ 1, 0, 1) for r in z_rel[: n // 2]],
        [(r ^ 1, 0, 1) for r in z_rel[n // 2 :]],
    ]

    block_cols = after(block_cols, y_all, x_all, grad_other)
    v_cols = mix_call(mixers[:2], block_cols, group)
    v = exchange(v_cols.reshape(seq_count, own, width, chan))

    far = [swap_core(p) for p in pieces[:3]] + [swap_core(after(p, v_cols)) for p in pieces[3:]]
    offsets += [[(r, 1, f) for r, _, f in o] for o in offsets]
    hi, lo = place_call(ids, pieces + far, tuple(map(tuple, offsets)), rows, columns)
    u = up_call(hi, lo, grad.reshape(own, rows, chan), seq_count)
    v = after(v, u)
    u_cols = exchange(u).reshape(total, width, chan)

    keep_a, send_a, keep_b, send_b = first_call(ids, grad_own, grad_other, v, swap_core(v))
    got_a, got_b = swap_seq(send_a, 1), swap_seq(send_b, 2)
    gate_grad = mixed_call(hi, lo, after(v, send_a), factor.reshape(own, rows, chan)).reshape(inputs.shape)
    keep_a, keep_b = keep_a + got_a, keep_b + got_b

    in_cols = mix_second_call(
        mixers[2:],
        after(u_cols, gate_grad, keep_a, keep_b),
        block_cols,
        group,
        own,
        1.0 / math.sqrt(rows * 2 * chan),
    )
    back = exchange(in_cols.reshape(seq_count, own, *in_cols.shape[1:]))
    input_grad = back[:, :, :width].transpose(1, 0, 2, 3).reshape(inputs.shape)
    second = jnp.sum(back[:, :, width:, :total], axis=0).reshape(total, total)
    second = second + swap_core(second)

    quarter = keep_a.shape[0] // 2
    got_a, got_b = swap_seq(keep_a[quarter:], 2), swap_seq(keep_b[quarter:], 1)
    keep = jnp.concatenate([keep_a[:quarter] + got_a, keep_b[:quarter] + got_b], axis=1)
    for b in range(2, bits):
        part = keep.shape[0] // 2
        keep = keep[:part] + swap_seq(keep[part:], 1 << b)
    first_grad = keep.reshape(unit, columns) * (1.0 / math.sqrt(total * 2 * chan))
    return input_grad, gate_grad, first_grad, second


def solution(mesh):
    return jax.shard_map(
        functools.partial(body, mesh.shape["seq"], mesh.shape["rep"]),
        mesh=mesh,
        in_specs=(
            P(("rep", "seq"), "chan"),
            P(("rep", "seq"), "chan"),
            P(("rep", "seq"), "chan"),
            P(("seq", "chan"), None),
            P(),
            P(),
        ),
        out_specs=(
            P(("rep", "seq"), "chan"),
            P(("rep", "seq"), "chan"),
            P(("rep", "seq", "chan"), None),
            P("rep", None),
        ),
        check_vma=False,
    )
```

time: 211 us -> 184 us (0.87)
  waiting for transfers between devices: 115 us -> 88.4 us
  other arithmetic: 8.27 us -> 1.69 us
  starting transfers between devices: 39.7 us -> 45.6 us
    ppermute x9 -> x10, waiting for transfers between devices: 97.7 us -> 72.3 us  [swap_seq(): return lax.ppermute(x, 'seq', [(i, i ^ bit) for i in range(seq_count)])]
    all_to_all x4, waiting for transfers between devices: 13.4 us -> 0.34 us  [exchange(): return lax.all_to_all(x, 'seq', split_axis=0, concat_axis=0, tiled=True)]
    ppermute x0 -> x2, waiting for transfers between devices: none -> 11.4 us  [swap_rep(): return lax.ppermute(x, 'rep', [(i, i ^ 1) for i in range(rep_count)])]
    unnamed x20 -> x46, local copies, waits for them, and re-layouts: 5.98 us -> 12.4 us
    mul x2 -> x0, local copies, waits for them, and re-layouts: 4.88 us -> none  [the longest x1 2.44 us: body(): w_second[:, None, :, None] * eye[None, :, None, :]]
    ppermute x9 -> x10, starting transfers between devices: 17 us -> 21.6 us  [swap_seq(): return lax.ppermute(x, 'seq', [(i, i ^ bit) for i in range(seq_count)])]
    concatenate x2, other arithmetic: 3.17 us -> 0.06 us  [the longest x1 0.04 us: body(): jnp.concatenate([half] + [swap_seq(half, b) for b in far_bits], axis=0)]
    ppermute x0 -> x2, starting transfers between devices: none -> 3.05 us  [swap_rep(): return lax.ppermute(x, 'rep', [(i, i ^ 1) for i in range(rep_count)])]
  transfers between devices with their start and end apart: 21 -> 25, of which waited for: 10 -> 14; matrix products, arithmetic and copies ran while one was open for 8% -> 3% of each run, Pallas kernels for 14% -> 11%
where the time goes in v2:
time: 184 us; the launch traced here: 183 us
  waiting for transfers between devices  88.4 us (48%)
  starting transfers between devices  45.6 us (25%)
  Pallas kernels  29.1 us (16%)
  local copies, waits for them, and re-layouts  17 us (9%)
    ppermute x10, waiting for transfers between devices, swap_seq(): return lax.ppermute(x, 'seq', [(i, i ^ bit) for i in range(seq_count)])  72.3 us
    ppermute x10, starting transfers between devices, swap_seq(): return lax.ppermute(x, 'seq', [(i, i ^ bit) for i in range(seq_count)])  21.6 us
    all_to_all x4, starting transfers between devices, exchange(): return lax.all_to_all(x, 'seq', split_axis=0, concat_axis=0, tiled=True)  19.2 us
    unnamed x46, local copies, waits for them, and re-layouts  12.4 us
    ppermute x2, waiting for transfers between devices, swap_rep(): return lax.ppermute(x, 'rep', [(i, i ^ 1) for i in range(rep_count)])  11.4 us
    pallas_call x1, Pallas kernels, place_call(): pl.pallas_call(functools.partial(place_kernel, offsets), in_specs=[pl.Blo...  7.91 us
    pallas_call x1, Pallas kernels, mixed_call(): pl.pallas_call(mixed_kernel, grid=(rows // tile,), in_specs=[wspec, wspec...  4.57 us
    ppermute x9, waiting for transfers between devices, swap_core(): return lax.ppermute(x, 'chan', [(0, 1), (1, 0)])  4.27 us
  transfers between devices with their start and end apart: 25, of which 14 were waited for; matrix products, arithmetic and copies ran while one was open for 3% of the time, Pallas kernels for 11%

profile of v2, /device:TPU:0, one launch (start us, length us, event | category | flops | bytes accessed | tf_op | source)
XLA Modules:
  0.0 182.7 jit_solution(9588694464713371640)
XLA Ops:
  0.6 0.5 collective-permute-start.10
  1.2 0.4 copy-done
  1.6 5.1 %collective-permute-start.2 = (f32[1,32,1024]{2,1,0:T(8,128)S(1)}, f32[1,32,1024]{2,1,0:T(8,128)S(1)}, u32[]{:S(2)}, u32[]{:S(2)}) collective-permute-start(f32[1,32,1024]{2,1,0:T(8,128)S(1)} %dynamic-slice_bitcast_fusion), channel_id=1, source_target_pairs={{0,12},{2,14},{4,8},{6,10},{8,4},{10,6},{12,0},{14,2},{1,13},{3,15... | collective-permute-start | bytes 393224 | tf_op jit(solution)/shard_map/ppermute | solution.py:378
  6.7 0.6 collective-permute-start
  7.4 1.1 fusion.4
  8.4 0.1 pad_add_fusion.ids_ref
  8.5 2.4 %copy.13 = f32[2,8,128,128]{3,2,0,1:T(8,128)} copy(f32[2,8,128,128]{3,2,1,0:T(8,128)} %bitcast.28) | data formatting | bytes 2097152 | tf_op jit(solution)/shard_map/reshape | solution.py:404
  10.9 0.2 collective-permute-done.2
  11.1 6.6 %collective-permute-done.1 = f32[1,32,1024]{2,1,0:T(8,128)S(1)} collective-permute-done((f32[1,32,1024]{2,1,0:T(8,128)S(1)}, f32[1,32,1024]{2,1,0:T(8,128)S(1)}, u32[]{:S(2)}, u32[]{:S(2)}) %collective-permute-start.1) | collective-permute-done | bytes 131104 | tf_op jit(solution)/shard_map/ppermute | solution.py:378
  17.9 3.1 %gate.1 = (f32[2048,128]{1,0:T(8,128)S(1)}, f32[2048,128]{1,0:T(8,128)S(1)}, f32[2,8,64,128]{3,2,1,0:T(8,128)S(1)}, f32[2,8,64,128]{3,2,1,0:T(8,128)}) custom-call(s32[3]{0:T(128)S(1)} %pad_add_fusion.ids_ref, f32[2048,128]{1,0:T(8,128)S(1)} %copy-done.12, f32[2048,128]{1,0:T(8,128)S(1)} %collective-permute-done.10.other_ref, f32[2048,128]{1,0:T(8,128)S(1)} %copy-done.13, ...), custom_call_target="tpu_custom_call" | custom-call | flops 402653184 | bytes 6291456 | tf_op jit(solution)/shard_map/gate/pallas_call | solution.py:66
  21.0 1.0 copy-done.10
  21.9 1.0 copy-done.14
  22.9 0.8 copy-done.18
  23.7 4.8 %all-to-all-start = ((f32[8,2,128,128]{3,2,1,0:T(8,128)}), f32[8,2,128,128]{3,2,1,0:T(8,128)S(1)}, u32[]{:S(2)}, u32[]{:S(2)}) async-start(f32[8,2,128,128]{3,2,1,0:T(8,128)} %bitcast.22), calls=%async_computation | async-start | bytes 2097152 | tf_op jit(solution)/shard_map/all_to_all | solution.py:381
  28.5 1.5 collective-permute-start.4
  30.0 2.0 %collective-permute-start.3 = (f32[4,32,1024]{2,1,0:T(8,128)S(1)}, f32[4,32,1024]{2,1,0:T(8,128)S(1)}, u32[]{:S(2)}, u32[]{:S(2)}) collective-permute-start(f32[4,32,1024]{2,1,0:T(8,128)S(1)} %pad_maximum_fusion.refs_0_), channel_id=1, source_target_pairs={{0,2},{2,0},{4,6},{6,4},{8,10},{10,8},{12,14},{14,12},{1,3},{3,1},... | collective-permute-start | bytes 1572872 | tf_op jit(solution)/shard_map/ppermute | solution.py:378
  32.0 1.0 spread.1
  33.1 8.0 %collective-permute-done.4.refs_2_ = f32[4,32,1024]{2,1,0:T(8,128)S(1)} collective-permute-done((f32[4,32,1024]{2,1,0:T(8,128)S(1)}, f32[4,32,1024]{2,1,0:T(8,128)S(1)}, u32[]{:S(2)}, u32[]{:S(2)}) %collective-permute-start.4) | collective-permute-done | bytes 524320 | tf_op jit(solution)/shard_map/ppermute | solution.py:375
  41.0 11.4 %collective-permute-done.3.refs_1_ = f32[4,32,1024]{2,1,0:T(8,128)S(1)} collective-permute-done((f32[4,32,1024]{2,1,0:T(8,128)S(1)}, f32[4,32,1024]{2,1,0:T(8,128)S(1)}, u32[]{:S(2)}, u32[]{:S(2)}) %collective-permute-start.3) | collective-permute-done | bytes 524320 | tf_op jit(solution)/shard_map/ppermute | solution.py:378
  52.5 0.8 copy-done.20
  53.3 0.3 all-to-all-done
  53.6 1.6 mix.1
  55.2 4.3 %all-to-all-start.2 = ((f32[8,2,128,128]{3,2,1,0:T(8,128)}), f32[8,2,128,128]{3,2,1,0:T(8,128)}, u32[]{:S(2)}, u32[]{:S(2)}) async-start(f32[8,2,128,128]{3,2,1,0:T(8,128)} %bitcast.9), calls=%async_computation.2 | async-start | bytes 2097152 | tf_op jit(solution)/shard_map/all_to_all | solution.py:381
  59.5 1.6 collective-permute-start.6
  61.1 2.0 %collective-permute-start.5 = (f32[2,32,1024]{2,1,0:T(8,128)S(1)}, f32[2,32,1024]{2,1,0:T(8,128)S(1)}, u32[]{:S(2)}, u32[]{:S(2)}) collective-permute-start(f32[2,32,1024]{2,1,0:T(8,128)S(1)} %slice.40), channel_id=1, source_target_pairs={{0,2},{2,0},{4,6},{6,4},{8,10},{10,8},{12,14},{14,12},{1,3},{3,1},... | collective-permute-start | bytes 786440 | tf_op jit(solution)/shard_map/ppermute | solution.py:378
  63.1 0.5 collective-permute-start.9
  63.7 0.1 collective-permute-start.8
  63.7 3.5 %collective-permute-done.6.refs_4_ = f32[2,32,1024]{2,1,0:T(8,128)S(1)} collective-permute-done((f32[2,32,1024]{2,1,0:T(8,128)S(1)}, f32[2,32,1024]{2,1,0:T(8,128)S(1)}, u32[]{:S(2)}, u32[]{:S(2)}) %collective-permute-start.6) | collective-permute-done | bytes 262176 | tf_op jit(solution)/shard_map/ppermute | solution.py:375
  67.2 9.9 %collective-permute-done.5.refs_3_ = f32[2,32,1024]{2,1,0:T(8,128)S(1)} collective-permute-done((f32[2,32,1024]{2,1,0:T(8,128)S(1)}, f32[2,32,1024]{2,1,0:T(8,128)S(1)}, u32[]{:S(2)}, u32[]{:S(2)}) %collective-permute-start.5) | collective-permute-done | bytes 262176 | tf_op jit(solution)/shard_map/ppermute | solution.py:378
  77.1 0.5 collective-permute-start.13
  77.7 1.0 collective-permute-done.12.refs_8_
  78.7 0.4 collective-permute-done.13.refs_9_
  79.1 1.0 copy-done.5
  80.1 1.0 copy-done.7
  81.1 1.0 copy-done.9
  82.2 7.9 %place.1 = (bf16[1024,1024]{1,0:T(8,128)(2,1)S(1)}, bf16[1024,1024]{1,0:T(8,128)(2,1)S(1)}) custom-call(s32[3]{0:T(128)S(1)} %pad_add_fusion.ids_ref, f32[4,32,1024]{2,1,0:T(8,128)S(1)} %copy-done.5, f32[4,32,1024]{2,1,0:T(8,128)S(1)} %copy-done.9, f32[4,32,1024]{2,1,0:T(8,128)S(1)} %copy-done.7, f32[2,32,1024]{2,1,0:T(8,128)S(1)} %collective-permute-done.5.refs_3_, ...), custom_call_target="tpu_custom_call" | custom-call | flops 1048576 | bytes 8388608 | tf_op jit(solution)/shard_map/place/pallas_call | solution.py:219
  90.1 3.3 %up.1 = f32[8,2,128,128]{3,2,1,0:T(8,128)S(1)} custom-call(bf16[1024,1024]{1,0:T(8,128)(2,1)S(1)} %get-tuple-element.35.hi_ref, bf16[1024,1024]{1,0:T(8,128)(2,1)S(1)} %get-tuple-element.36.lo_ref, f32[2,1024,128]{2,1,0:T(8,128)S(1)} %bitcast.26), custom_call_target="tpu_custom_call" | custom-call | flops 1610612736 | bytes 6291456 | tf_op jit(solution)/shard_map/up/pallas_call | solution.py:250
  93.4 1.3 copy-done.1
  94.7 1.0 copy-done.3
  95.7 5.9 %all-to-all-start.1 = ((f32[8,2,128,128]{3,2,1,0:T(8,128)}), f32[8,2,128,128]{3,2,1,0:T(8,128)}, u32[]{:S(2)}, u32[]{:S(2)}) async-start(f32[8,2,128,128]{3,2,1,0:T(8,128)} %copy-done.3), calls=%async_computation.1 | async-start | bytes 2097152 | tf_op jit(solution)/shard_map/all_to_all | solution.py:381
  101.7 2.9 %collective-permute-done.14.vb_ref = f32[8,2,128,128]{3,2,1,0:T(8,128)S(1)} collective-permute-done((f32[8,2,128,128]{3,2,1,0:T(8,128)}, f32[8,2,128,128]{3,2,1,0:T(8,128)S(1)}, u32[]{:S(2)}, u32[]{:S(2)}) %collective-permute-start.14) | collective-permute-done | bytes 1048608 | tf_op jit(solution)/shard_map/ppermute | solution.py:372
  104.5 1.0 copy-done.19
  105.6 1.0 copy-done.21
  106.6 4.2 %first.1 = (f32[4,32,1024]{2,1,0:T(8,128)S(1)}, f32[4,32,1024]{2,1,0:T(8,128)S(1)}, f32[4,32,1024]{2,1,0:T(8,128)S(1)}, f32[4,32,1024]{2,1,0:T(8,128)S(1)}) custom-call(s32[3]{0:T(128)S(1)} %pad_add_fusion.ids_ref, f32[2,8,64,128]{3,2,1,0:T(8,128)S(1)} %copy-done.19, f32[2,8,64,128]{3,2,1,0:T(8,128)S(1)} %copy-done.21, ...), custom_call_target="tpu_custom_call" | custom-call | flops 1610612736 | bytes 6291456 | tf_op jit(solution)/shard_map/first/pallas_call | solution.py:344
  110.8 2.1 %collective-permute-start.16 = (f32[4,32,1024]{2,1,0:T(8,128)S(1)}, f32[4,32,1024]{2,1,0:T(8,128)S(1)}, u32[]{:S(2)}, u32[]{:S(2)}) collective-permute-start(f32[4,32,1024]{2,1,0:T(8,128)S(1)} %get-tuple-element.44), channel_id=1, source_target_pairs={{0,4},{2,6},{4,0},{6,2},{8,12},{10,14},{12,8},{14,10},{1,5},{3,7},... | collective-permute-start | bytes 1572872 | tf_op jit(solution)/shard_map/ppermute | solution.py:378
  112.9 1.5 collective-permute-start.15
  114.4 4.6 %mixed.1 = f32[2,1024,128]{2,1,0:T(8,128)} custom-call(bf16[1024,1024]{1,0:T(8,128)(2,1)S(1)} %get-tuple-element.35.hi_ref, bf16[1024,1024]{1,0:T(8,128)(2,1)S(1)} %copy-done.2, f32[8,2,128,128]{3,2,1,0:T(8,128)} %all-to-all-done.2.va_ref.v_ref, f32[2,1024,128]{2,1,0:T(8,128)S(1)} %bitcast.25), custom_call_target="tpu_custom_call" | custom-call | flops 1610612736 | bytes 7340032 | tf_op jit(solution)/shard_map/mixed/pallas_call | solution.py:286
  119.0 13.8 %collective-permute-done.16 = f32[4,32,1024]{2,1,0:T(8,128)S(1)} collective-permute-done((f32[4,32,1024]{2,1,0:T(8,128)S(1)}, f32[4,32,1024]{2,1,0:T(8,128)S(1)}, u32[]{:S(2)}, u32[]{:S(2)}) %collective-permute-start.16) | collective-permute-done | bytes 524320 | tf_op jit(solution)/shard_map/ppermute | solution.py:378
  132.8 0.1 add.36
  132.9 0.1 add.35
  133.0 0.8 copy-done.17
  133.8 3.4 %mix_second.1 = f32[16,136,128]{2,1,0:T(8,128)} custom-call(bf16[256,256]{1,0:T(8,128)(2,1)S(1)} %get-tuple-element.25.kh, bf16[256,256]{1,0:T(8,128)(2,1)S(1)} %copy-done.17, f32[16,128,128]{2,1,0:T(8,128)} %bitcast.8.u_ref, f32[16,128,128]{2,1,0:T(8,128)S(1)} %bitcast.24), custom_call_target="tpu_custom_call" | custom-call | flops 805306368 | bytes 3145728 | tf_op jit(solution)/shard_map/mix_second/pallas_call | solution.py:183
  137.2 4.2 %all-to-all-start.3 = ((f32[8,2,136,128]{3,2,1,0:T(8,128)}), f32[8,2,136,128]{3,2,1,0:T(8,128)S(1)}, u32[]{:S(2)}, u32[]{:S(2)}) async-start(f32[8,2,136,128]{3,2,1,0:T(8,128)} %bitcast.12), calls=%async_computation.3 | async-start | bytes 2228224 | tf_op jit(solution)/shard_map/all_to_all | solution.py:381
  141.5 2.1 %collective-permute-start.18 = (f32[2,32,1024]{2,1,0:T(8,128)S(1)}, f32[2,32,1024]{2,1,0:T(8,128)S(1)}, u32[]{:S(2)}, u32[]{:S(2)}) collective-permute-start(f32[2,32,1024]{2,1,0:T(8,128)S(1)} %slice.46), channel_id=1, source_target_pairs={{0,2},{2,0},{4,6},{6,4},{8,10},{10,8},{12,14},{14,12},{1,3},{3,1},... | collective-permute-start | bytes 786440 | tf_op jit(solution)/shard_map/ppermute | solution.py:378
  143.6 1.5 collective-permute-start.17
  145.1 14.4 %collective-permute-done.18 = f32[2,32,1024]{2,1,0:T(8,128)S(1)} collective-permute-done((f32[2,32,1024]{2,1,0:T(8,128)S(1)}, f32[2,32,1024]{2,1,0:T(8,128)S(1)}, u32[]{:S(2)}, u32[]{:S(2)}) %collective-permute-start.18) | collective-permute-done | bytes 262176 | tf_op jit(solution)/shard_map/ppermute | solution.py:378
  159.6 5.3 %collective-permute-done.17 = f32[2,32,1024]{2,1,0:T(8,128)S(1)} collective-permute-done((f32[2,32,1024]{2,1,0:T(8,128)S(1)}, f32[2,32,1024]{2,1,0:T(8,128)S(1)}, u32[]{:S(2)}, u32[]{:S(2)}) %collective-permute-start.17) | collective-permute-done | bytes 262176 | tf_op jit(solution)/shard_map/ppermute | solution.py:378
  164.9 4.7 %collective-permute-start.19 = (f32[1,64,1024]{2,1,0:T(8,128)S(1)}, f32[1,64,1024]{2,1,0:T(8,128)S(1)}, u32[]{:S(2)}, u32[]{:S(2)}) collective-permute-start(f32[1,64,1024]{2,1,0:T(8,128)S(1)} %pad_maximum_fusion.1), channel_id=1, source_target_pairs={{0,8},{2,10},{4,12},{6,14},{8,0},{10,2},{12,4},{14,6},{1,9},{3,11}... | collective-permute-start | bytes 786440 | tf_op jit(solution)/shard_map/ppermute | solution.py:378
  169.6 10.5 %collective-permute-done.19 = f32[1,64,1024]{2,1,0:T(8,128)S(1)} collective-permute-done((f32[1,64,1024]{2,1,0:T(8,128)S(1)}, f32[1,64,1024]{2,1,0:T(8,128)S(1)}, u32[]{:S(2)}, u32[]{:S(2)}) %collective-permute-start.19) | collective-permute-done | bytes 262176 | tf_op jit(solution)/shard_map/ppermute | solution.py:378
  180.1 0.7 fusion.3
  180.8 0.1 collective-permute-start.20
  180.9 0.1 slice_bitcast_fusion
  181.0 1.1 copy.11
  182.1 0.6 bitcast_add_fusion
  (60 shorter events, 0.4 us)
Async XLA Ops:
  0.6 1.0 copy-start
  0.6 17.2 %collective-permute-start.10 = (f32[2048,128]{1,0:T(8,128)}, f32[2048,128]{1,0:T(8,128)S(1)}, u32[]{:S(2)}, u32[]{:S(2)}) collective-permute-start(f32[2048,128]{1,0:T(8,128)} %own_ref.1), channel_id=1, source_target_pairs={{0,1},{1,0},{2,3},{3,2},{4,5},{5,4},{6,7},{7,6},{8,9},{9,8},{10,11... | collective-permute-start | bytes 3145736 | tf_op jit(solution)/shard_map/ppermute | solution.py:372
  1.6 9.5 %collective-permute-start.2 = (f32[1,32,1024]{2,1,0:T(8,128)S(1)}, f32[1,32,1024]{2,1,0:T(8,128)S(1)}, u32[]{:S(2)}, u32[]{:S(2)}) collective-permute-start(f32[1,32,1024]{2,1,0:T(8,128)S(1)} %dynamic-slice_bitcast_fusion), channel_id=1, source_target_pairs={{0,12},{2,14},{4,8},{6,10},{8,4},{10,6},{12,0},{14,2},{1,13},{3,15... | collective-permute-start | bytes 393224 | tf_op jit(solution)/shard_map/ppermute | solution.py:378
  6.7 11.1 %collective-permute-start.1 = (f32[1,32,1024]{2,1,0:T(8,128)S(1)}, f32[1,32,1024]{2,1,0:T(8,128)S(1)}, u32[]{:S(2)}, u32[]{:S(2)}) collective-permute-start(f32[1,32,1024]{2,1,0:T(8,128)S(1)} %dynamic-slice_bitcast_fusion), channel_id=1, source_target_pairs={{0,8},{2,10},{4,12},{6,14},{8,0},{10,2},{12,4},{14,6},{1,9},{3,11}... | collective-permute-start | bytes 393224 | tf_op jit(solution)/shard_map/ppermute | solution.py:378
  6.7 11.1 %collective-permute-start = (f32[1,32,1024]{2,1,0:T(8,128)S(1)}, f32[1,32,1024]{2,1,0:T(8,128)S(1)}, u32[]{:S(2)}, u32[]{:S(2)}) collective-permute-start(f32[1,32,1024]{2,1,0:T(8,128)S(1)} %dynamic-slice_bitcast_fusion), channel_id=1, source_target_pairs={{0,4},{2,6},{4,0},{6,2},{8,12},{10,14},{12,8},{14,10},{1,5},{3,7},... | collective-permute-start | bytes 393224 | tf_op jit(solution)/shard_map/ppermute | solution.py:378
  8.5 9.4 %copy-start.13 = (f32[2048,128]{1,0:T(8,128)S(1)}, f32[2048,128]{1,0:T(8,128)}, u32[]{:S(2)}) copy-start(f32[2048,128]{1,0:T(8,128)} %gate_ref.1) | copy-start | bytes 3145732
  10.9 7.0 %copy-start.12 = (f32[2048,128]{1,0:T(8,128)S(1)}, f32[2048,128]{1,0:T(8,128)}, u32[]{:S(2)}) copy-start(f32[2048,128]{1,0:T(8,128)} %own_ref.1) | copy-start | bytes 3145732
  17.8 45.3 %copy-start.4 = (f32[4,32,1024]{2,1,0:T(8,128)}, f32[4,32,1024]{2,1,0:T(8,128)S(1)}, u32[]{:S(2)}) copy-start(f32[4,32,1024]{2,1,0:T(8,128)S(1)} %pad_maximum_fusion.refs_0_) | copy-start | bytes 1572868
  20.9 1.0 copy-start.10
  21.9 1.0 copy-start.14
  22.9 0.8 copy-start.18
  23.7 8.4 %copy-start.22 = (f32[16,16]{1,0:T(8,128)S(1)}, f32[16,16]{1,0:T(8,128)}, u32[]{:S(2)}) copy-start(f32[16,16]{1,0:T(8,128)} %w_ref.1) | copy-start | bytes 3076
  23.7 30.0 %all-to-all-start = ((f32[8,2,128,128]{3,2,1,0:T(8,128)}), f32[8,2,128,128]{3,2,1,0:T(8,128)S(1)}, u32[]{:S(2)}, u32[]{:S(2)}) async-start(f32[8,2,128,128]{3,2,1,0:T(8,128)} %bitcast.22), calls=%async_computation | async-start | bytes 2097152 | tf_op jit(solution)/shard_map/all_to_all | solution.py:381
  28.5 12.5 %collective-permute-start.4 = (f32[4,32,1024]{2,1,0:T(8,128)S(1)}, f32[4,32,1024]{2,1,0:T(8,128)S(1)}, u32[]{:S(2)}, u32[]{:S(2)}) collective-permute-start(f32[4,32,1024]{2,1,0:T(8,128)S(1)} %pad_maximum_fusion.refs_0_), channel_id=1, source_target_pairs={{0,16},{16,0},{1,17},{17,1},{2,18},{18,2},{3,19},{19,3},{4,20},{20... | collective-permute-start | bytes 1572872 | tf_op jit(solution)/shard_map/ppermute | solution.py:375
  30.0 22.5 %collective-permute-start.3 = (f32[4,32,1024]{2,1,0:T(8,128)S(1)}, f32[4,32,1024]{2,1,0:T(8,128)S(1)}, u32[]{:S(2)}, u32[]{:S(2)}) collective-permute-start(f32[4,32,1024]{2,1,0:T(8,128)S(1)} %pad_maximum_fusion.refs_0_), channel_id=1, source_target_pairs={{0,2},{2,0},{4,6},{6,4},{8,10},{10,8},{12,14},{14,12},{1,3},{3,1},... | collective-permute-start | bytes 1572872 | tf_op jit(solution)/shard_map/ppermute | solution.py:378
  32.0 20.4 %collective-permute-start.11 = (f32[2,8,64,128]{3,2,1,0:T(8,128)}, f32[2,8,64,128]{3,2,1,0:T(8,128)S(1)}, u32[]{:S(2)}, u32[]{:S(2)}) collective-permute-start(f32[2,8,64,128]{3,2,1,0:T(8,128)} %get-tuple-element.31), channel_id=1, source_target_pairs={{0,1},{1,0},{2,3},{3,2},{4,5},{5,4},{6,7},{7,6},{8,9},{9,8},{10,11... | collective-permute-start | bytes 1572872 | tf_op jit(solution)/shard_map/ppermute | solution.py:372
  33.1 22.2 %copy-start.16 = (bf16[256,256]{1,0:T(8,128)(2,1)}, bf16[256,256]{1,0:T(8,128)(2,1)S(1)}, u32[]{:S(2)}) copy-start(bf16[256,256]{1,0:T(8,128)(2,1)S(1)} %get-tuple-element.26.kl) | copy-start | bytes 393220
  41.0 22.1 %copy-start.6 = (f32[4,32,1024]{2,1,0:T(8,128)}, f32[4,32,1024]{2,1,0:T(8,128)S(1)}, u32[]{:S(2)}) copy-start(f32[4,32,1024]{2,1,0:T(8,128)S(1)} %collective-permute-done.4.refs_2_) | copy-start | bytes 1572868
  52.5 11.2 %copy-start.8 = (f32[4,32,1024]{2,1,0:T(8,128)}, f32[4,32,1024]{2,1,0:T(8,128)S(1)}, u32[]{:S(2)}) copy-start(f32[4,32,1024]{2,1,0:T(8,128)S(1)} %collective-permute-done.3.refs_1_) | copy-start | bytes 1572868
  52.5 0.8 copy-start.20
  55.2 40.5 %all-to-all-start.2 = ((f32[8,2,128,128]{3,2,1,0:T(8,128)}), f32[8,2,128,128]{3,2,1,0:T(8,128)}, u32[]{:S(2)}, u32[]{:S(2)}) async-start(f32[8,2,128,128]{3,2,1,0:T(8,128)} %bitcast.9), calls=%async_computation.2 | async-start | bytes 2097152 | tf_op jit(solution)/shard_map/all_to_all | solution.py:381
  59.5 7.7 %collective-permute-start.6 = (f32[2,32,1024]{2,1,0:T(8,128)S(1)}, f32[2,32,1024]{2,1,0:T(8,128)S(1)}, u32[]{:S(2)}, u32[]{:S(2)}) collective-permute-start(f32[2,32,1024]{2,1,0:T(8,128)S(1)} %slice.41), channel_id=1, source_target_pairs={{0,16},{16,0},{1,17},{17,1},{2,18},{18,2},{3,19},{19,3},{4,20},{20... | collective-permute-start | bytes 786440 | tf_op jit(solution)/shard_map/ppermute | solution.py:375
  61.1 16.0 %collective-permute-start.5 = (f32[2,32,1024]{2,1,0:T(8,128)S(1)}, f32[2,32,1024]{2,1,0:T(8,128)S(1)}, u32[]{:S(2)}, u32[]{:S(2)}) collective-permute-start(f32[2,32,1024]{2,1,0:T(8,128)S(1)} %slice.40), channel_id=1, source_target_pairs={{0,2},{2,0},{4,6},{6,4},{8,10},{10,8},{12,14},{14,12},{1,3},{3,1},... | collective-permute-start | bytes 786440 | tf_op jit(solution)/shard_map/ppermute | solution.py:378
  63.1 14.5 %collective-permute-start.7 = (f32[4,32,1024]{2,1,0:T(8,128)S(1)}, f32[4,32,1024]{2,1,0:T(8,128)S(1)}, u32[]{:S(2)}, u32[]{:S(2)}) collective-permute-start(f32[4,32,1024]{2,1,0:T(8,128)S(1)} %pad_maximum_fusion.refs_0_), channel_id=1, source_target_pairs={{0,1},{1,0},{2,3},{3,2},{4,5},{5,4},{6,7},{7,6},{8,9},{9,8},{10,11... | collective-permute-start | bytes 1572872 | tf_op jit(solution)/shard_map/ppermute | solution.py:372
  63.1 14.5 %collective-permute-start.9 = (f32[4,32,1024]{2,1,0:T(8,128)S(1)}, f32[4,32,1024]{2,1,0:T(8,128)S(1)}, u32[]{:S(2)}, u32[]{:S(2)}) collective-permute-start(f32[4,32,1024]{2,1,0:T(8,128)S(1)} %collective-permute-done.4.refs_2_), channel_id=1, source_target_pairs={{0,1},{1,0},{2,3},{3,2},{4,5},{5,4},{6,7},{7,6},{8,9},{9,8},{10,11... | collective-permute-start | bytes 1572872 | tf_op jit(solution)/shard_map/ppermute | solution.py:372
  63.7 14.0 %collective-permute-start.8 = (f32[4,32,1024]{2,1,0:T(8,128)S(1)}, f32[4,32,1024]{2,1,0:T(8,128)S(1)}, u32[]{:S(2)}, u32[]{:S(2)}) collective-permute-start(f32[4,32,1024]{2,1,0:T(8,128)S(1)} %collective-permute-done.3.refs_1_), channel_id=1, source_target_pairs={{0,1},{1,0},{2,3},{3,2},{4,5},{5,4},{6,7},{7,6},{8,9},{9,8},{10,11... | collective-permute-start | bytes 1572872 | tf_op jit(solution)/shard_map/ppermute | solution.py:372
  77.1 1.5 collective-permute-start.12
  77.1 1.9 %collective-permute-start.13 = (f32[2,32,1024]{2,1,0:T(8,128)S(1)}, f32[2,32,1024]{2,1,0:T(8,128)S(1)}, u32[]{:S(2)}, u32[]{:S(2)}) collective-permute-start(f32[2,32,1024]{2,1,0:T(8,128)S(1)} %collective-permute-done.6.refs_4_), channel_id=1, source_target_pairs={{0,1},{1,0},{2,3},{3,2},{4,5},{5,4},{6,7},{7,6},{8,9},{9,8},{10,11... | collective-permute-start | bytes 786440 | tf_op jit(solution)/shard_map/ppermute | solution.py:372
  79.1 1.0 copy-start.5
  80.1 1.0 copy-start.7
  81.1 1.0 copy-start.9
  82.2 7.9 %copy-start.15 = (f32[2048,128]{1,0:T(8,128)S(1)}, f32[2048,128]{1,0:T(8,128)}, u32[]{:S(2)}) copy-start(f32[2048,128]{1,0:T(8,128)} %copy-done.14) | copy-start | bytes 3145732
  93.4 1.3 copy-start.1
  94.7 1.0 copy-start.3
  95.7 37.3 %all-to-all-start.1 = ((f32[8,2,128,128]{3,2,1,0:T(8,128)}), f32[8,2,128,128]{3,2,1,0:T(8,128)}, u32[]{:S(2)}, u32[]{:S(2)}) async-start(f32[8,2,128,128]{3,2,1,0:T(8,128)} %copy-done.3), calls=%async_computation.1 | async-start | bytes 2097152 | tf_op jit(solution)/shard_map/all_to_all | solution.py:381
  101.6 2.9 %collective-permute-start.14 = (f32[8,2,128,128]{3,2,1,0:T(8,128)}, f32[8,2,128,128]{3,2,1,0:T(8,128)S(1)}, u32[]{:S(2)}, u32[]{:S(2)}) collective-permute-start(f32[8,2,128,128]{3,2,1,0:T(8,128)} %all-to-all-done.2.va_ref.v_ref), channel_id=1, source_target_pairs={{0,1},{1,0},{2,3},{3,2},{4,5},{5,4},{6,7},{7,6},{8,9},{9,8},{10,11... | collective-permute-start | bytes 3145736 | tf_op jit(solution)/shard_map/ppermute | solution.py:372
  104.5 1.0 copy-start.19
  105.6 1.0 copy-start.21
  106.6 7.8 %copy-start.2 = (bf16[1024,1024]{1,0:T(8,128)(2,1)S(1)}, bf16[1024,1024]{1,0:T(8,128)(2,1)}, u32[]{:S(2)}) copy-start(bf16[1024,1024]{1,0:T(8,128)(2,1)} %copy-done.1) | copy-start | bytes 6291460
  106.6 7.8 %copy-start.11 = (f32[2048,128]{1,0:T(8,128)S(1)}, f32[2048,128]{1,0:T(8,128)}, u32[]{:S(2)}) copy-start(f32[2048,128]{1,0:T(8,128)} %copy-done.10) | copy-start | bytes 3145732
  110.8 22.0 %collective-permute-start.16 = (f32[4,32,1024]{2,1,0:T(8,128)S(1)}, f32[4,32,1024]{2,1,0:T(8,128)S(1)}, u32[]{:S(2)}, u32[]{:S(2)}) collective-permute-start(f32[4,32,1024]{2,1,0:T(8,128)S(1)} %get-tuple-element.44), channel_id=1, source_target_pairs={{0,4},{2,6},{4,0},{6,2},{8,12},{10,14},{12,8},{14,10},{1,5},{3,7},... | collective-permute-start | bytes 1572872 | tf_op jit(solution)/shard_map/ppermute | solution.py:378
  112.9 20.0 %collective-permute-start.15 = (f32[4,32,1024]{2,1,0:T(8,128)S(1)}, f32[4,32,1024]{2,1,0:T(8,128)S(1)}, u32[]{:S(2)}, u32[]{:S(2)}) collective-permute-start(f32[4,32,1024]{2,1,0:T(8,128)S(1)} %get-tuple-element.39), channel_id=1, source_target_pairs={{0,2},{2,0},{4,6},{6,4},{8,10},{10,8},{12,14},{14,12},{1,3},{3,1},... | collective-permute-start | bytes 1572872 | tf_op jit(solution)/shard_map/ppermute | solution.py:378
  132.9 0.9 copy-start.17
  137.2 43.6 %all-to-all-start.3 = ((f32[8,2,136,128]{3,2,1,0:T(8,128)}), f32[8,2,136,128]{3,2,1,0:T(8,128)S(1)}, u32[]{:S(2)}, u32[]{:S(2)}) async-start(f32[8,2,136,128]{3,2,1,0:T(8,128)} %bitcast.12), calls=%async_computation.3 | async-start | bytes 2228224 | tf_op jit(solution)/shard_map/all_to_all | solution.py:381
  141.5 18.1 %collective-permute-start.18 = (f32[2,32,1024]{2,1,0:T(8,128)S(1)}, f32[2,32,1024]{2,1,0:T(8,128)S(1)}, u32[]{:S(2)}, u32[]{:S(2)}) collective-permute-start(f32[2,32,1024]{2,1,0:T(8,128)S(1)} %slice.46), channel_id=1, source_target_pairs={{0,2},{2,0},{4,6},{6,4},{8,10},{10,8},{12,14},{14,12},{1,3},{3,1},... | collective-permute-start | bytes 786440 | tf_op jit(solution)/shard_map/ppermute | solution.py:378
  143.6 21.3 %collective-permute-start.17 = (f32[2,32,1024]{2,1,0:T(8,128)S(1)}, f32[2,32,1024]{2,1,0:T(8,128)S(1)}, u32[]{:S(2)}, u32[]{:S(2)}) collective-permute-start(f32[2,32,1024]{2,1,0:T(8,128)S(1)} %slice.44), channel_id=1, source_target_pairs={{0,4},{2,6},{4,0},{6,2},{8,12},{10,14},{12,8},{14,10},{1,5},{3,7},... | collective-permute-start | bytes 786440 | tf_op jit(solution)/shard_map/ppermute | solution.py:378
  164.9 15.2 %collective-permute-start.19 = (f32[1,64,1024]{2,1,0:T(8,128)S(1)}, f32[1,64,1024]{2,1,0:T(8,128)S(1)}, u32[]{:S(2)}, u32[]{:S(2)}) collective-permute-start(f32[1,64,1024]{2,1,0:T(8,128)S(1)} %pad_maximum_fusion.1), channel_id=1, source_target_pairs={{0,8},{2,10},{4,12},{6,14},{8,0},{10,2},{12,4},{14,6},{1,9},{3,11}... | collective-permute-start | bytes 786440 | tf_op jit(solution)/shard_map/ppermute | solution.py:378
  180.8 1.3 collective-permute-start.20

commit v3 on v2

--- a/solution.py
+++ b/solution.py
@@ -28,6 +28,10 @@
         return lax.dot_general(u, v, dims, preferred_element_type=F32)
 
     return d(ah, bh) + (d(ah, bl) + d(al, bh))
+
+
+def hbm(x):
+    return pltpu.with_memory_space_constraint(x, pltpu.HBM)
 
 
 def params():
@@ -61,8 +65,8 @@
     count = tile // (2 * unit)
     row = pl.BlockSpec((tile, width), lambda i: (i, 0))
     part = pl.BlockSpec((1, count, unit, width), lambda i: (i // per, i % per, 0, 0))
-    shape = jax.ShapeDtypeStruct(own.shape, F32)
-    part_shape = jax.ShapeDtypeStruct((blocks, per * count, unit, width), F32)
+    shape = pltpu.HBM(own.shape, F32)
+    part_shape = pltpu.HBM((blocks, per * count, unit, width), F32)
     return pl.pallas_call(
         gate_kernel,
         grid=(blocks * per,),
@@ -78,7 +82,7 @@
         compiler_params=params(),
         cost_estimate=cost(6 * rows * width * 2 * width, 6 * 4 * rows * width),
         name="gate",
-    )(ids, own, other, gate, w)
+    )(ids, hbm(own), other, hbm(gate), w)
 
 
 def grouped(ref, group):
@@ -121,7 +125,7 @@
     size = w.shape[0] * group
     return pl.pallas_call(
         functools.partial(spread_kernel, group),
-        out_shape=[jax.ShapeDtypeStruct((size, size), BF16)] * 4,
+        out_shape=[pltpu.HBM((size, size), BF16)] * 4,
         compiler_params=params(),
         cost_estimate=cost(8 * size * size * w.shape[0], 8 * size * size),
         name="spread",
@@ -190,9 +194,7 @@
     )(*k, u, b)
 
 
-def place_kernel(offsets, ids_ref, *refs):
-    pieces = refs[: len(offsets)]
-    hi_ref, lo_ref, whole, sem = refs[len(offsets) :]
+def place_copies(offsets, ids_ref, pieces, whole, sem):
     half = pieces[0].shape[1]
     copies = []
     for piece, rels in zip(pieces, offsets):
@@ -201,99 +203,117 @@
             place = 2 * place + lax.bitwise_xor(ids_ref[2], flip)
             start = pl.multiple_of(place * half, half)
             copies.append(pltpu.make_async_copy(piece.at[u], whole.at[pl.ds(start, half)], sem.at[len(copies)]))
-    for c in copies:
+    return copies
+
+
+def up_kernel(offsets, ids_ref, g_ref, *refs):
+    pieces = refs[: len(offsets)]
+    o_ref, whole, g, o, sem, g_sem, o_sem = refs[len(offsets) :]
+    loads = place_copies(offsets, ids_ref, pieces, whole, sem)
+    g_load = pltpu.make_async_copy(g_ref, g, g_sem)
+    g_load.start()
+    for c in loads:
         c.start()
-    for c in copies:
+    g_load.wait()
+    blocks, rows, chan = g.shape
+    slices, _, width, _ = o.shape
+    both = split(jnp.concatenate([g[m] for m in range(blocks)], axis=1))
+    for c in loads:
+        c.wait()
+    tile = max(width, 256)
+    per = tile // width
+    stores = []
+    for n in range(rows // tile):
+        res = dot3(split(whole[:, n * tile : (n + 1) * tile]), both, TN)
+        for t in range(per):
+            for m in range(blocks):
+                o[n * per + t, m] = res[t * width : (t + 1) * width, m * chan : (m + 1) * chan]
+        part = pl.ds(n * per, per)
+        stores.append(pltpu.make_async_copy(o.at[part], o_ref.at[part], o_sem.at[n]))
+        stores[-1].start()
+    for c in stores:
+        c.wait()
+
+
+def up_call(ids, pieces, offsets, grad, slices, columns):
+    blocks, rows, chan = grad.shape
+    shape = (slices, blocks, rows // slices, chan)
+    space = pl.BlockSpec(memory_space=pltpu.HBM)
+    return pl.pallas_call(
+        functools.partial(up_kernel, offsets),
+        in_specs=[pl.BlockSpec(memory_space=pltpu.SMEM)] + [space] * (1 + len(pieces)),
+        out_specs=space,
+        out_shape=pltpu.HBM(shape, F32),
+        scratch_shapes=[
+            pltpu.VMEM((rows, columns), F32),
+            pltpu.VMEM(grad.shape, F32),
+            pltpu.VMEM(shape, F32),
+            pltpu.SemaphoreType.DMA((sum(map(len, offsets)),)),
+            pltpu.SemaphoreType.DMA,
+            pltpu.SemaphoreType.DMA((rows // 256,)),
+        ],
+        compiler_params=params(),
+        cost_estimate=cost(6 * rows * rows * blocks * chan, 4 * rows * rows + 8 * rows * blocks * chan),
+        name="up",
+    )(ids, hbm(grad), *map(hbm, pieces))
+
+
+def mixed_kernel(offsets, ids_ref, v_ref, f_ref, *refs):
+    pieces = refs[: len(offsets)]
+    o_ref, whole, v, f, o, sem, v_sem, o_sem = refs[len(offsets) :]
+    loads = place_copies(offsets, ids_ref, pieces, whole, sem)
+    v_loads = [
+        pltpu.make_async_copy(v_ref, v, v_sem.at[0]),
+        pltpu.make_async_copy(f_ref, f, v_sem.at[1]),
+    ]
+    for c in v_loads + loads:
+        c.start()
+    for c in v_loads:
+        c.wait()
+    slices, blocks, _, chan = v.shape
+    both = split(
+        jnp.concatenate(
+            [jnp.concatenate([v[t, m] for m in range(blocks)], axis=1) for t in range(slices)], axis=0
+        )
+    )
+    for c in loads:
         c.wait()
     rows = whole.shape[0]
     tile = 256
-    for t in range(rows // tile):
-        hi, lo = split(whole[t * tile : (t + 1) * tile, :])
-        hi_ref[t * tile : (t + 1) * tile, :] = hi
-        lo_ref[t * tile : (t + 1) * tile, :] = lo
-
-
-def place_call(ids, pieces, offsets, rows, columns):
-    shape = jax.ShapeDtypeStruct((rows, columns), BF16)
-    vmem = pl.BlockSpec(memory_space=pltpu.VMEM)
-    return pl.pallas_call(
-        functools.partial(place_kernel, offsets),
-        in_specs=[pl.BlockSpec(memory_space=pltpu.SMEM)] + [pl.BlockSpec(memory_space=pltpu.HBM)] * len(pieces),
-        out_specs=[vmem, vmem],
-        out_shape=[shape, shape],
-        scratch_shapes=[pltpu.VMEM((rows, columns), F32), pltpu.SemaphoreType.DMA((sum(map(len, offsets)),))],
-        compiler_params=params(),
-        cost_estimate=cost(rows * columns, 8 * rows * columns),
-        name="place",
-    )(ids, *pieces)
-
-
-def up_kernel(hi_ref, lo_ref, g_ref, o_ref, gh, gl):
-    @pl.when(pl.program_id(0) == 0)
-    def _():
-        both = jnp.concatenate([g_ref[m] for m in range(g_ref.shape[0])], axis=1)
-        gh[...], gl[...] = split(both)
-
-    res = dot3((hi_ref[...], lo_ref[...]), (gh[...], gl[...]), TN)
-    slices, blocks, width, chan = o_ref.shape
-    for t in range(slices):
+    stores = []
+    for n in range(rows // tile):
+        part = pl.ds(n * tile, tile)
+        res = dot3(split(whole[part, :]), both, NN)
         for m in range(blocks):
-            o_ref[t, m] = res[t * width : (t + 1) * width, m * chan : (m + 1) * chan]
-
-
-def up_call(hi, lo, grad, slices):
-    blocks, rows, chan = grad.shape
-    tile = 256
-    width = rows // slices
-    per = tile // width
-    wspec = pl.BlockSpec((rows, tile), lambda i: (0, i))
-    return pl.pallas_call(
-        up_kernel,
-        grid=(rows // tile,),
-        in_specs=[wspec, wspec, pl.BlockSpec(grad.shape, lambda i: (0, 0, 0))],
-        out_specs=pl.BlockSpec((per, blocks, width, chan), lambda i: (i, 0, 0, 0)),
-        out_shape=jax.ShapeDtypeStruct((slices, blocks, width, chan), F32),
-        scratch_shapes=[pltpu.VMEM((rows, blocks * chan), BF16)] * 2,
-        compiler_params=params(),
-        cost_estimate=cost(6 * rows * rows * blocks * chan, 4 * rows * rows + 8 * rows * blocks * chan),
-        name="up",
-    )(hi, lo, grad)
-
-
-def join(ref):
-    slices, blocks = ref.shape[0], ref.shape[1]
-    return jnp.concatenate(
-        [jnp.concatenate([ref[t, m] for m in range(blocks)], axis=1) for t in range(slices)], axis=0
-    )
-
-
-def mixed_kernel(hi_ref, lo_ref, v_ref, f_ref, o_ref, vh, vl):
-    @pl.when(pl.program_id(0) == 0)
-    def _():
-        vh[...], vl[...] = split(join(v_ref))
-
-    res = dot3((hi_ref[...], lo_ref[...]), (vh[...], vl[...]), NN)
-    chan = o_ref.shape[2]
-    for m in range(o_ref.shape[0]):
-        o_ref[m] = res[:, m * chan : (m + 1) * chan] * f_ref[m]
-
-
-def mixed_call(hi, lo, v, factor):
+            o[m, part, :] = res[:, m * chan : (m + 1) * chan] * f[m, part, :]
+        stores.append(pltpu.make_async_copy(o.at[:, part], o_ref.at[:, part], o_sem.at[n]))
+        stores[-1].start()
+    for c in stores:
+        c.wait()
+
+
+def mixed_call(ids, pieces, offsets, v, factor, columns):
     blocks, rows, chan = factor.shape
-    tile = 256
-    wspec = pl.BlockSpec((tile, rows), lambda i: (i, 0))
-    ospec = pl.BlockSpec((blocks, tile, chan), lambda i: (0, i, 0))
-    return pl.pallas_call(
-        mixed_kernel,
-        grid=(rows // tile,),
-        in_specs=[wspec, wspec, pl.BlockSpec(v.shape, lambda i: (0, 0, 0, 0)), ospec],
-        out_specs=ospec,
-        out_shape=jax.ShapeDtypeStruct(factor.shape, F32),
-        scratch_shapes=[pltpu.VMEM((rows, blocks * chan), BF16)] * 2,
+    space = pl.BlockSpec(memory_space=pltpu.HBM)
+    return pl.pallas_call(
+        functools.partial(mixed_kernel, offsets),
+        in_specs=[pl.BlockSpec(memory_space=pltpu.SMEM), pl.BlockSpec(memory_space=pl.ANY)]
+        + [space] * (1 + len(pieces)),
+        out_specs=space,
+        out_shape=pltpu.HBM(factor.shape, F32),
+        scratch_shapes=[
+            pltpu.VMEM((rows, columns), F32),
+            pltpu.VMEM(v.shape, F32),
+            pltpu.VMEM(factor.shape, F32),
+            pltpu.VMEM(factor.shape, F32),
+            pltpu.SemaphoreType.DMA((sum(map(len, offsets)),)),
+            pltpu.SemaphoreType.DMA((2,)),
+            pltpu.SemaphoreType.DMA((rows // 256,)),
+        ],
         compiler_params=params(),
         cost_estimate=cost(6 * rows * rows * blocks * chan, 4 * rows * rows + 12 * rows * blocks * chan),
         name="mixed",
-    )(hi, lo, v, factor)
+    )(ids, v, hbm(factor), *map(hbm, pieces))
 
 
 def flip_bits(q, bits):
@@ -351,7 +371,7 @@
         compiler_params=params(),
         cost_estimate=cost(6 * rows * count * unit * depth, 4 * (rows * count * unit + 2 * rows * depth)),
         name="first",
-    )(ids, grad_own, grad_other, v_own, v_other)
+    )(ids, hbm(grad_own), grad_other, v_own, v_other)
 
 
 def body(seq_count, rep_count, inputs, gate_in, out_grad, w_first, w_second, w_out):
@@ -386,7 +406,7 @@
     other_cot = swap_core(out_grad)
     half = lax.dynamic_slice_in_dim(w_first, side * (unit // 2), unit // 2, 0).reshape(1, unit // 2, columns)
     far_bits = range(2, seq_count, 2)
-    z_all = jnp.concatenate([half] + [swap_seq(half, b) for b in far_bits], axis=0)
+    z_far = [swap_seq(half, b) for b in far_bits]
     z_rel = (0, *far_bits)
 
     own_rows = lax.dynamic_slice_in_dim(w_out, h * chan, chan, 0)
@@ -400,22 +420,20 @@
     grad, factor, grad_own, grad_send = gate_call(ids, out_grad, other_cot, gate_in, w_cat, own, unit)
     grad_other = swap_core(grad_send)
     mixers = spread_call(w_second, group)
+    z_all = jnp.concatenate([after(half, grad, mixers[0])] + z_far, axis=0)
 
     sliced = inputs.reshape(own, seq_count, width, chan).transpose(1, 0, 2, 3)
-    block_cols = exchange(after(sliced, grad, z_all)).reshape(total, width, chan)
-
-    n = len(z_rel)
+    block_cols = exchange(after(sliced, z_all)).reshape(total, width, chan)
+
     y_all = swap_seq(z_all, 1)
     x_all = swap_rep(z_all)
-    yx_a = swap_seq(x_all[: n // 2], 1)
-    yx_b = swap_rep(y_all[n // 2 :])
-    pieces = [z_all, y_all, x_all, yx_a, yx_b]
+    yx_all = swap_rep(y_all)
+    pieces = [z_all, y_all, x_all, yx_all]
     offsets = [
         [(r, 0, 0) for r in z_rel],
         [(r ^ 1, 0, 0) for r in z_rel],
         [(r, 0, 1) for r in z_rel],
-        [(r ^ 1, 0, 1) for r in z_rel[: n // 2]],
-        [(r ^ 1, 0, 1) for r in z_rel[n // 2 :]],
+        [(r ^ 1, 0, 1) for r in z_rel],
     ]
 
     block_cols = after(block_cols, y_all, x_all, grad_other)
@@ -424,14 +442,17 @@
 
     far = [swap_core(p) for p in pieces[:3]] + [swap_core(after(p, v_cols)) for p in pieces[3:]]
     offsets += [[(r, 1, f) for r, _, f in o] for o in offsets]
-    hi, lo = place_call(ids, pieces + far, tuple(map(tuple, offsets)), rows, columns)
-    u = up_call(hi, lo, grad.reshape(own, rows, chan), seq_count)
+    pieces += far
+    offsets = tuple(map(tuple, offsets))
+    u = up_call(ids, pieces, offsets, grad.reshape(own, rows, chan), seq_count, columns)
     v = after(v, u)
     u_cols = exchange(u).reshape(total, width, chan)
 
     keep_a, send_a, keep_b, send_b = first_call(ids, grad_own, grad_other, v, swap_core(v))
     got_a, got_b = swap_seq(send_a, 1), swap_seq(send_b, 2)
-    gate_grad = mixed_call(hi, lo, after(v, send_a), factor.reshape(own, rows, chan)).reshape(inputs.shape)
+    gate_grad = mixed_call(
+        ids, pieces, offsets, after(v, send_a), factor.reshape(own, rows, chan), columns
+    ).reshape(inputs.shape)
     keep_a, keep_b = keep_a + got_a, keep_b + got_b
 
     in_cols = mix_second_call(

time: 184 us -> 163 us (0.89)
  local copies, waits for them, and re-layouts: 17 us -> 6.05 us
  starting transfers between devices: 45.6 us -> 40.9 us
  waiting for transfers between devices: 88.4 us -> 84.6 us
  Pallas kernels: 29.1 us -> 27 us
    ppermute x10 -> x9, waiting for transfers between devices: 72.3 us -> 55.5 us  [swap_seq(): return lax.ppermute(x, 'seq', [(i, i ^ bit) for i in range(seq_count)])]
    unnamed x46 -> x37, local copies, waits for them, and re-layouts: 12.4 us -> 2.42 us
    ppermute x2, waiting for transfers between devices: 11.4 us -> 20.5 us  [swap_rep(): return lax.ppermute(x, 'rep', [(i, i ^ 1) for i in range(rep_count)])]
    all_to_all x4, waiting for transfers between devices: 0.34 us -> 4.07 us  [exchange(): return lax.all_to_all(x, 'seq', split_axis=0, concat_axis=0, tiled=True)]
    all_to_all x4, starting transfers between devices: 19.2 us -> 16.7 us  [exchange(): return lax.all_to_all(x, 'seq', split_axis=0, concat_axis=0, tiled=True)]
    pallas_call x4 -> x3, Pallas kernels: 16.8 us -> 14.6 us  [the longest x1 6.46 us: up_call(): pl.pallas_call(functools.partial(up_kernel, offsets), in_specs=[pl.BlockS...]
    ppermute x10 -> x9, starting transfers between devices: 21.6 us -> 19.9 us  [swap_seq(): return lax.ppermute(x, 'seq', [(i, i ^ bit) for i in range(seq_count)])]
    ppermute x9 -> x8, waiting for transfers between devices: 4.27 us -> 4.52 us  [swap_core(): return lax.ppermute(x, 'chan', [(0, 1), (1, 0)])]
  transfers between devices with their start and end apart: 25 -> 23, of which waited for: 14 -> 12; matrix products, arithmetic and copies ran while one was open for 3% -> 3% of each run, Pallas kernels for 11% -> 14%
where the time goes in v3:
time: 163 us; the launch traced here: 162 us
  waiting for transfers between devices  84.6 us (52%)
  starting transfers between devices  40.9 us (25%)
  Pallas kernels  27 us (17%)
  local copies, waits for them, and re-layouts  6.05 us (4%)
  other arithmetic  2.44 us (1%)
    ppermute x9, waiting for transfers between devices, swap_seq(): return lax.ppermute(x, 'seq', [(i, i ^ bit) for i in range(seq_count)])  55.5 us
    ppermute x2, waiting for transfers between devices, swap_rep(): return lax.ppermute(x, 'rep', [(i, i ^ 1) for i in range(rep_count)])  20.5 us
    ppermute x9, starting transfers between devices, swap_seq(): return lax.ppermute(x, 'seq', [(i, i ^ bit) for i in range(seq_count)])  19.9 us
    all_to_all x4, starting transfers between devices, exchange(): return lax.all_to_all(x, 'seq', split_axis=0, concat_axis=0, tiled=True)  16.7 us
    pallas_call x1, Pallas kernels, up_call(): pl.pallas_call(functools.partial(up_kernel, offsets), in_specs=[pl.BlockS...  6.46 us
    pallas_call x1, Pallas kernels, mixed_call(): pl.pallas_call(functools.partial(mixed_kernel, offsets), in_specs=[pl.Blo...  6.46 us
    pallas_call x1, Pallas kernels, gate_call(): pl.pallas_call(gate_kernel, grid=(blocks * per,), in_specs=[pl.BlockSpec(...  4.65 us
    ppermute x8, waiting for transfers between devices, swap_core(): return lax.ppermute(x, 'chan', [(0, 1), (1, 0)])  4.52 us
  transfers between devices with their start and end apart: 23, of which 12 were waited for; matrix products, arithmetic and copies ran while one was open for 3% of the time, Pallas kernels for 14%

profile of v3, /device:TPU:0, one launch (start us, length us, event | category | flops | bytes accessed | tf_op | source)
XLA Modules:
  0.0 161.9 jit_solution(7883468004899144125)
XLA Ops:
  0.6 0.0 copy-start
  0.6 0.5 collective-permute-start
  1.2 0.4 copy-done
  1.6 0.0 copy-start.7
  1.6 0.0 copy-start.16
  1.6 5.1 %collective-permute-start.3 = (f32[1,32,1024]{2,1,0:T(8,128)S(1)}, f32[1,32,1024]{2,1,0:T(8,128)S(1)}, u32[]{:S(2)}, u32[]{:S(2)}) collective-permute-start(f32[1,32,1024]{2,1,0:T(8,128)S(1)} %dynamic-slice_bitcast_fusion), channel_id=1, source_target_pairs={{0,12},{2,14},{4,8},{6,10},{8,4},{10,6},{12,0},{14,2},{1,13},{3,15... | collective-permute-start | bytes 393224 | tf_op jit(solution)/shard_map/ppermute | solution.py:398
  6.7 0.0 collective-permute-start.2
  6.7 0.6 collective-permute-start.1
  7.4 2.3 %copy.13 = f32[2,8,128,128]{3,2,0,1:T(8,128)} copy(f32[2,8,128,128]{3,2,1,0:T(8,128)} %bitcast.27) | data formatting | bytes 2097152 | tf_op jit(solution)/shard_map/reshape | solution.py:425
  9.7 1.7 %spread.1 = (bf16[256,256]{1,0:T(8,128)(2,1)}, bf16[256,256]{1,0:T(8,128)(2,1)}, bf16[256,256]{1,0:T(8,128)(2,1)}, bf16[256,256]{1,0:T(8,128)(2,1)}) custom-call(f32[16,16]{1,0:T(8,128)S(1)} %copy-done.7), custom_call_target="tpu_custom_call" | custom-call | flops 8388608 | bytes 524288 | tf_op jit(solution)/shard_map/spread/pallas_call | solution.py:126
  11.4 0.1 pad_add_fusion.ids_ref
  11.5 0.1 fusion.4
  11.6 0.0 collective-permute-done.other_ref
  11.7 4.7 %gate.1 = (f32[2048,128]{1,0:T(8,128)}, f32[2048,128]{1,0:T(8,128)}, f32[2,8,64,128]{3,2,1,0:T(8,128)}, f32[2,8,64,128]{3,2,1,0:T(8,128)}) custom-call(s32[3]{0:T(128)S(1)} %pad_add_fusion.ids_ref, f32[2048,128]{1,0:T(8,128)} %own_ref.1, f32[2048,128]{1,0:T(8,128)S(1)} %collective-permute-done.other_ref, f32[2048,128]{1,0:T(8,128)} %gate_ref.1, ...), custom_call_target="tpu_custom_call" | custom-call | flops 402653184 | bytes 6291456 | tf_op jit(solution)/shard_map/gate/pallas_call | solution.py:70
  16.4 1.5 collective-permute-done.2
  17.8 0.0 collective-permute-done.3
  17.9 0.0 copy-start.1
  17.9 4.9 %all-to-all-start = ((f32[8,2,128,128]{3,2,1,0:T(8,128)}), f32[8,2,128,128]{3,2,1,0:T(8,128)S(1)}, u32[]{:S(2)}, u32[]{:S(2)}) async-start(f32[8,2,128,128]{3,2,1,0:T(8,128)} %bitcast.22), calls=%async_computation | async-start | bytes 2097152 | tf_op jit(solution)/shard_map/all_to_all | solution.py:401
  22.7 1.5 collective-permute-start.5
  24.2 2.0 %collective-permute-start.4 = (f32[4,32,1024]{2,1,0:T(8,128)S(1)}, f32[4,32,1024]{2,1,0:T(8,128)}, u32[]{:S(2)}, u32[]{:S(2)}) collective-permute-start(f32[4,32,1024]{2,1,0:T(8,128)S(1)} %constant_dynamic-update-slice_fusion.refs_0_), channel_id=1, source_target_pairs={{0,2},{2,0},{4,6},{6,4},{8,10},{10,8},{12,14},{14,12},{1,3},{3,1},... | collective-permute-start | bytes 1572872 | tf_op jit(solution)/shard_map/ppermute | solution.py:398
  26.3 0.0 collective-permute-start.10
  26.3 9.0 %collective-permute-done.5.refs_2_ = f32[4,32,1024]{2,1,0:T(8,128)S(1)} collective-permute-done((f32[4,32,1024]{2,1,0:T(8,128)S(1)}, f32[4,32,1024]{2,1,0:T(8,128)S(1)}, u32[]{:S(2)}, u32[]{:S(2)}) %collective-permute-start.5) | collective-permute-done | bytes 524320 | tf_op jit(solution)/shard_map/ppermute | solution.py:395
  35.3 11.5 %collective-permute-done.4.refs_1_ = f32[4,32,1024]{2,1,0:T(8,128)} collective-permute-done((f32[4,32,1024]{2,1,0:T(8,128)S(1)}, f32[4,32,1024]{2,1,0:T(8,128)}, u32[]{:S(2)}, u32[]{:S(2)}) %collective-permute-start.4) | collective-permute-done | bytes 524320 | tf_op jit(solution)/shard_map/ppermute | solution.py:398
  46.8 1.1 all-to-all-done
  47.9 1.6 mix.1
  49.5 3.6 %all-to-all-start.2 = ((f32[8,2,128,128]{3,2,1,0:T(8,128)}), f32[8,2,128,128]{3,2,1,0:T(8,128)S(1)}, u32[]{:S(2)}, u32[]{:S(2)}) async-start(f32[8,2,128,128]{3,2,1,0:T(8,128)} %bitcast.9), calls=%async_computation.2 | async-start | bytes 2097152 | tf_op jit(solution)/shard_map/all_to_all | solution.py:401
  53.0 1.6 collective-permute-start.6
  54.6 0.5 collective-permute-start.9
  55.1 0.1 collective-permute-start.8
  55.2 11.5 %collective-permute-done.6.refs_3_ = f32[4,32,1024]{2,1,0:T(8,128)S(1)} collective-permute-done((f32[4,32,1024]{2,1,0:T(8,128)}, f32[4,32,1024]{2,1,0:T(8,128)S(1)}, u32[]{:S(2)}, u32[]{:S(2)}) %collective-permute-start.6) | collective-permute-done | bytes 524320 | tf_op jit(solution)/shard_map/ppermute | solution.py:395
  66.6 0.0 collective-permute-start.11
  66.6 0.0 collective-permute-done.7.refs_4_
  66.7 0.0 collective-permute-done.9.refs_6_
  66.7 1.9 %collective-permute-done.11.refs_7_ = f32[4,32,1024]{2,1,0:T(8,128)S(1)} collective-permute-done((f32[4,32,1024]{2,1,0:T(8,128)S(1)}, f32[4,32,1024]{2,1,0:T(8,128)S(1)}, u32[]{:S(2)}, u32[]{:S(2)}) %collective-permute-start.11) | collective-permute-done | bytes 524320 | tf_op jit(solution)/shard_map/ppermute | solution.py:392
  68.6 0.8 copy-done.15
  69.3 6.5 %up.1 = f32[8,2,128,128]{3,2,1,0:T(8,128)} custom-call(s32[3]{0:T(128)S(1)} %pad_add_fusion.ids_ref, f32[2,1024,128]{2,1,0:T(8,128)} %bitcast.26, f32[4,32,1024]{2,1,0:T(8,128)} %copy-done.8, f32[4,32,1024]{2,1,0:T(8,128)} %collective-permute-done.4.refs_1_, f32[4,32,1024]{2,1,0:T(8,128)} %copy-done.10, f32[4,32,1024]{2,1,0:T(8,128)} %copy-done.11, ...), custom_call_target="tpu_custom_call" | custom-call | flops 1610612736 | bytes 6291456 | tf_op jit(solution)/shard_map/up/pallas_call | solution.py:242
  75.8 3.0 %all-to-all-done.2.va_ref.v_ref = f32[8,2,128,128]{3,2,1,0:T(8,128)S(1)} async-done(((f32[8,2,128,128]{3,2,1,0:T(8,128)}), f32[8,2,128,128]{3,2,1,0:T(8,128)S(1)}, u32[]{:S(2)}, u32[]{:S(2)}) %all-to-all-start.2) | async-done | bytes 1048608 | tf_op jit(solution)/shard_map/all_to_all | solution.py:401
  78.8 3.6 %all-to-all-start.1 = ((f32[8,2,128,128]{3,2,1,0:T(8,128)}), f32[8,2,128,128]{3,2,1,0:T(8,128)S(1)}, u32[]{:S(2)}, u32[]{:S(2)}) async-start(f32[8,2,128,128]{3,2,1,0:T(8,128)} %up.1), calls=%async_computation.1 | async-start | bytes 2097152 | tf_op jit(solution)/shard_map/all_to_all | solution.py:401
  82.5 0.0 collective-permute-start.12
  82.5 2.6 %collective-permute-done.12.vb_ref = f32[8,2,128,128]{3,2,1,0:T(8,128)S(1)} collective-permute-done((f32[8,2,128,128]{3,2,1,0:T(8,128)S(1)}, f32[8,2,128,128]{3,2,1,0:T(8,128)S(1)}, u32[]{:S(2)}, u32[]{:S(2)}) %collective-permute-start.12) | collective-permute-done | bytes 1048608 | tf_op jit(solution)/shard_map/ppermute | solution.py:392
  85.1 1.0 copy-done.6
  86.2 3.9 %first.1 = (f32[4,32,1024]{2,1,0:T(8,128)S(1)}, f32[4,32,1024]{2,1,0:T(8,128)S(1)}, f32[4,32,1024]{2,1,0:T(8,128)S(1)}, f32[4,32,1024]{2,1,0:T(8,128)S(1)}) custom-call(s32[3]{0:T(128)S(1)} %pad_add_fusion.ids_ref, f32[2,8,64,128]{3,2,1,0:T(8,128)} %get-tuple-element.34.ga_ref, f32[2,8,64,128]{3,2,1,0:T(8,128)S(1)} %copy-done.6, ...), custom_call_target="tpu_custom_call" | custom-call | flops 1610612736 | bytes 6291456 | tf_op jit(solution)/shard_map/first/pallas_call | solution.py:364
  90.1 2.1 %collective-permute-start.14 = (f32[4,32,1024]{2,1,0:T(8,128)S(1)}, f32[4,32,1024]{2,1,0:T(8,128)S(1)}, u32[]{:S(2)}, u32[]{:S(2)}) collective-permute-start(f32[4,32,1024]{2,1,0:T(8,128)S(1)} %get-tuple-element.40), channel_id=1, source_target_pairs={{0,4},{2,6},{4,0},{6,2},{8,12},{10,14},{12,8},{14,10},{1,5},{3,7},... | collective-permute-start | bytes 1572872 | tf_op jit(solution)/shard_map/ppermute | solution.py:398
  92.1 1.5 collective-permute-start.13
  93.6 6.5 %mixed.1 = f32[2,1024,128]{2,1,0:T(8,128)} custom-call(s32[3]{0:T(128)S(1)} %pad_add_fusion.ids_ref, f32[8,2,128,128]{3,2,1,0:T(8,128)S(1)} %all-to-all-done.2.va_ref.v_ref, f32[2,1024,128]{2,1,0:T(8,128)} %bitcast.29, f32[4,32,1024]{2,1,0:T(8,128)} %copy-done.8, f32[4,32,1024]{2,1,0:T(8,128)} %collective-permute-done.4.refs_1_, f32[4,32,1024]{2,1,0:T(8,128)} %copy-done.10, ...), custom_call_target="tpu_custom_call" | custom-call | flops 1610612736 | bytes 7340032 | tf_op jit(solution)/shard_map/mixed/pallas_call | solution.py:298
  100.1 13.1 %collective-permute-done.14 = f32[4,32,1024]{2,1,0:T(8,128)S(1)} collective-permute-done((f32[4,32,1024]{2,1,0:T(8,128)S(1)}, f32[4,32,1024]{2,1,0:T(8,128)S(1)}, u32[]{:S(2)}, u32[]{:S(2)}) %collective-permute-start.14) | collective-permute-done | bytes 524320 | tf_op jit(solution)/shard_map/ppermute | solution.py:398
  113.1 0.1 add.36
  113.2 0.9 add.35
  114.1 0.0 copy-done.3
  114.1 0.1 copy-done.4
  114.2 2.2 %mix_second.1 = f32[16,136,128]{2,1,0:T(8,128)} custom-call(bf16[256,256]{1,0:T(8,128)(2,1)S(1)} %copy-done.3, bf16[256,256]{1,0:T(8,128)(2,1)S(1)} %copy-done.4, f32[16,128,128]{2,1,0:T(8,128)S(1)} %bitcast.25, f32[16,128,128]{2,1,0:T(8,128)S(1)} %bitcast.24), custom_call_target="tpu_custom_call" | custom-call | flops 805306368 | bytes 3145728 | tf_op jit(solution)/shard_map/mix_second/pallas_call | solution.py:187
  116.4 4.7 %all-to-all-start.3 = ((f32[8,2,136,128]{3,2,1,0:T(8,128)}), f32[8,2,136,128]{3,2,1,0:T(8,128)S(1)}, u32[]{:S(2)}, u32[]{:S(2)}) async-start(f32[8,2,136,128]{3,2,1,0:T(8,128)} %bitcast.12), calls=%async_computation.3 | async-start | bytes 2228224 | tf_op jit(solution)/shard_map/all_to_all | solution.py:401
  121.1 2.1 %collective-permute-start.16 = (f32[2,32,1024]{2,1,0:T(8,128)S(1)}, f32[2,32,1024]{2,1,0:T(8,128)S(1)}, u32[]{:S(2)}, u32[]{:S(2)}) collective-permute-start(f32[2,32,1024]{2,1,0:T(8,128)S(1)} %slice.36), channel_id=1, source_target_pairs={{0,2},{2,0},{4,6},{6,4},{8,10},{10,8},{12,14},{14,12},{1,3},{3,1},... | collective-permute-start | bytes 786440 | tf_op jit(solution)/shard_map/ppermute | solution.py:398
  123.2 1.5 collective-permute-start.15
  124.7 14.1 %collective-permute-done.16 = f32[2,32,1024]{2,1,0:T(8,128)S(1)} collective-permute-done((f32[2,32,1024]{2,1,0:T(8,128)S(1)}, f32[2,32,1024]{2,1,0:T(8,128)S(1)}, u32[]{:S(2)}, u32[]{:S(2)}) %collective-permute-start.16) | collective-permute-done | bytes 262176 | tf_op jit(solution)/shard_map/ppermute | solution.py:398
  138.9 5.3 %collective-permute-done.15 = f32[2,32,1024]{2,1,0:T(8,128)S(1)} collective-permute-done((f32[2,32,1024]{2,1,0:T(8,128)S(1)}, f32[2,32,1024]{2,1,0:T(8,128)S(1)}, u32[]{:S(2)}, u32[]{:S(2)}) %collective-permute-start.15) | collective-permute-done | bytes 262176 | tf_op jit(solution)/shard_map/ppermute | solution.py:398
  144.2 5.0 %collective-permute-start.17 = (f32[1,64,1024]{2,1,0:T(8,128)S(1)}, f32[1,64,1024]{2,1,0:T(8,128)S(1)}, u32[]{:S(2)}, u32[]{:S(2)}) collective-permute-start(f32[1,64,1024]{2,1,0:T(8,128)S(1)} %pad_maximum_fusion), channel_id=1, source_target_pairs={{0,8},{2,10},{4,12},{6,14},{8,0},{10,2},{12,4},{14,6},{1,9},{3,11}... | collective-permute-start | bytes 786440 | tf_op jit(solution)/shard_map/ppermute | solution.py:398
  149.2 10.1 %collective-permute-done.17 = f32[1,64,1024]{2,1,0:T(8,128)S(1)} collective-permute-done((f32[1,64,1024]{2,1,0:T(8,128)S(1)}, f32[1,64,1024]{2,1,0:T(8,128)S(1)}, u32[]{:S(2)}, u32[]{:S(2)}) %collective-permute-start.17) | collective-permute-done | bytes 262176 | tf_op jit(solution)/shard_map/ppermute | solution.py:398
  159.3 0.7 fusion.3
  160.0 0.1 collective-permute-start.18
  160.1 0.1 slice_bitcast_fusion
  160.2 1.0 copy.11
  161.2 0.0 collective-permute-done.18
  161.3 0.6 bitcast_add_fusion
  (44 shorter events, 0.3 us)
Async XLA Ops:
  0.6 1.0 copy-start
  0.6 11.0 %collective-permute-start = (f32[2048,128]{1,0:T(8,128)}, f32[2048,128]{1,0:T(8,128)S(1)}, u32[]{:S(2)}, u32[]{:S(2)}) collective-permute-start(f32[2048,128]{1,0:T(8,128)} %own_ref.1), channel_id=1, source_target_pairs={{0,1},{1,0},{2,3},{3,2},{4,5},{5,4},{6,7},{7,6},{8,9},{9,8},{10,11... | collective-permute-start | bytes 3145736 | tf_op jit(solution)/shard_map/ppermute | solution.py:392
  1.6 8.1 %copy-start.7 = (f32[16,16]{1,0:T(8,128)S(1)}, f32[16,16]{1,0:T(8,128)}, u32[]{:S(2)}) copy-start(f32[16,16]{1,0:T(8,128)} %w_ref.1) | copy-start | bytes 3076
  1.6 9.9 %copy-start.16 = (f32[256,256]{1,0:T(8,128)S(1)}, f32[256,256]{1,0:T(8,128)}, u32[]{:S(2)}) copy-start(f32[256,256]{1,0:T(8,128)} %param.11) | copy-start | bytes 786436
  1.6 16.2 %collective-permute-start.3 = (f32[1,32,1024]{2,1,0:T(8,128)S(1)}, f32[1,32,1024]{2,1,0:T(8,128)S(1)}, u32[]{:S(2)}, u32[]{:S(2)}) collective-permute-start(f32[1,32,1024]{2,1,0:T(8,128)S(1)} %dynamic-slice_bitcast_fusion), channel_id=1, source_target_pairs={{0,12},{2,14},{4,8},{6,10},{8,4},{10,6},{12,0},{14,2},{1,13},{3,15... | collective-permute-start | bytes 393224 | tf_op jit(solution)/shard_map/ppermute | solution.py:398
  6.7 11.1 %collective-permute-start.2 = (f32[1,32,1024]{2,1,0:T(8,128)S(1)}, f32[1,32,1024]{2,1,0:T(8,128)S(1)}, u32[]{:S(2)}, u32[]{:S(2)}) collective-permute-start(f32[1,32,1024]{2,1,0:T(8,128)S(1)} %dynamic-slice_bitcast_fusion), channel_id=1, source_target_pairs={{0,8},{2,10},{4,12},{6,14},{8,0},{10,2},{12,4},{14,6},{1,9},{3,11}... | collective-permute-start | bytes 393224 | tf_op jit(solution)/shard_map/ppermute | solution.py:398
  6.7 9.6 %collective-permute-start.1 = (f32[1,32,1024]{2,1,0:T(8,128)S(1)}, f32[1,32,1024]{2,1,0:T(8,128)S(1)}, u32[]{:S(2)}, u32[]{:S(2)}) collective-permute-start(f32[1,32,1024]{2,1,0:T(8,128)S(1)} %dynamic-slice_bitcast_fusion), channel_id=1, source_target_pairs={{0,4},{2,6},{4,0},{6,2},{8,12},{10,14},{12,8},{14,10},{1,5},{3,7},... | collective-permute-start | bytes 393224 | tf_op jit(solution)/shard_map/ppermute | solution.py:398
  17.9 36.7 %copy-start.8 = (f32[4,32,1024]{2,1,0:T(8,128)}, f32[4,32,1024]{2,1,0:T(8,128)S(1)}, u32[]{:S(2)}) copy-start(f32[4,32,1024]{2,1,0:T(8,128)S(1)} %constant_dynamic-update-slice_fusion.refs_0_) | copy-start | bytes 1572868
  17.9 30.0 %copy-start.1 = (bf16[256,256]{1,0:T(8,128)(2,1)S(1)}, bf16[256,256]{1,0:T(8,128)(2,1)}, u32[]{:S(2)}) copy-start(bf16[256,256]{1,0:T(8,128)(2,1)} %get-tuple-element.26.kh) | copy-start | bytes 393220
  17.9 30.0 %copy-start.2 = (bf16[256,256]{1,0:T(8,128)(2,1)S(1)}, bf16[256,256]{1,0:T(8,128)(2,1)}, u32[]{:S(2)}) copy-start(bf16[256,256]{1,0:T(8,128)(2,1)} %get-tuple-element.28.kl) | copy-start | bytes 393220
  17.9 30.0 %all-to-all-start = ((f32[8,2,128,128]{3,2,1,0:T(8,128)}), f32[8,2,128,128]{3,2,1,0:T(8,128)S(1)}, u32[]{:S(2)}, u32[]{:S(2)}) async-start(f32[8,2,128,128]{3,2,1,0:T(8,128)} %bitcast.22), calls=%async_computation | async-start | bytes 2097152 | tf_op jit(solution)/shard_map/all_to_all | solution.py:401
  22.7 12.5 %collective-permute-start.5 = (f32[4,32,1024]{2,1,0:T(8,128)S(1)}, f32[4,32,1024]{2,1,0:T(8,128)S(1)}, u32[]{:S(2)}, u32[]{:S(2)}) collective-permute-start(f32[4,32,1024]{2,1,0:T(8,128)S(1)} %constant_dynamic-update-slice_fusion.refs_0_), channel_id=1, source_target_pairs={{0,16},{16,0},{1,17},{17,1},{2,18},{18,2},{3,19},{19,3},{4,20},{20... | collective-permute-start | bytes 1572872 | tf_op jit(solution)/shard_map/ppermute | solution.py:395
  24.2 22.6 %collective-permute-start.4 = (f32[4,32,1024]{2,1,0:T(8,128)S(1)}, f32[4,32,1024]{2,1,0:T(8,128)}, u32[]{:S(2)}, u32[]{:S(2)}) collective-permute-start(f32[4,32,1024]{2,1,0:T(8,128)S(1)} %constant_dynamic-update-slice_fusion.refs_0_), channel_id=1, source_target_pairs={{0,2},{2,0},{4,6},{6,4},{8,10},{10,8},{12,14},{14,12},{1,3},{3,1},... | collective-permute-start | bytes 1572872 | tf_op jit(solution)/shard_map/ppermute | solution.py:398
  26.3 20.5 %collective-permute-start.10 = (f32[2,8,64,128]{3,2,1,0:T(8,128)}, f32[2,8,64,128]{3,2,1,0:T(8,128)S(1)}, u32[]{:S(2)}, u32[]{:S(2)}) collective-permute-start(f32[2,8,64,128]{3,2,1,0:T(8,128)} %get-tuple-element.30), channel_id=1, source_target_pairs={{0,1},{1,0},{2,3},{3,2},{4,5},{5,4},{6,7},{7,6},{8,9},{9,8},{10,11... | collective-permute-start | bytes 1572872 | tf_op jit(solution)/shard_map/ppermute | solution.py:392
  35.3 19.3 %copy-start.10 = (f32[4,32,1024]{2,1,0:T(8,128)}, f32[4,32,1024]{2,1,0:T(8,128)S(1)}, u32[]{:S(2)}) copy-start(f32[4,32,1024]{2,1,0:T(8,128)S(1)} %collective-permute-done.5.refs_2_) | copy-start | bytes 1572868
  46.8 2.7 %copy-start.5 = (f32[2,8,64,128]{3,2,1,0:T(8,128)}, f32[2,8,64,128]{3,2,1,0:T(8,128)S(1)}, u32[]{:S(2)}) copy-start(f32[2,8,64,128]{3,2,1,0:T(8,128)S(1)} %collective-permute-done.10.gb_ref) | copy-start | bytes 1572868
  49.5 29.4 %all-to-all-start.2 = ((f32[8,2,128,128]{3,2,1,0:T(8,128)}), f32[8,2,128,128]{3,2,1,0:T(8,128)S(1)}, u32[]{:S(2)}, u32[]{:S(2)}) async-start(f32[8,2,128,128]{3,2,1,0:T(8,128)} %bitcast.9), calls=%async_computation.2 | async-start | bytes 2097152 | tf_op jit(solution)/shard_map/all_to_all | solution.py:401
  53.0 13.6 %collective-permute-start.6 = (f32[4,32,1024]{2,1,0:T(8,128)}, f32[4,32,1024]{2,1,0:T(8,128)S(1)}, u32[]{:S(2)}, u32[]{:S(2)}) collective-permute-start(f32[4,32,1024]{2,1,0:T(8,128)} %collective-permute-done.4.refs_1_), channel_id=1, source_target_pairs={{0,16},{16,0},{1,17},{17,1},{2,18},{18,2},{3,19},{19,3},{4,20},{20... | collective-permute-start | bytes 1572872 | tf_op jit(solution)/shard_map/ppermute | solution.py:395
  54.6 12.1 %collective-permute-start.7 = (f32[4,32,1024]{2,1,0:T(8,128)S(1)}, f32[4,32,1024]{2,1,0:T(8,128)S(1)}, u32[]{:S(2)}, u32[]{:S(2)}) collective-permute-start(f32[4,32,1024]{2,1,0:T(8,128)S(1)} %constant_dynamic-update-slice_fusion.refs_0_), channel_id=1, source_target_pairs={{0,1},{1,0},{2,3},{3,2},{4,5},{5,4},{6,7},{7,6},{8,9},{9,8},{10,11... | collective-permute-start | bytes 1572872 | tf_op jit(solution)/shard_map/ppermute | solution.py:392
  54.6 12.1 %collective-permute-start.9 = (f32[4,32,1024]{2,1,0:T(8,128)S(1)}, f32[4,32,1024]{2,1,0:T(8,128)S(1)}, u32[]{:S(2)}, u32[]{:S(2)}) collective-permute-start(f32[4,32,1024]{2,1,0:T(8,128)S(1)} %collective-permute-done.5.refs_2_), channel_id=1, source_target_pairs={{0,1},{1,0},{2,3},{3,2},{4,5},{5,4},{6,7},{7,6},{8,9},{9,8},{10,11... | collective-permute-start | bytes 1572872 | tf_op jit(solution)/shard_map/ppermute | solution.py:392
  55.1 11.6 %collective-permute-start.8 = (f32[4,32,1024]{2,1,0:T(8,128)}, f32[4,32,1024]{2,1,0:T(8,128)S(1)}, u32[]{:S(2)}, u32[]{:S(2)}) collective-permute-start(f32[4,32,1024]{2,1,0:T(8,128)} %collective-permute-done.4.refs_1_), channel_id=1, source_target_pairs={{0,1},{1,0},{2,3},{3,2},{4,5},{5,4},{6,7},{7,6},{8,9},{9,8},{10,11... | collective-permute-start | bytes 1572872 | tf_op jit(solution)/shard_map/ppermute | solution.py:392
  66.6 1.9 %copy-start.11 = (f32[4,32,1024]{2,1,0:T(8,128)}, f32[4,32,1024]{2,1,0:T(8,128)S(1)}, u32[]{:S(2)}) copy-start(f32[4,32,1024]{2,1,0:T(8,128)S(1)} %collective-permute-done.6.refs_3_) | copy-start | bytes 1572868
  66.6 1.9 %collective-permute-start.11 = (f32[4,32,1024]{2,1,0:T(8,128)S(1)}, f32[4,32,1024]{2,1,0:T(8,128)S(1)}, u32[]{:S(2)}, u32[]{:S(2)}) collective-permute-start(f32[4,32,1024]{2,1,0:T(8,128)S(1)} %collective-permute-done.6.refs_3_), channel_id=1, source_target_pairs={{0,1},{1,0},{2,3},{3,2},{4,5},{5,4},{6,7},{7,6},{8,9},{9,8},{10,11... | collective-permute-start | bytes 1572872 | tf_op jit(solution)/shard_map/ppermute | solution.py:392
  66.7 1.9 %copy-start.12 = (f32[4,32,1024]{2,1,0:T(8,128)}, f32[4,32,1024]{2,1,0:T(8,128)S(1)}, u32[]{:S(2)}) copy-start(f32[4,32,1024]{2,1,0:T(8,128)S(1)} %collective-permute-done.7.refs_4_) | copy-start | bytes 1572868
  66.7 1.9 %copy-start.13 = (f32[4,32,1024]{2,1,0:T(8,128)}, f32[4,32,1024]{2,1,0:T(8,128)S(1)}, u32[]{:S(2)}) copy-start(f32[4,32,1024]{2,1,0:T(8,128)S(1)} %collective-permute-done.9.refs_6_) | copy-start | bytes 1572868
  66.7 1.9 %copy-start.14 = (f32[4,32,1024]{2,1,0:T(8,128)}, f32[4,32,1024]{2,1,0:T(8,128)S(1)}, u32[]{:S(2)}) copy-start(f32[4,32,1024]{2,1,0:T(8,128)S(1)} %collective-permute-done.8.refs_5_) | copy-start | bytes 1572868
  68.6 0.8 copy-start.15
  78.8 35.3 %all-to-all-start.1 = ((f32[8,2,128,128]{3,2,1,0:T(8,128)}), f32[8,2,128,128]{3,2,1,0:T(8,128)S(1)}, u32[]{:S(2)}, u32[]{:S(2)}) async-start(f32[8,2,128,128]{3,2,1,0:T(8,128)} %up.1), calls=%async_computation.1 | async-start | bytes 2097152 | tf_op jit(solution)/shard_map/all_to_all | solution.py:401
  82.5 2.7 %collective-permute-start.12 = (f32[8,2,128,128]{3,2,1,0:T(8,128)S(1)}, f32[8,2,128,128]{3,2,1,0:T(8,128)S(1)}, u32[]{:S(2)}, u32[]{:S(2)}) collective-permute-start(f32[8,2,128,128]{3,2,1,0:T(8,128)S(1)} %all-to-all-done.2.va_ref.v_ref), channel_id=1, source_target_pairs={{0,1},{1,0},{2,3},{3,2},{4,5},{5,4},{6,7},{7,6},{8,9},{9,8},{10,11... | collective-permute-start | bytes 3145736 | tf_op jit(solution)/shard_map/ppermute | solution.py:392
  85.1 1.0 copy-start.6
  90.1 23.1 %collective-permute-start.14 = (f32[4,32,1024]{2,1,0:T(8,128)S(1)}, f32[4,32,1024]{2,1,0:T(8,128)S(1)}, u32[]{:S(2)}, u32[]{:S(2)}) collective-permute-start(f32[4,32,1024]{2,1,0:T(8,128)S(1)} %get-tuple-element.40), channel_id=1, source_target_pairs={{0,4},{2,6},{4,0},{6,2},{8,12},{10,14},{12,8},{14,10},{1,5},{3,7},... | collective-permute-start | bytes 1572872 | tf_op jit(solution)/shard_map/ppermute | solution.py:398
  92.1 21.1 %collective-permute-start.13 = (f32[4,32,1024]{2,1,0:T(8,128)S(1)}, f32[4,32,1024]{2,1,0:T(8,128)S(1)}, u32[]{:S(2)}, u32[]{:S(2)}) collective-permute-start(f32[4,32,1024]{2,1,0:T(8,128)S(1)} %get-tuple-element.35), channel_id=1, source_target_pairs={{0,2},{2,0},{4,6},{6,4},{8,10},{10,8},{12,14},{14,12},{1,3},{3,1},... | collective-permute-start | bytes 1572872 | tf_op jit(solution)/shard_map/ppermute | solution.py:398
  113.2 0.9 copy-start.3
  113.2 1.0 copy-start.4
  116.4 6.8 %copy-start.9 = (f32[4,32,1024]{2,1,0:T(8,128)S(1)}, f32[4,32,1024]{2,1,0:T(8,128)}, u32[]{:S(2)}) copy-start(f32[4,32,1024]{2,1,0:T(8,128)} %add.35) | copy-start | bytes 1572868
  116.4 43.6 %all-to-all-start.3 = ((f32[8,2,136,128]{3,2,1,0:T(8,128)}), f32[8,2,136,128]{3,2,1,0:T(8,128)S(1)}, u32[]{:S(2)}, u32[]{:S(2)}) async-start(f32[8,2,136,128]{3,2,1,0:T(8,128)} %bitcast.12), calls=%async_computation.3 | async-start | bytes 2228224 | tf_op jit(solution)/shard_map/all_to_all | solution.py:401
  121.1 17.7 %collective-permute-start.16 = (f32[2,32,1024]{2,1,0:T(8,128)S(1)}, f32[2,32,1024]{2,1,0:T(8,128)S(1)}, u32[]{:S(2)}, u32[]{:S(2)}) collective-permute-start(f32[2,32,1024]{2,1,0:T(8,128)S(1)} %slice.36), channel_id=1, source_target_pairs={{0,2},{2,0},{4,6},{6,4},{8,10},{10,8},{12,14},{14,12},{1,3},{3,1},... | collective-permute-start | bytes 786440 | tf_op jit(solution)/shard_map/ppermute | solution.py:398
  123.2 20.9 %collective-permute-start.15 = (f32[2,32,1024]{2,1,0:T(8,128)S(1)}, f32[2,32,1024]{2,1,0:T(8,128)S(1)}, u32[]{:S(2)}, u32[]{:S(2)}) collective-permute-start(f32[2,32,1024]{2,1,0:T(8,128)S(1)} %slice.34), channel_id=1, source_target_pairs={{0,4},{2,6},{4,0},{6,2},{8,12},{10,14},{12,8},{14,10},{1,5},{3,7},... | collective-permute-start | bytes 786440 | tf_op jit(solution)/shard_map/ppermute | solution.py:398
  144.2 15.0 %collective-permute-start.17 = (f32[1,64,1024]{2,1,0:T(8,128)S(1)}, f32[1,64,1024]{2,1,0:T(8,128)S(1)}, u32[]{:S(2)}, u32[]{:S(2)}) collective-permute-start(f32[1,64,1024]{2,1,0:T(8,128)S(1)} %pad_maximum_fusion), channel_id=1, source_target_pairs={{0,8},{2,10},{4,12},{6,14},{8,0},{10,2},{12,4},{14,6},{1,9},{3,11}... | collective-permute-start | bytes 786440 | tf_op jit(solution)/shard_map/ppermute | solution.py:398
  160.0 1.2 collective-permute-start.18

commit v4 on v3

--- a/solution.py
+++ b/solution.py
@@ -144,7 +144,14 @@
         scatter_groups(o_ref.at[:, a : a + step], group, dot3(k, split(x), NN))
 
 
-def mix_second_kernel(group, scale, own, kh, kl, u_ref, b_ref, o_ref, acc):
+def scatter_rows(ids_ref, ref, pieces):
+    own = pieces[0].shape[0]
+    for d, piece in enumerate(pieces):
+        piece[...] = ref[pl.ds(own * lax.bitwise_xor(ids_ref[0], d), own)]
+
+
+def mix_second_kernel(group, scale, count, ids_ref, kh, kl, u_ref, b_ref, *refs):
+    outs, (o_ref, acc) = refs[:count], refs[count:]
     k = kh[...], kl[...]
     n, width, _ = u_ref.shape
     for a, step in spans(width, group):
@@ -164,10 +171,12 @@
         == lax.broadcasted_iota(jnp.int32, (size, lanes), 1)
     ).astype(F32)
     second = scale * jnp.dot(rows, pick, precision=lax.Precision.HIGHEST, preferred_element_type=F32)
+    own = n // count
     part = n // own
     for m in range(n):
         start = (m % own) * part
         o_ref[m, width:, :] = second[start : start + part, :]
+    scatter_rows(ids_ref, o_ref, outs)
 
 
 def mix_call(k, x, group):
@@ -181,17 +190,61 @@
     )(*k, x)
 
 
-def mix_second_call(k, u, b, group, own, scale):
+SMEM_SPEC = pl.BlockSpec(memory_space=pltpu.SMEM)
+VMEM_SPEC = pl.BlockSpec(memory_space=pltpu.VMEM)
+
+
+def mix_second_call(ids, k, u, b, group, count, scale):
     n, width, chan = u.shape
+    own = n // count
     size = n * group
-    return pl.pallas_call(
-        functools.partial(mix_second_kernel, group, scale, own),
-        out_shape=jax.ShapeDtypeStruct((n, width + n // own, chan), F32),
-        scratch_shapes=[pltpu.VMEM((size, size), F32)],
+    tall = width + n // own
+    return pl.pallas_call(
+        functools.partial(mix_second_kernel, group, scale, count),
+        in_specs=[SMEM_SPEC] + [VMEM_SPEC] * 4,
+        out_specs=[VMEM_SPEC] * count,
+        out_shape=[jax.ShapeDtypeStruct((own, tall, chan), F32)] * count,
+        scratch_shapes=[pltpu.VMEM((n, tall, chan), F32), pltpu.VMEM((size, size), F32)],
         compiler_params=params(),
         cost_estimate=cost(12 * size * n * width * chan, 12 * n * width * chan),
         name="mix_second",
-    )(*k, u, b)
+    )(ids, *k, u, b)
+
+
+def finish_kernel(width, ids_ref, *refs):
+    pieces, (o_ref, s_ref, sem) = refs[:-3], refs[-3:]
+    copies = []
+    for d, piece in enumerate(pieces):
+        start = pl.multiple_of(lax.bitwise_xor(ids_ref[0], d) * width, width)
+        copies.append(
+            pltpu.make_async_copy(piece.at[:, :width], o_ref.at[:, pl.ds(start, width)], sem.at[d])
+        )
+    for c in copies:
+        c.start()
+    total = pieces[0][:, width:, :]
+    for piece in pieces[1:]:
+        total = total + piece[:, width:, :]
+    s_ref[...] = total
+    for c in copies:
+        c.wait()
+
+
+def finish_call(ids, pieces, width):
+    own, tall, chan = pieces[0].shape
+    count = len(pieces)
+    return pl.pallas_call(
+        functools.partial(finish_kernel, width),
+        in_specs=[SMEM_SPEC] + [VMEM_SPEC] * count,
+        out_specs=[pl.BlockSpec(memory_space=pltpu.HBM), VMEM_SPEC],
+        out_shape=[
+            pltpu.HBM((own, count * width, chan), F32),
+            jax.ShapeDtypeStruct((own, tall - width, chan), F32),
+        ],
+        scratch_shapes=[pltpu.SemaphoreType.DMA((count,))],
+        compiler_params=params(),
+        cost_estimate=cost(0, 8 * own * tall * count * chan),
+        name="finish",
+    )(ids, *pieces)
 
 
 def place_copies(offsets, ids_ref, pieces, whole, sem):
@@ -323,55 +376,86 @@
     return r
 
 
-def first_kernel(bits, ids_ref, ga_ref, gb_ref, va_ref, vb_ref, ka_ref, sa_ref, kb_ref, sb_ref, lh, ll):
-    count, unit = ga_ref.shape[1], ga_ref.shape[2]
-    blocks = ga_ref.shape[0]
-
-    @pl.when(pl.program_id(0) == 0)
-    def _():
+def first_kernel(
+    bits, ids_ref, ga_hbm, gb_hbm, va_ref, vb_ref, ka_ref, sa_ref, kb_ref, sb_ref, ga_ref, gb_ref, lh, ll, sem
+):
+    blocks, count, unit, _ = ga_ref.shape
+    loads = [
+        pltpu.make_async_copy(ga_hbm, ga_ref, sem.at[0]),
+        pltpu.make_async_copy(gb_hbm, gb_ref, sem.at[1]),
+    ]
+    for c in loads:
+        c.start()
+    for c in loads:
+        c.wait()
+    slices, _, width, _ = va_ref.shape
+    for q in range(count):
+        src = lax.bitwise_xor(ids_ref[0], flip_bits(q, bits))
+        row = jnp.concatenate([r[m, src] for m in range(blocks) for r in (ga_ref, gb_ref)], axis=1)
+        lh[q * unit : (q + 1) * unit, :], ll[q * unit : (q + 1) * unit, :] = split(row)
+    left = lh[...], ll[...]
+    quarter, half = count // 4, unit // 2
+    tile = max(width, 256)
+    per = tile // width
+    for n in range(slices // per):
+        v = jnp.concatenate(
+            [
+                jnp.concatenate([r[t, m] for m in range(blocks) for r in (va_ref, vb_ref)], axis=1)
+                for t in range(n * per, (n + 1) * per)
+            ],
+            axis=0,
+        )
+        res = dot3(left, split(v), NT)
+        part = slice(n * tile, (n + 1) * tile)
         for q in range(count):
-            src = lax.bitwise_xor(ids_ref[0], flip_bits(q, bits))
-            row = jnp.concatenate([r[m, src] for m in range(blocks) for r in (ga_ref, gb_ref)], axis=1)
-            lh[q * unit : (q + 1) * unit, :], ll[q * unit : (q + 1) * unit, :] = split(row)
-
-    v = jnp.concatenate(
-        [
-            jnp.concatenate([r[t, m] for m in range(blocks) for r in (va_ref, vb_ref)], axis=1)
-            for t in range(va_ref.shape[0])
-        ],
-        axis=0,
-    )
-    res = dot3((lh[...], ll[...]), split(v), NT)
-    quarter, half = count // 4, unit // 2
-    for q in range(count):
-        r0, r1, rest = q // (2 * quarter), (q // quarter) % 2, q % quarter
-        (sa_ref if r0 else ka_ref)[r1 * quarter + rest] = res[q * unit : q * unit + half, :]
-        (sb_ref if r1 else kb_ref)[r0 * quarter + rest] = res[q * unit + half : (q + 1) * unit, :]
+            r0, r1, rest = q // (2 * quarter), (q // quarter) % 2, q % quarter
+            (sa_ref if r0 else ka_ref)[r1 * quarter + rest, :, part] = res[q * unit : q * unit + half, :]
+            (sb_ref if r1 else kb_ref)[r0 * quarter + rest, :, part] = res[q * unit + half : (q + 1) * unit, :]
 
 
 def first_call(ids, grad_own, grad_other, v_own, v_other):
     blocks, count, unit, chan = grad_own.shape
     slices, _, width, _ = v_own.shape
     rows = slices * width
-    tile = 256
-    per = tile // width
     bits = count.bit_length() - 1
-    gspec = pl.BlockSpec(grad_own.shape, lambda i: (0, 0, 0, 0))
-    vspec = pl.BlockSpec((per, blocks, width, chan), lambda i: (i, 0, 0, 0))
-    ospec = pl.BlockSpec((count // 2, unit // 2, tile), lambda i: (0, 0, i))
+    vmem = pl.BlockSpec(memory_space=pltpu.VMEM)
     shape = jax.ShapeDtypeStruct((count // 2, unit // 2, rows), F32)
     depth = 2 * blocks * chan
     return pl.pallas_call(
         functools.partial(first_kernel, bits),
-        grid=(rows // tile,),
-        in_specs=[pl.BlockSpec(memory_space=pltpu.SMEM), gspec, gspec, vspec, vspec],
-        out_specs=[ospec] * 4,
+        in_specs=[pl.BlockSpec(memory_space=pltpu.SMEM)]
+        + [pl.BlockSpec(memory_space=pltpu.HBM)] * 2
+        + [vmem] * 2,
+        out_specs=[vmem] * 4,
         out_shape=[shape] * 4,
-        scratch_shapes=[pltpu.VMEM((count * unit, depth), BF16)] * 2,
+        scratch_shapes=[pltpu.VMEM(grad_own.shape, F32)] * 2
+        + [pltpu.VMEM((count * unit, depth), BF16)] * 2
+        + [pltpu.SemaphoreType.DMA((2,))],
         compiler_params=params(),
         cost_estimate=cost(6 * rows * count * unit * depth, 4 * (rows * count * unit + 2 * rows * depth)),
         name="first",
-    )(ids, hbm(grad_own), grad_other, v_own, v_other)
+    )(ids, hbm(grad_own), hbm(grad_other), v_own, v_other)
+
+
+def sums_kernel(ka_ref, ga_ref, kb_ref, gb_ref, oa_ref, sa_ref, ob_ref, sb_ref):
+    half = oa_ref.shape[0]
+    for k_ref, g_ref, o_ref, s_ref in ((ka_ref, ga_ref, oa_ref, sa_ref), (kb_ref, gb_ref, ob_ref, sb_ref)):
+        s_ref[...] = k_ref[half:] + g_ref[half:]
+        o_ref[...] = k_ref[:half] + g_ref[:half]
+
+
+def sums_call(keep_a, got_a, keep_b, got_b):
+    half, unit, columns = keep_a.shape[0] // 2, *keep_a.shape[1:]
+    shape = jax.ShapeDtypeStruct((half, unit, columns), F32)
+    return pl.pallas_call(
+        sums_kernel,
+        in_specs=[VMEM_SPEC] * 4,
+        out_specs=[VMEM_SPEC] * 4,
+        out_shape=[shape] * 4,
+        compiler_params=params(),
+        cost_estimate=cost(4 * half * unit * columns, 48 * half * unit * columns),
+        name="sums",
+    )(keep_a, got_a, keep_b, got_b)
 
 
 def body(seq_count, rep_count, inputs, gate_in, out_grad, w_first, w_second, w_out):
@@ -403,6 +487,9 @@
     def after(x, *deps):
         return lax.optimization_barrier((x, *deps))[0]
 
+    def all_after(xs, *deps):
+        return lax.optimization_barrier((*xs, *deps))[: len(xs)]
+
     other_cot = swap_core(out_grad)
     half = lax.dynamic_slice_in_dim(w_first, side * (unit // 2), unit // 2, 0).reshape(1, unit // 2, columns)
     far_bits = range(2, seq_count, 2)
@@ -453,28 +540,35 @@
     gate_grad = mixed_call(
         ids, pieces, offsets, after(v, send_a), factor.reshape(own, rows, chan), columns
     ).reshape(inputs.shape)
-    keep_a, keep_b = keep_a + got_a, keep_b + got_b
-
-    in_cols = mix_second_call(
+
+    in_pieces = mix_second_call(
+        ids,
         mixers[2:],
-        after(u_cols, gate_grad, keep_a, keep_b),
+        after(u_cols, gate_grad),
         block_cols,
         group,
-        own,
+        seq_count,
         1.0 / math.sqrt(rows * 2 * chan),
     )
-    back = exchange(in_cols.reshape(seq_count, own, *in_cols.shape[1:]))
-    input_grad = back[:, :, :width].transpose(1, 0, 2, 3).reshape(inputs.shape)
-    second = jnp.sum(back[:, :, width:, :total], axis=0).reshape(total, total)
-    second = second + swap_core(second)
-
-    quarter = keep_a.shape[0] // 2
-    got_a, got_b = swap_seq(keep_a[quarter:], 2), swap_seq(keep_b[quarter:], 1)
-    keep = jnp.concatenate([keep_a[:quarter] + got_a, keep_b[:quarter] + got_b], axis=1)
+    got_a, got_b = all_after([got_a, got_b], in_pieces[0])
+    keep_a, send_a, keep_b, send_b = sums_call(keep_a, got_a, keep_b, got_b)
+    got_a, got_b = swap_seq(send_a, 2), swap_seq(send_b, 1)
+
+    back = {0: in_pieces[0]}
+    for d in reversed(range(1, seq_count)):
+        piece = in_pieces[d] if 2 * d >= seq_count else after(in_pieces[d], got_a, got_b)
+        back[d] = swap_seq(piece, d)
+
+    keep = jnp.concatenate([keep_a + got_a, keep_b + got_b], axis=1)
     for b in range(2, bits):
         part = keep.shape[0] // 2
         keep = keep[:part] + swap_seq(keep[part:], 1 << b)
     first_grad = keep.reshape(unit, columns) * (1.0 / math.sqrt(total * 2 * chan))
+
+    input_grad, second = finish_call(ids, [back[d] for d in range(seq_count)], width)
+    input_grad = input_grad.reshape(inputs.shape)
+    second = second[:, :, :total].reshape(total, total)
+    second = second + swap_core(second)
     return input_grad, gate_grad, first_grad, second
 
 

time: 163 us -> 156 us (0.957)
  waiting for transfers between devices: 84.6 us -> 70.8 us
  starting transfers between devices: 40.9 us -> 45.4 us
  Pallas kernels: 27 us -> 30.1 us
    ppermute x9 -> x16, waiting for transfers between devices: 55.5 us -> 33.3 us  [swap_seq(): return lax.ppermute(x, 'seq', [(i, i ^ bit) for i in range(seq_count)])]
    ppermute x9 -> x16, starting transfers between devices: 19.9 us -> 29.1 us  [swap_seq(): return lax.ppermute(x, 'seq', [(i, i ^ bit) for i in range(seq_count)])]
    all_to_all x4 -> x3, waiting for transfers between devices: 4.07 us -> 11.3 us  [exchange(): return lax.all_to_all(x, 'seq', split_axis=0, concat_axis=0, tiled=True)]
    all_to_all x4 -> x3, starting transfers between devices: 16.7 us -> 12.1 us  [exchange(): return lax.all_to_all(x, 'seq', split_axis=0, concat_axis=0, tiled=True)]
    pallas_call x2 -> x4, Pallas kernels: 6.11 us -> 9.3 us  [the longest x1 4.62 us: first_call(): pl.pallas_call(functools.partial(first_kernel, bits), in_specs=[pl.BlockS...]
    unnamed x37 -> x41, local copies, waits for them, and re-layouts: 2.42 us -> 3.84 us
  transfers between devices with their start and end apart: 23 -> 29, of which waited for: 12 -> 15; matrix products, arithmetic and copies ran while one was open for 3% -> 2% of each run, Pallas kernels for 14% -> 18%
where the time goes in v4:
time: 156 us; the launch traced here: 155 us
  waiting for transfers between devices  70.8 us (45%)
  starting transfers between devices  45.4 us (29%)
  Pallas kernels  30.1 us (19%)
  local copies, waits for them, and re-layouts  6.36 us (4%)
    ppermute x16, waiting for transfers between devices, swap_seq(): return lax.ppermute(x, 'seq', [(i, i ^ bit) for i in range(seq_count)])  33.3 us
    ppermute x16, starting transfers between devices, swap_seq(): return lax.ppermute(x, 'seq', [(i, i ^ bit) for i in range(seq_count)])  29.1 us
    ppermute x2, waiting for transfers between devices, swap_rep(): return lax.ppermute(x, 'rep', [(i, i ^ 1) for i in range(rep_count)])  20.5 us
    all_to_all x3, starting transfers between devices, exchange(): return lax.all_to_all(x, 'seq', split_axis=0, concat_axis=0, tiled=True)  12.1 us
    all_to_all x3, waiting for transfers between devices, exchange(): return lax.all_to_all(x, 'seq', split_axis=0, concat_axis=0, tiled=True)  11.3 us
    pallas_call x1, Pallas kernels, mixed_call(): pl.pallas_call(functools.partial(mixed_kernel, offsets), in_specs=[pl.Blo...  6.46 us
    pallas_call x1, Pallas kernels, up_call(): pl.pallas_call(functools.partial(up_kernel, offsets), in_specs=[pl.BlockS...  6.43 us
    ppermute x8, waiting for transfers between devices, swap_core(): return lax.ppermute(x, 'chan', [(0, 1), (1, 0)])  5.67 us
  transfers between devices with their start and end apart: 29, of which 15 were waited for; matrix products, arithmetic and copies ran while one was open for 2% of the time, Pallas kernels for 18%

profile of v4, /device:TPU:0, one launch (start us, length us, event | category | flops | bytes accessed | tf_op | source)
XLA Modules:
  0.0 155.2 jit_solution(12631940761089997334)
XLA Ops:
  0.6 0.0 copy-start
  0.6 0.5 collective-permute-start
  1.2 0.4 copy-done
  1.6 5.1 %collective-permute-start.3 = (f32[1,32,1024]{2,1,0:T(8,128)S(1)}, f32[1,32,1024]{2,1,0:T(8,128)S(1)}, u32[]{:S(2)}, u32[]{:S(2)}) collective-permute-start(f32[1,32,1024]{2,1,0:T(8,128)S(1)} %dynamic-slice_bitcast_fusion), channel_id=1, source_target_pairs={{0,12},{2,14},{4,8},{6,10},{8,4},{10,6},{12,0},{14,2},{1,13},{3,15... | collective-permute-start | bytes 393224 | tf_op jit(solution)/shard_map/ppermute | solution.py:482
  6.7 0.6 collective-permute-start.1
  7.4 2.4 %copy.12 = f32[2,8,128,128]{3,2,0,1:T(8,128)} copy(f32[2,8,128,128]{3,2,1,0:T(8,128)} %bitcast.26) | data formatting | bytes 2097152 | tf_op jit(solution)/shard_map/reshape | solution.py:512
  9.7 1.7 %spread.1 = (bf16[256,256]{1,0:T(8,128)(2,1)}, bf16[256,256]{1,0:T(8,128)(2,1)}, bf16[256,256]{1,0:T(8,128)(2,1)}, bf16[256,256]{1,0:T(8,128)(2,1)}) custom-call(f32[16,16]{1,0:T(8,128)S(1)} %copy-done.7), custom_call_target="tpu_custom_call" | custom-call | flops 8388608 | bytes 524288 | tf_op jit(solution)/shard_map/spread/pallas_call | solution.py:126
  11.5 0.1 pad_add_fusion.ids_ref
  11.5 0.1 fusion.5
  11.7 0.0 collective-permute-done.other_ref
  11.7 4.6 %gate.1 = (f32[2048,128]{1,0:T(8,128)}, f32[2048,128]{1,0:T(8,128)}, f32[2,8,64,128]{3,2,1,0:T(8,128)}, f32[2,8,64,128]{3,2,1,0:T(8,128)}) custom-call(s32[3]{0:T(128)S(1)} %pad_add_fusion.ids_ref, f32[2048,128]{1,0:T(8,128)} %own_ref.1, f32[2048,128]{1,0:T(8,128)S(1)} %collective-permute-done.other_ref, f32[2048,128]{1,0:T(8,128)} %gate_ref.1, ...), custom_call_target="tpu_custom_call" | custom-call | flops 402653184 | bytes 6291456 | tf_op jit(solution)/shard_map/gate/pallas_call | solution.py:70
  16.3 0.0 collective-permute-done.1
  16.4 1.4 collective-permute-done.2
  17.8 0.0 copy-start.5
  17.9 4.9 %all-to-all-start = ((f32[8,2,128,128]{3,2,1,0:T(8,128)}), f32[8,2,128,128]{3,2,1,0:T(8,128)S(1)}, u32[]{:S(2)}, u32[]{:S(2)}) async-start(f32[8,2,128,128]{3,2,1,0:T(8,128)} %bitcast.21), calls=%async_computation | async-start | bytes 2097152 | tf_op jit(solution)/shard_map/all_to_all | solution.py:485
  22.7 1.5 collective-permute-start.5
  24.2 2.0 %collective-permute-start.4 = (f32[4,32,1024]{2,1,0:T(8,128)S(1)}, f32[4,32,1024]{2,1,0:T(8,128)S(1)}, u32[]{:S(2)}, u32[]{:S(2)}) collective-permute-start(f32[4,32,1024]{2,1,0:T(8,128)S(1)} %constant_dynamic-update-slice_fusion.refs_0_), channel_id=1, source_target_pairs={{0,2},{2,0},{4,6},{6,4},{8,10},{10,8},{12,14},{14,12},{1,3},{3,1},... | collective-permute-start | bytes 1572872 | tf_op jit(solution)/shard_map/ppermute | solution.py:482
  26.2 9.0 %collective-permute-done.5.refs_2_ = f32[4,32,1024]{2,1,0:T(8,128)S(1)} collective-permute-done((f32[4,32,1024]{2,1,0:T(8,128)S(1)}, f32[4,32,1024]{2,1,0:T(8,128)S(1)}, u32[]{:S(2)}, u32[]{:S(2)}) %collective-permute-start.5) | collective-permute-done | bytes 524320 | tf_op jit(solution)/shard_map/ppermute | solution.py:479
  35.2 11.4 %collective-permute-done.4.refs_1_ = f32[4,32,1024]{2,1,0:T(8,128)S(1)} collective-permute-done((f32[4,32,1024]{2,1,0:T(8,128)S(1)}, f32[4,32,1024]{2,1,0:T(8,128)S(1)}, u32[]{:S(2)}, u32[]{:S(2)}) %collective-permute-start.4) | collective-permute-done | bytes 524320 | tf_op jit(solution)/shard_map/ppermute | solution.py:482
  46.7 0.0 collective-permute-done.10.gb_hbm
  46.7 1.2 all-to-all-done
  47.8 1.6 %mix.1 = f32[16,128,128]{2,1,0:T(8,128)} custom-call(bf16[256,256]{1,0:T(8,128)(2,1)S(1)} %copy-done.5, bf16[256,256]{1,0:T(8,128)(2,1)S(1)} %copy-done.6, f32[16,128,128]{2,1,0:T(8,128)S(1)} %bitcast.22), custom_call_target="tpu_custom_call" | custom-call | flops 402653184 | bytes 2097152 | tf_op jit(solution)/shard_map/mix/pallas_call | solution.py:184
  49.4 3.6 %all-to-all-start.2 = ((f32[8,2,128,128]{3,2,1,0:T(8,128)}), f32[8,2,128,128]{3,2,1,0:T(8,128)S(1)}, u32[]{:S(2)}, u32[]{:S(2)}) async-start(f32[8,2,128,128]{3,2,1,0:T(8,128)} %bitcast.9), calls=%async_computation.2 | async-start | bytes 2097152 | tf_op jit(solution)/shard_map/all_to_all | solution.py:485
  53.0 1.6 %collective-permute-start.6 = (f32[4,32,1024]{2,1,0:T(8,128)}, f32[4,32,1024]{2,1,0:T(8,128)S(1)}, u32[]{:S(2)}, u32[]{:S(2)}) collective-permute-start(f32[4,32,1024]{2,1,0:T(8,128)} %copy-done.12), channel_id=1, source_target_pairs={{0,16},{16,0},{1,17},{17,1},{2,18},{18,2},{3,19},{19,3},{4,20},{20... | collective-permute-start | bytes 1572872 | tf_op jit(solution)/shard_map/ppermute | solution.py:479
  54.6 0.5 collective-permute-start.9
  55.1 0.1 collective-permute-start.8
  55.1 11.5 %collective-permute-done.6.refs_3_ = f32[4,32,1024]{2,1,0:T(8,128)S(1)} collective-permute-done((f32[4,32,1024]{2,1,0:T(8,128)}, f32[4,32,1024]{2,1,0:T(8,128)S(1)}, u32[]{:S(2)}, u32[]{:S(2)}) %collective-permute-start.6) | collective-permute-done | bytes 524320 | tf_op jit(solution)/shard_map/ppermute | solution.py:479
  66.7 1.9 %collective-permute-done.11.refs_7_ = f32[4,32,1024]{2,1,0:T(8,128)S(1)} collective-permute-done((f32[4,32,1024]{2,1,0:T(8,128)S(1)}, f32[4,32,1024]{2,1,0:T(8,128)S(1)}, u32[]{:S(2)}, u32[]{:S(2)}) %collective-permute-start.11) | collective-permute-done | bytes 524320 | tf_op jit(solution)/shard_map/ppermute | solution.py:476
  68.6 0.8 copy-done.17
  69.3 6.4 %up.1 = f32[8,2,128,128]{3,2,1,0:T(8,128)} custom-call(s32[3]{0:T(128)S(1)} %pad_add_fusion.ids_ref, f32[2,1024,128]{2,1,0:T(8,128)} %bitcast.25, f32[4,32,1024]{2,1,0:T(8,128)} %copy-done.10, f32[4,32,1024]{2,1,0:T(8,128)} %copy-done.12, f32[4,32,1024]{2,1,0:T(8,128)} %copy-done.11, f32[4,32,1024]{2,1,0:T(8,128)} %copy-done.13, f32[4,32,1024]{2,1,0:T(8,128)} %copy-done.14, ...), custom_call_target="tpu_custom_call" | custom-call | flops 1610612736 | bytes 6291456 | tf_op jit(solution)/shard_map/up/pallas_call | solution.py:295
  75.8 3.0 %all-to-all-done.2.va_ref.v_ref = f32[8,2,128,128]{3,2,1,0:T(8,128)S(1)} async-done(((f32[8,2,128,128]{3,2,1,0:T(8,128)}), f32[8,2,128,128]{3,2,1,0:T(8,128)S(1)}, u32[]{:S(2)}, u32[]{:S(2)}) %all-to-all-start.2) | async-done | bytes 1048608 | tf_op jit(solution)/shard_map/all_to_all | solution.py:485
  78.8 3.6 %all-to-all-start.1 = ((f32[8,2,128,128]{3,2,1,0:T(8,128)}), f32[8,2,128,128]{3,2,1,0:T(8,128)S(1)}, u32[]{:S(2)}, u32[]{:S(2)}) async-start(f32[8,2,128,128]{3,2,1,0:T(8,128)} %up.1), calls=%async_computation.1 | async-start | bytes 2097152 | tf_op jit(solution)/shard_map/all_to_all | solution.py:485
  82.4 0.0 collective-permute-start.12
  82.5 2.6 %collective-permute-done.12.vb_ref = f32[8,2,128,128]{3,2,1,0:T(8,128)S(1)} collective-permute-done((f32[8,2,128,128]{3,2,1,0:T(8,128)S(1)}, f32[8,2,128,128]{3,2,1,0:T(8,128)S(1)}, u32[]{:S(2)}, u32[]{:S(2)}) %collective-permute-start.12) | collective-permute-done | bytes 1048608 | tf_op jit(solution)/shard_map/ppermute | solution.py:476
  85.1 4.6 %first.1 = (f32[4,32,1024]{2,1,0:T(8,128)S(1)}, f32[4,32,1024]{2,1,0:T(8,128)}, f32[4,32,1024]{2,1,0:T(8,128)S(1)}, f32[4,32,1024]{2,1,0:T(8,128)}) custom-call(s32[3]{0:T(128)S(1)} %pad_add_fusion.ids_ref, f32[2,8,64,128]{3,2,1,0:T(8,128)} %get-tuple-element.53.ga_hbm, f32[2,8,64,128]{3,2,1,0:T(8,128)} %collective-permute-done.10.gb_hbm, ...), custom_call_target="tpu_custom_call" | custom-call | flops 1610612736 | bytes 6291456 | tf_op jit(solution)/shard_map/first/pallas_call | solution.py:424
  89.8 0.8 copy-done.1
  90.5 0.8 copy-done.3
  91.4 2.0 %collective-permute-start.14 = (f32[4,32,1024]{2,1,0:T(8,128)}, f32[4,32,1024]{2,1,0:T(8,128)}, u32[]{:S(2)}, u32[]{:S(2)}) collective-permute-start(f32[4,32,1024]{2,1,0:T(8,128)} %get-tuple-element.61), channel_id=1, source_target_pairs={{0,4},{2,6},{4,0},{6,2},{8,12},{10,14},{12,8},{14,10},{1,5},{3,7},... | collective-permute-start | bytes 1572872 | tf_op jit(solution)/shard_map/ppermute | solution.py:482
  93.4 1.5 collective-permute-start.13
  94.9 6.5 %mixed.1 = f32[2,1024,128]{2,1,0:T(8,128)} custom-call(s32[3]{0:T(128)S(1)} %pad_add_fusion.ids_ref, f32[8,2,128,128]{3,2,1,0:T(8,128)S(1)} %all-to-all-done.2.va_ref.v_ref, f32[2,1024,128]{2,1,0:T(8,128)} %bitcast.28, f32[4,32,1024]{2,1,0:T(8,128)} %copy-done.10, f32[4,32,1024]{2,1,0:T(8,128)} %copy-done.12, f32[4,32,1024]{2,1,0:T(8,128)} %copy-done.11, ...), custom_call_target="tpu_custom_call" | custom-call | flops 1610612736 | bytes 7340032 | tf_op jit(solution)/shard_map/mixed/pallas_call | solution.py:351
  101.3 7.2 %all-to-all-done.1 = f32[8,2,128,128]{3,2,1,0:T(8,128)S(1)} async-done(((f32[8,2,128,128]{3,2,1,0:T(8,128)}), f32[8,2,128,128]{3,2,1,0:T(8,128)S(1)}, u32[]{:S(2)}, u32[]{:S(2)}) %all-to-all-start.1) | async-done | bytes 1048608 | tf_op jit(solution)/shard_map/all_to_all | solution.py:485
  108.5 0.9 copy-done.9
  109.4 1.8 %mix_second.1 = (f32[2,136,128]{2,1,0:T(8,128)S(1)}, f32[2,136,128]{2,1,0:T(8,128)S(1)}, f32[2,136,128]{2,1,0:T(8,128)S(1)}, f32[2,136,128]{2,1,0:T(8,128)S(1)},...) custom-call(s32[3]{0:T(128)S(1)} %pad_add_fusion.ids_ref, ...), custom_call_target="tpu_custom_call" | custom-call | flops 805306368 | bytes 3145728 | tf_op jit(solution)/shard_map/mix_second/pallas_call | solution.py:202
  111.2 2.3 %collective-permute-done.14.gb_ref = f32[4,32,1024]{2,1,0:T(8,128)} collective-permute-done((f32[4,32,1024]{2,1,0:T(8,128)}, f32[4,32,1024]{2,1,0:T(8,128)}, u32[]{:S(2)}, u32[]{:S(2)}) %collective-permute-start.14) | collective-permute-done | bytes 524320 | tf_op jit(solution)/shard_map/ppermute | solution.py:482
  113.5 1.3 sums.1
  114.8 0.5 collective-permute-start.15
  115.3 1.3 collective-permute-start.16
  116.6 2.3 %collective-permute-start.20 = (f32[2,136,128]{2,1,0:T(8,128)S(1)}, f32[2,136,128]{2,1,0:T(8,128)S(1)}, u32[]{:S(2)}, u32[]{:S(2)}) collective-permute-start(f32[2,136,128]{2,1,0:T(8,128)S(1)} %get-tuple-element.72), channel_id=1, source_target_pairs={{0,8},{2,10},{4,12},{6,14},{8,0},{10,2},{12,4},{14,6},{1,9},{3,11}... | collective-permute-start | bytes 417800 | tf_op jit(solution)/shard_map/ppermute | solution.py:482
  118.9 0.8 collective-permute-start.21
  119.7 3.1 %collective-permute-start.22 = (f32[2,136,128]{2,1,0:T(8,128)S(1)}, f32[2,136,128]{2,1,0:T(8,128)S(1)}, u32[]{:S(2)}, u32[]{:S(2)}) collective-permute-start(f32[2,136,128]{2,1,0:T(8,128)S(1)} %get-tuple-element.74), channel_id=1, source_target_pairs={{0,12},{2,14},{4,8},{6,10},{8,4},{10,6},{12,0},{14,2},{1,13},{3,15... | collective-permute-start | bytes 417800 | tf_op jit(solution)/shard_map/ppermute | solution.py:482
  122.8 4.5 %collective-permute-done.15 = f32[2,32,1024]{2,1,0:T(8,128)S(1)} collective-permute-done((f32[2,32,1024]{2,1,0:T(8,128)S(1)}, f32[2,32,1024]{2,1,0:T(8,128)S(1)}, u32[]{:S(2)}, u32[]{:S(2)}) %collective-permute-start.15) | collective-permute-done | bytes 262176 | tf_op jit(solution)/shard_map/ppermute | solution.py:482
  127.3 1.0 collective-permute-start.23
  128.4 0.8 collective-permute-start.17
  129.1 6.0 %collective-permute-done.20.refs_4_ = f32[2,136,128]{2,1,0:T(8,128)S(1)} collective-permute-done((f32[2,136,128]{2,1,0:T(8,128)S(1)}, f32[2,136,128]{2,1,0:T(8,128)S(1)}, u32[]{:S(2)}, u32[]{:S(2)}) %collective-permute-start.20) | collective-permute-done | bytes 139296 | tf_op jit(solution)/shard_map/ppermute | solution.py:482
  135.2 1.1 collective-permute-start.18
  136.3 2.7 %collective-permute-done.21.refs_5_ = f32[2,136,128]{2,1,0:T(8,128)S(1)} collective-permute-done((f32[2,136,128]{2,1,0:T(8,128)S(1)}, f32[2,136,128]{2,1,0:T(8,128)S(1)}, u32[]{:S(2)}, u32[]{:S(2)}) %collective-permute-start.21) | collective-permute-done | bytes 139296 | tf_op jit(solution)/shard_map/ppermute | solution.py:482
  139.0 0.1 collective-permute-start.19
  139.2 6.8 %collective-permute-start.24 = (f32[1,64,1024]{2,1,0:T(8,128)S(1)}, f32[1,64,1024]{2,1,0:T(8,128)S(1)}, u32[]{:S(2)}, u32[]{:S(2)}) collective-permute-start(f32[1,64,1024]{2,1,0:T(8,128)S(1)} %pad_maximum_fusion), channel_id=1, source_target_pairs={{0,8},{2,10},{4,12},{6,14},{8,0},{10,2},{12,4},{14,6},{1,9},{3,11}... | collective-permute-start | bytes 786440 | tf_op jit(solution)/shard_map/ppermute | solution.py:482
  146.1 1.6 %finish.1 = (f32[2,1024,128]{2,1,0:T(8,128)}, f32[2,8,128]{2,1,0:T(8,128)S(1)}) custom-call(s32[3]{0:T(128)S(1)} %pad_add_fusion.ids_ref, f32[2,136,128]{2,1,0:T(8,128)S(1)} %get-tuple-element.58.refs_0_, f32[2,136,128]{2,1,0:T(8,128)S(1)} %collective-permute-done.17.refs_1_, f32[2,136,128]{2,1,0:T(8,128)S(1)} %collective-permute-done.18.refs_2_, ...), custom_call_target="tpu_custom_call" | custom-call | bytes 2228224 | tf_op jit(solution)/shard_map/finish/pallas_call | solution.py:235
  147.7 0.1 collective-permute-start.25
  147.7 1.2 collective-permute-done.25
  148.9 0.6 fusion.4
  149.5 4.9 %collective-permute-done.24 = f32[1,64,1024]{2,1,0:T(8,128)S(1)} collective-permute-done((f32[1,64,1024]{2,1,0:T(8,128)S(1)}, f32[1,64,1024]{2,1,0:T(8,128)S(1)}, u32[]{:S(2)}, u32[]{:S(2)}) %collective-permute-start.24) | collective-permute-done | bytes 262176 | tf_op jit(solution)/shard_map/ppermute | solution.py:482
  154.4 0.7 fusion.3
  (56 shorter events, 0.3 us)
Async XLA Ops:
  0.6 1.0 copy-start
  0.6 11.0 %collective-permute-start = (f32[2048,128]{1,0:T(8,128)}, f32[2048,128]{1,0:T(8,128)S(1)}, u32[]{:S(2)}, u32[]{:S(2)}) collective-permute-start(f32[2048,128]{1,0:T(8,128)} %own_ref.1), channel_id=1, source_target_pairs={{0,1},{1,0},{2,3},{3,2},{4,5},{5,4},{6,7},{7,6},{8,9},{9,8},{10,11... | collective-permute-start | bytes 3145736 | tf_op jit(solution)/shard_map/ppermute | solution.py:476
  1.6 16.2 %collective-permute-start.3 = (f32[1,32,1024]{2,1,0:T(8,128)S(1)}, f32[1,32,1024]{2,1,0:T(8,128)S(1)}, u32[]{:S(2)}, u32[]{:S(2)}) collective-permute-start(f32[1,32,1024]{2,1,0:T(8,128)S(1)} %dynamic-slice_bitcast_fusion), channel_id=1, source_target_pairs={{0,12},{2,14},{4,8},{6,10},{8,4},{10,6},{12,0},{14,2},{1,13},{3,15... | collective-permute-start | bytes 393224 | tf_op jit(solution)/shard_map/ppermute | solution.py:482
  6.7 11.1 %collective-permute-start.2 = (f32[1,32,1024]{2,1,0:T(8,128)S(1)}, f32[1,32,1024]{2,1,0:T(8,128)S(1)}, u32[]{:S(2)}, u32[]{:S(2)}) collective-permute-start(f32[1,32,1024]{2,1,0:T(8,128)S(1)} %dynamic-slice_bitcast_fusion), channel_id=1, source_target_pairs={{0,8},{2,10},{4,12},{6,14},{8,0},{10,2},{12,4},{14,6},{1,9},{3,11}... | collective-permute-start | bytes 393224 | tf_op jit(solution)/shard_map/ppermute | solution.py:482
  6.7 9.6 %collective-permute-start.1 = (f32[1,32,1024]{2,1,0:T(8,128)S(1)}, f32[1,32,1024]{2,1,0:T(8,128)S(1)}, u32[]{:S(2)}, u32[]{:S(2)}) collective-permute-start(f32[1,32,1024]{2,1,0:T(8,128)S(1)} %dynamic-slice_bitcast_fusion), channel_id=1, source_target_pairs={{0,4},{2,6},{4,0},{6,2},{8,12},{10,14},{12,8},{14,10},{1,5},{3,7},... | collective-permute-start | bytes 393224 | tf_op jit(solution)/shard_map/ppermute | solution.py:482
  7.4 2.4 %copy-start.7 = (f32[16,16]{1,0:T(8,128)S(1)}, f32[16,16]{1,0:T(8,128)}, u32[]{:S(2)}) copy-start(f32[16,16]{1,0:T(8,128)} %w_ref.1) | copy-start | bytes 3076
  7.4 4.2 %copy-start.18 = (f32[256,256]{1,0:T(8,128)S(1)}, f32[256,256]{1,0:T(8,128)}, u32[]{:S(2)}) copy-start(f32[256,256]{1,0:T(8,128)} %param.11) | copy-start | bytes 786436
  17.8 36.7 %copy-start.10 = (f32[4,32,1024]{2,1,0:T(8,128)}, f32[4,32,1024]{2,1,0:T(8,128)S(1)}, u32[]{:S(2)}) copy-start(f32[4,32,1024]{2,1,0:T(8,128)S(1)} %constant_dynamic-update-slice_fusion.refs_0_) | copy-start | bytes 1572868
  17.8 30.0 %copy-start.5 = (bf16[256,256]{1,0:T(8,128)(2,1)S(1)}, bf16[256,256]{1,0:T(8,128)(2,1)}, u32[]{:S(2)}) copy-start(bf16[256,256]{1,0:T(8,128)(2,1)} %get-tuple-element.45.kh) | copy-start | bytes 393220
  17.9 30.0 %copy-start.6 = (bf16[256,256]{1,0:T(8,128)(2,1)S(1)}, bf16[256,256]{1,0:T(8,128)(2,1)}, u32[]{:S(2)}) copy-start(bf16[256,256]{1,0:T(8,128)(2,1)} %get-tuple-element.47.kl) | copy-start | bytes 393220
  17.9 30.0 %all-to-all-start = ((f32[8,2,128,128]{3,2,1,0:T(8,128)}), f32[8,2,128,128]{3,2,1,0:T(8,128)S(1)}, u32[]{:S(2)}, u32[]{:S(2)}) async-start(f32[8,2,128,128]{3,2,1,0:T(8,128)} %bitcast.21), calls=%async_computation | async-start | bytes 2097152 | tf_op jit(solution)/shard_map/all_to_all | solution.py:485
  22.7 12.5 %collective-permute-start.5 = (f32[4,32,1024]{2,1,0:T(8,128)S(1)}, f32[4,32,1024]{2,1,0:T(8,128)S(1)}, u32[]{:S(2)}, u32[]{:S(2)}) collective-permute-start(f32[4,32,1024]{2,1,0:T(8,128)S(1)} %constant_dynamic-update-slice_fusion.refs_0_), channel_id=1, source_target_pairs={{0,16},{16,0},{1,17},{17,1},{2,18},{18,2},{3,19},{19,3},{4,20},{20... | collective-permute-start | bytes 1572872 | tf_op jit(solution)/shard_map/ppermute | solution.py:479
  24.2 22.5 %collective-permute-start.4 = (f32[4,32,1024]{2,1,0:T(8,128)S(1)}, f32[4,32,1024]{2,1,0:T(8,128)S(1)}, u32[]{:S(2)}, u32[]{:S(2)}) collective-permute-start(f32[4,32,1024]{2,1,0:T(8,128)S(1)} %constant_dynamic-update-slice_fusion.refs_0_), channel_id=1, source_target_pairs={{0,2},{2,0},{4,6},{6,4},{8,10},{10,8},{12,14},{14,12},{1,3},{3,1},... | collective-permute-start | bytes 1572872 | tf_op jit(solution)/shard_map/ppermute | solution.py:482
  26.2 20.4 %collective-permute-start.10 = (f32[2,8,64,128]{3,2,1,0:T(8,128)}, f32[2,8,64,128]{3,2,1,0:T(8,128)}, u32[]{:S(2)}, u32[]{:S(2)}) collective-permute-start(f32[2,8,64,128]{3,2,1,0:T(8,128)} %get-tuple-element.49), channel_id=1, source_target_pairs={{0,1},{1,0},{2,3},{3,2},{4,5},{5,4},{6,7},{7,6},{8,9},{9,8},{10,11... | collective-permute-start | bytes 1572872 | tf_op jit(solution)/shard_map/ppermute | solution.py:476
  35.2 19.3 %copy-start.11 = (f32[4,32,1024]{2,1,0:T(8,128)}, f32[4,32,1024]{2,1,0:T(8,128)S(1)}, u32[]{:S(2)}) copy-start(f32[4,32,1024]{2,1,0:T(8,128)S(1)} %collective-permute-done.5.refs_2_) | copy-start | bytes 1572868
  46.7 2.7 %copy-start.12 = (f32[4,32,1024]{2,1,0:T(8,128)}, f32[4,32,1024]{2,1,0:T(8,128)S(1)}, u32[]{:S(2)}) copy-start(f32[4,32,1024]{2,1,0:T(8,128)S(1)} %collective-permute-done.4.refs_1_) | copy-start | bytes 1572868
  49.4 29.4 %all-to-all-start.2 = ((f32[8,2,128,128]{3,2,1,0:T(8,128)}), f32[8,2,128,128]{3,2,1,0:T(8,128)S(1)}, u32[]{:S(2)}, u32[]{:S(2)}) async-start(f32[8,2,128,128]{3,2,1,0:T(8,128)} %bitcast.9), calls=%async_computation.2 | async-start | bytes 2097152 | tf_op jit(solution)/shard_map/all_to_all | solution.py:485
  53.0 13.6 %collective-permute-start.6 = (f32[4,32,1024]{2,1,0:T(8,128)}, f32[4,32,1024]{2,1,0:T(8,128)S(1)}, u32[]{:S(2)}, u32[]{:S(2)}) collective-permute-start(f32[4,32,1024]{2,1,0:T(8,128)} %copy-done.12), channel_id=1, source_target_pairs={{0,16},{16,0},{1,17},{17,1},{2,18},{18,2},{3,19},{19,3},{4,20},{20... | collective-permute-start | bytes 1572872 | tf_op jit(solution)/shard_map/ppermute | solution.py:479
  54.5 12.1 %collective-permute-start.7 = (f32[4,32,1024]{2,1,0:T(8,128)S(1)}, f32[4,32,1024]{2,1,0:T(8,128)S(1)}, u32[]{:S(2)}, u32[]{:S(2)}) collective-permute-start(f32[4,32,1024]{2,1,0:T(8,128)S(1)} %constant_dynamic-update-slice_fusion.refs_0_), channel_id=1, source_target_pairs={{0,1},{1,0},{2,3},{3,2},{4,5},{5,4},{6,7},{7,6},{8,9},{9,8},{10,11... | collective-permute-start | bytes 1572872 | tf_op jit(solution)/shard_map/ppermute | solution.py:476
  54.6 12.1 %collective-permute-start.9 = (f32[4,32,1024]{2,1,0:T(8,128)S(1)}, f32[4,32,1024]{2,1,0:T(8,128)S(1)}, u32[]{:S(2)}, u32[]{:S(2)}) collective-permute-start(f32[4,32,1024]{2,1,0:T(8,128)S(1)} %collective-permute-done.5.refs_2_), channel_id=1, source_target_pairs={{0,1},{1,0},{2,3},{3,2},{4,5},{5,4},{6,7},{7,6},{8,9},{9,8},{10,11... | collective-permute-start | bytes 1572872 | tf_op jit(solution)/shard_map/ppermute | solution.py:476
  55.1 11.6 %collective-permute-start.8 = (f32[4,32,1024]{2,1,0:T(8,128)}, f32[4,32,1024]{2,1,0:T(8,128)S(1)}, u32[]{:S(2)}, u32[]{:S(2)}) collective-permute-start(f32[4,32,1024]{2,1,0:T(8,128)} %copy-done.12), channel_id=1, source_target_pairs={{0,1},{1,0},{2,3},{3,2},{4,5},{5,4},{6,7},{7,6},{8,9},{9,8},{10,11... | collective-permute-start | bytes 1572872 | tf_op jit(solution)/shard_map/ppermute | solution.py:476
  66.6 1.9 %copy-start.13 = (f32[4,32,1024]{2,1,0:T(8,128)}, f32[4,32,1024]{2,1,0:T(8,128)S(1)}, u32[]{:S(2)}) copy-start(f32[4,32,1024]{2,1,0:T(8,128)S(1)} %collective-permute-done.6.refs_3_) | copy-start | bytes 1572868
  66.6 1.9 %collective-permute-start.11 = (f32[4,32,1024]{2,1,0:T(8,128)S(1)}, f32[4,32,1024]{2,1,0:T(8,128)S(1)}, u32[]{:S(2)}, u32[]{:S(2)}) collective-permute-start(f32[4,32,1024]{2,1,0:T(8,128)S(1)} %collective-permute-done.6.refs_3_), channel_id=1, source_target_pairs={{0,1},{1,0},{2,3},{3,2},{4,5},{5,4},{6,7},{7,6},{8,9},{9,8},{10,11... | collective-permute-start | bytes 1572872 | tf_op jit(solution)/shard_map/ppermute | solution.py:476
  66.6 1.9 %copy-start.14 = (f32[4,32,1024]{2,1,0:T(8,128)}, f32[4,32,1024]{2,1,0:T(8,128)S(1)}, u32[]{:S(2)}) copy-start(f32[4,32,1024]{2,1,0:T(8,128)S(1)} %collective-permute-done.7.refs_4_) | copy-start | bytes 1572868
  66.7 1.9 %copy-start.15 = (f32[4,32,1024]{2,1,0:T(8,128)}, f32[4,32,1024]{2,1,0:T(8,128)S(1)}, u32[]{:S(2)}) copy-start(f32[4,32,1024]{2,1,0:T(8,128)S(1)} %collective-permute-done.9.refs_6_) | copy-start | bytes 1572868
  66.7 1.9 %copy-start.16 = (f32[4,32,1024]{2,1,0:T(8,128)}, f32[4,32,1024]{2,1,0:T(8,128)S(1)}, u32[]{:S(2)}) copy-start(f32[4,32,1024]{2,1,0:T(8,128)S(1)} %collective-permute-done.8.refs_5_) | copy-start | bytes 1572868
  68.5 0.8 copy-start.17
  78.8 29.7 %all-to-all-start.1 = ((f32[8,2,128,128]{3,2,1,0:T(8,128)}), f32[8,2,128,128]{3,2,1,0:T(8,128)S(1)}, u32[]{:S(2)}, u32[]{:S(2)}) async-start(f32[8,2,128,128]{3,2,1,0:T(8,128)} %up.1), calls=%async_computation.1 | async-start | bytes 2097152 | tf_op jit(solution)/shard_map/all_to_all | solution.py:485
  82.4 2.7 %collective-permute-start.12 = (f32[8,2,128,128]{3,2,1,0:T(8,128)S(1)}, f32[8,2,128,128]{3,2,1,0:T(8,128)S(1)}, u32[]{:S(2)}, u32[]{:S(2)}) collective-permute-start(f32[8,2,128,128]{3,2,1,0:T(8,128)S(1)} %all-to-all-done.2.va_ref.v_ref), channel_id=1, source_target_pairs={{0,1},{1,0},{2,3},{3,2},{4,5},{5,4},{6,7},{7,6},{8,9},{9,8},{10,11... | collective-permute-start | bytes 3145736 | tf_op jit(solution)/shard_map/ppermute | solution.py:476
  89.7 0.8 copy-start.1
  90.5 0.9 copy-start.3
  91.4 22.1 %collective-permute-start.14 = (f32[4,32,1024]{2,1,0:T(8,128)}, f32[4,32,1024]{2,1,0:T(8,128)}, u32[]{:S(2)}, u32[]{:S(2)}) collective-permute-start(f32[4,32,1024]{2,1,0:T(8,128)} %get-tuple-element.61), channel_id=1, source_target_pairs={{0,4},{2,6},{4,0},{6,2},{8,12},{10,14},{12,8},{14,10},{1,5},{3,7},... | collective-permute-start | bytes 1572872 | tf_op jit(solution)/shard_map/ppermute | solution.py:482
  93.4 20.1 %collective-permute-start.13 = (f32[4,32,1024]{2,1,0:T(8,128)}, f32[4,32,1024]{2,1,0:T(8,128)}, u32[]{:S(2)}, u32[]{:S(2)}) collective-permute-start(f32[4,32,1024]{2,1,0:T(8,128)} %get-tuple-element.54), channel_id=1, source_target_pairs={{0,2},{2,0},{4,6},{6,4},{8,10},{10,8},{12,14},{14,12},{1,3},{3,1},... | collective-permute-start | bytes 1572872 | tf_op jit(solution)/shard_map/ppermute | solution.py:482
  94.9 13.6 %copy-start.8 = (bf16[256,256]{1,0:T(8,128)(2,1)S(1)}, bf16[256,256]{1,0:T(8,128)(2,1)}, u32[]{:S(2)}) copy-start(bf16[256,256]{1,0:T(8,128)(2,1)} %get-tuple-element.42.kh) | copy-start | bytes 393220
  108.5 0.9 copy-start.9
  109.4 4.1 %copy-start.2 = (f32[4,32,1024]{2,1,0:T(8,128)S(1)}, f32[4,32,1024]{2,1,0:T(8,128)}, u32[]{:S(2)}) copy-start(f32[4,32,1024]{2,1,0:T(8,128)} %copy-done.1) | copy-start | bytes 1572868
  109.4 4.1 %copy-start.4 = (f32[4,32,1024]{2,1,0:T(8,128)S(1)}, f32[4,32,1024]{2,1,0:T(8,128)}, u32[]{:S(2)}) copy-start(f32[4,32,1024]{2,1,0:T(8,128)} %copy-done.3) | copy-start | bytes 1572868
  114.8 12.5 %collective-permute-start.15 = (f32[2,32,1024]{2,1,0:T(8,128)S(1)}, f32[2,32,1024]{2,1,0:T(8,128)S(1)}, u32[]{:S(2)}, u32[]{:S(2)}) collective-permute-start(f32[2,32,1024]{2,1,0:T(8,128)S(1)} %get-tuple-element.65), channel_id=1, source_target_pairs={{0,4},{2,6},{4,0},{6,2},{8,12},{10,14},{12,8},{14,10},{1,5},{3,7},... | collective-permute-start | bytes 786440 | tf_op jit(solution)/shard_map/ppermute | solution.py:482
  115.3 13.0 %collective-permute-start.16 = (f32[2,32,1024]{2,1,0:T(8,128)S(1)}, f32[2,32,1024]{2,1,0:T(8,128)S(1)}, u32[]{:S(2)}, u32[]{:S(2)}) collective-permute-start(f32[2,32,1024]{2,1,0:T(8,128)S(1)} %get-tuple-element.66), channel_id=1, source_target_pairs={{0,2},{2,0},{4,6},{6,4},{8,10},{10,8},{12,14},{14,12},{1,3},{3,1},... | collective-permute-start | bytes 786440 | tf_op jit(solution)/shard_map/ppermute | solution.py:482
  116.6 18.6 %collective-permute-start.20 = (f32[2,136,128]{2,1,0:T(8,128)S(1)}, f32[2,136,128]{2,1,0:T(8,128)S(1)}, u32[]{:S(2)}, u32[]{:S(2)}) collective-permute-start(f32[2,136,128]{2,1,0:T(8,128)S(1)} %get-tuple-element.72), channel_id=1, source_target_pairs={{0,8},{2,10},{4,12},{6,14},{8,0},{10,2},{12,4},{14,6},{1,9},{3,11}... | collective-permute-start | bytes 417800 | tf_op jit(solution)/shard_map/ppermute | solution.py:482
  118.9 20.1 %collective-permute-start.21 = (f32[2,136,128]{2,1,0:T(8,128)S(1)}, f32[2,136,128]{2,1,0:T(8,128)S(1)}, u32[]{:S(2)}, u32[]{:S(2)}) collective-permute-start(f32[2,136,128]{2,1,0:T(8,128)S(1)} %get-tuple-element.73), channel_id=1, source_target_pairs={{0,10},{2,8},{4,14},{6,12},{8,2},{10,0},{12,6},{14,4},{1,11},{3,9}... | collective-permute-start | bytes 417800 | tf_op jit(solution)/shard_map/ppermute | solution.py:482
  119.7 19.5 %collective-permute-start.22 = (f32[2,136,128]{2,1,0:T(8,128)S(1)}, f32[2,136,128]{2,1,0:T(8,128)S(1)}, u32[]{:S(2)}, u32[]{:S(2)}) collective-permute-start(f32[2,136,128]{2,1,0:T(8,128)S(1)} %get-tuple-element.74), channel_id=1, source_target_pairs={{0,12},{2,14},{4,8},{6,10},{8,4},{10,6},{12,0},{14,2},{1,13},{3,15... | collective-permute-start | bytes 417800 | tf_op jit(solution)/shard_map/ppermute | solution.py:482
  127.3 18.7 %collective-permute-start.23 = (f32[2,136,128]{2,1,0:T(8,128)S(1)}, f32[2,136,128]{2,1,0:T(8,128)S(1)}, u32[]{:S(2)}, u32[]{:S(2)}) collective-permute-start(f32[2,136,128]{2,1,0:T(8,128)S(1)} %get-tuple-element.75), channel_id=1, source_target_pairs={{0,14},{2,12},{4,10},{6,8},{8,6},{10,4},{12,2},{14,0},{1,15},{3,13... | collective-permute-start | bytes 417800 | tf_op jit(solution)/shard_map/ppermute | solution.py:482
  128.4 17.7 %collective-permute-start.17 = (f32[2,136,128]{2,1,0:T(8,128)S(1)}, f32[2,136,128]{2,1,0:T(8,128)S(1)}, u32[]{:S(2)}, u32[]{:S(2)}) collective-permute-start(f32[2,136,128]{2,1,0:T(8,128)S(1)} %get-tuple-element.67), channel_id=1, source_target_pairs={{0,2},{2,0},{4,6},{6,4},{8,10},{10,8},{12,14},{14,12},{1,3},{3,1},... | collective-permute-start | bytes 417800 | tf_op jit(solution)/shard_map/ppermute | solution.py:482
  135.2 10.9 %collective-permute-start.18 = (f32[2,136,128]{2,1,0:T(8,128)S(1)}, f32[2,136,128]{2,1,0:T(8,128)S(1)}, u32[]{:S(2)}, u32[]{:S(2)}) collective-permute-start(f32[2,136,128]{2,1,0:T(8,128)S(1)} %get-tuple-element.69), channel_id=1, source_target_pairs={{0,4},{2,6},{4,0},{6,2},{8,12},{10,14},{12,8},{14,10},{1,5},{3,7},... | collective-permute-start | bytes 417800 | tf_op jit(solution)/shard_map/ppermute | solution.py:482
  139.0 7.0 %collective-permute-start.19 = (f32[2,136,128]{2,1,0:T(8,128)S(1)}, f32[2,136,128]{2,1,0:T(8,128)S(1)}, u32[]{:S(2)}, u32[]{:S(2)}) collective-permute-start(f32[2,136,128]{2,1,0:T(8,128)S(1)} %get-tuple-element.71), channel_id=1, source_target_pairs={{0,6},{2,4},{4,2},{6,0},{8,14},{10,12},{12,10},{14,8},{1,7},{3,5},... | collective-permute-start | bytes 417800 | tf_op jit(solution)/shard_map/ppermute | solution.py:482
  139.2 15.2 %collective-permute-start.24 = (f32[1,64,1024]{2,1,0:T(8,128)S(1)}, f32[1,64,1024]{2,1,0:T(8,128)S(1)}, u32[]{:S(2)}, u32[]{:S(2)}) collective-permute-start(f32[1,64,1024]{2,1,0:T(8,128)S(1)} %pad_maximum_fusion), channel_id=1, source_target_pairs={{0,8},{2,10},{4,12},{6,14},{8,0},{10,2},{12,4},{14,6},{1,9},{3,11}... | collective-permute-start | bytes 786440 | tf_op jit(solution)/shard_map/ppermute | solution.py:482
  147.7 1.2 collective-permute-start.25

commit v5 on v4

--- a/solution.py
+++ b/solution.py
@@ -211,7 +211,8 @@
     )(ids, *k, u, b)
 
 
-def finish_kernel(width, ids_ref, *refs):
+def finish_kernel(width, ids_ref, ahead_ref, *refs):
+    del ahead_ref
     pieces, (o_ref, s_ref, sem) = refs[:-3], refs[-3:]
     copies = []
     for d, piece in enumerate(pieces):
@@ -229,12 +230,12 @@
         c.wait()
 
 
-def finish_call(ids, pieces, width):
+def finish_call(ids, pieces, width, ahead):
     own, tall, chan = pieces[0].shape
     count = len(pieces)
     return pl.pallas_call(
         functools.partial(finish_kernel, width),
-        in_specs=[SMEM_SPEC] + [VMEM_SPEC] * count,
+        in_specs=[SMEM_SPEC, pl.BlockSpec(memory_space=pl.ANY)] + [VMEM_SPEC] * count,
         out_specs=[pl.BlockSpec(memory_space=pltpu.HBM), VMEM_SPEC],
         out_shape=[
             pltpu.HBM((own, count * width, chan), F32),
@@ -244,7 +245,7 @@
         compiler_params=params(),
         cost_estimate=cost(0, 8 * own * tall * count * chan),
         name="finish",
-    )(ids, *pieces)
+    )(ids, ahead, *pieces)
 
 
 def place_copies(offsets, ids_ref, pieces, whole, sem):
@@ -550,22 +551,25 @@
         seq_count,
         1.0 / math.sqrt(rows * 2 * chan),
     )
+    mid = seq_count // 2
+    back = {0: in_pieces[0]}
+    for d in range(mid, seq_count):
+        back[d] = swap_seq(in_pieces[d], d)
     got_a, got_b = all_after([got_a, got_b], in_pieces[0])
     keep_a, send_a, keep_b, send_b = sums_call(keep_a, got_a, keep_b, got_b)
     got_a, got_b = swap_seq(send_a, 2), swap_seq(send_b, 1)
-
-    back = {0: in_pieces[0]}
-    for d in reversed(range(1, seq_count)):
-        piece = in_pieces[d] if 2 * d >= seq_count else after(in_pieces[d], got_a, got_b)
-        back[d] = swap_seq(piece, d)
-
+    for d in reversed(range(1, mid)):
+        back[d] = swap_seq(after(in_pieces[d], back[mid]), d)
+
+    got_a, got_b = all_after([got_a, got_b], *[back[d] for d in range(mid, seq_count)])
     keep = jnp.concatenate([keep_a + got_a, keep_b + got_b], axis=1)
+    summed = keep
     for b in range(2, bits):
         part = keep.shape[0] // 2
         keep = keep[:part] + swap_seq(keep[part:], 1 << b)
     first_grad = keep.reshape(unit, columns) * (1.0 / math.sqrt(total * 2 * chan))
 
-    input_grad, second = finish_call(ids, [back[d] for d in range(seq_count)], width)
+    input_grad, second = finish_call(ids, [back[d] for d in range(seq_count)], width, summed)
     input_grad = input_grad.reshape(inputs.shape)
     second = second[:, :, :total].reshape(total, total)
     second = second + swap_core(second)

time: 156 us -> 153 us (0.981)
  starting transfers between devices: 45.4 us -> 43.7 us
    ppermute x16, starting transfers between devices: 29.1 us -> 27.4 us  [swap_seq(): return lax.ppermute(x, 'seq', [(i, i ^ bit) for i in range(seq_count)])]
  transfers between devices with their start and end apart: 29 -> 29, of which waited for: 15 -> 15; matrix products, arithmetic and copies ran while one was open for 2% -> 2% of each run, Pallas kernels for 18% -> 19%
where the time goes in v5:
time: 153 us
  waiting for transfers between devices  69.9 us (46%)
  starting transfers between devices  43.7 us (29%)
  Pallas kernels  30.1 us (20%)
  local copies, waits for them, and re-layouts  6.36 us (4%)
  other arithmetic  1.56 us (1%)
    ppermute x16, waiting for transfers between devices, swap_seq(): return lax.ppermute(x, 'seq', [(i, i ^ bit) for i in range(seq_count)])  32.4 us
    ppermute x16, starting transfers between devices, swap_seq(): return lax.ppermute(x, 'seq', [(i, i ^ bit) for i in range(seq_count)])  27.4 us
    ppermute x2, waiting for transfers between devices, swap_rep(): return lax.ppermute(x, 'rep', [(i, i ^ 1) for i in range(rep_count)])  20.5 us
    all_to_all x3, starting transfers between devices, exchange(): return lax.all_to_all(x, 'seq', split_axis=0, concat_axis=0, tiled=True)  12.1 us
    all_to_all x3, waiting for transfers between devices, exchange(): return lax.all_to_all(x, 'seq', split_axis=0, concat_axis=0, tiled=True)  11.3 us
    pallas_call x1, Pallas kernels, mixed_call(): pl.pallas_call(functools.partial(mixed_kernel, offsets), in_specs=[pl.Blo...  6.46 us
    pallas_call x1, Pallas kernels, up_call(): pl.pallas_call(functools.partial(up_kernel, offsets), in_specs=[pl.BlockS...  6.43 us
    ppermute x8, waiting for transfers between devices, swap_core(): return lax.ppermute(x, 'chan', [(0, 1), (1, 0)])  5.67 us
  transfers between devices with their start and end apart: 29, of which 15 were waited for; matrix products, arithmetic and copies ran while one was open for 2% of the time, Pallas kernels for 19%

profile of v5, /device:TPU:0, one launch (start us, length us, event | category | flops | bytes accessed | tf_op | source)
XLA Modules:
  0.0 152.6 jit_solution(10390338709764478241)
XLA Ops:
  0.6 0.0 copy-start
  0.6 0.5 collective-permute-start
  1.2 0.4 copy-done
  1.6 5.1 %collective-permute-start.4 = (f32[1,32,1024]{2,1,0:T(8,128)S(1)}, f32[1,32,1024]{2,1,0:T(8,128)S(1)}, u32[]{:S(2)}, u32[]{:S(2)}) collective-permute-start(f32[1,32,1024]{2,1,0:T(8,128)S(1)} %dynamic-slice_bitcast_fusion), channel_id=1, source_target_pairs={{0,12},{2,14},{4,8},{6,10},{8,4},{10,6},{12,0},{14,2},{1,13},{3,15... | collective-permute-start | bytes 393224 | tf_op jit(solution)/shard_map/ppermute | solution.py:483
  6.7 0.6 collective-permute-start.2
  7.4 2.4 %copy.12 = f32[2,8,128,128]{3,2,0,1:T(8,128)} copy(f32[2,8,128,128]{3,2,1,0:T(8,128)} %bitcast.26) | data formatting | bytes 2097152 | tf_op jit(solution)/shard_map/reshape | solution.py:513
  9.7 1.7 %spread.1 = (bf16[256,256]{1,0:T(8,128)(2,1)}, bf16[256,256]{1,0:T(8,128)(2,1)}, bf16[256,256]{1,0:T(8,128)(2,1)}, bf16[256,256]{1,0:T(8,128)(2,1)}) custom-call(f32[16,16]{1,0:T(8,128)S(1)} %copy-done.7), custom_call_target="tpu_custom_call" | custom-call | flops 8388608 | bytes 524288 | tf_op jit(solution)/shard_map/spread/pallas_call | solution.py:126
  11.5 0.1 pad_add_fusion.ids_ref
  11.5 0.1 fusion.6
  11.7 0.0 collective-permute-done.other_ref
  11.7 4.6 %gate.1 = (f32[2048,128]{1,0:T(8,128)}, f32[2048,128]{1,0:T(8,128)}, f32[2,8,64,128]{3,2,1,0:T(8,128)}, f32[2,8,64,128]{3,2,1,0:T(8,128)}) custom-call(s32[3]{0:T(128)S(1)} %pad_add_fusion.ids_ref, f32[2048,128]{1,0:T(8,128)} %own_ref.1, f32[2048,128]{1,0:T(8,128)S(1)} %collective-permute-done.other_ref, f32[2048,128]{1,0:T(8,128)} %gate_ref.1, ...), custom_call_target="tpu_custom_call" | custom-call | flops 402653184 | bytes 6291456 | tf_op jit(solution)/shard_map/gate/pallas_call | solution.py:70
  16.3 0.0 collective-permute-done.2
  16.4 1.4 collective-permute-done.3
  17.8 0.0 copy-start.5
  17.9 4.9 %all-to-all-start = ((f32[8,2,128,128]{3,2,1,0:T(8,128)}), f32[8,2,128,128]{3,2,1,0:T(8,128)S(1)}, u32[]{:S(2)}, u32[]{:S(2)}) async-start(f32[8,2,128,128]{3,2,1,0:T(8,128)} %bitcast.21), calls=%async_computation | async-start | bytes 2097152 | tf_op jit(solution)/shard_map/all_to_all | solution.py:486
  22.7 1.5 collective-permute-start.6
  24.2 2.0 %collective-permute-start.5 = (f32[4,32,1024]{2,1,0:T(8,128)S(1)}, f32[4,32,1024]{2,1,0:T(8,128)S(1)}, u32[]{:S(2)}, u32[]{:S(2)}) collective-permute-start(f32[4,32,1024]{2,1,0:T(8,128)S(1)} %constant_dynamic-update-slice_fusion.refs_0_), channel_id=1, source_target_pairs={{0,2},{2,0},{4,6},{6,4},{8,10},{10,8},{12,14},{14,12},{1,3},{3,1},... | collective-permute-start | bytes 1572872 | tf_op jit(solution)/shard_map/ppermute | solution.py:483
  26.2 9.0 %collective-permute-done.6.refs_2_ = f32[4,32,1024]{2,1,0:T(8,128)S(1)} collective-permute-done((f32[4,32,1024]{2,1,0:T(8,128)S(1)}, f32[4,32,1024]{2,1,0:T(8,128)S(1)}, u32[]{:S(2)}, u32[]{:S(2)}) %collective-permute-start.6) | collective-permute-done | bytes 524320 | tf_op jit(solution)/shard_map/ppermute | solution.py:480
  35.2 11.4 %collective-permute-done.5.refs_1_ = f32[4,32,1024]{2,1,0:T(8,128)S(1)} collective-permute-done((f32[4,32,1024]{2,1,0:T(8,128)S(1)}, f32[4,32,1024]{2,1,0:T(8,128)S(1)}, u32[]{:S(2)}, u32[]{:S(2)}) %collective-permute-start.5) | collective-permute-done | bytes 524320 | tf_op jit(solution)/shard_map/ppermute | solution.py:483
  46.7 0.0 collective-permute-done.1.gb_hbm
  46.7 1.2 all-to-all-done
  47.8 1.6 %mix.1 = f32[16,128,128]{2,1,0:T(8,128)} custom-call(bf16[256,256]{1,0:T(8,128)(2,1)S(1)} %copy-done.5, bf16[256,256]{1,0:T(8,128)(2,1)S(1)} %copy-done.6, f32[16,128,128]{2,1,0:T(8,128)S(1)} %bitcast.22), custom_call_target="tpu_custom_call" | custom-call | flops 402653184 | bytes 2097152 | tf_op jit(solution)/shard_map/mix/pallas_call | solution.py:184
  49.4 3.6 %all-to-all-start.1 = ((f32[8,2,128,128]{3,2,1,0:T(8,128)}), f32[8,2,128,128]{3,2,1,0:T(8,128)S(1)}, u32[]{:S(2)}, u32[]{:S(2)}) async-start(f32[8,2,128,128]{3,2,1,0:T(8,128)} %bitcast.7), calls=%async_computation.1 | async-start | bytes 2097152 | tf_op jit(solution)/shard_map/all_to_all | solution.py:486
  53.0 1.6 %collective-permute-start.7 = (f32[4,32,1024]{2,1,0:T(8,128)}, f32[4,32,1024]{2,1,0:T(8,128)S(1)}, u32[]{:S(2)}, u32[]{:S(2)}) collective-permute-start(f32[4,32,1024]{2,1,0:T(8,128)} %copy-done.12), channel_id=1, source_target_pairs={{0,16},{16,0},{1,17},{17,1},{2,18},{18,2},{3,19},{19,3},{4,20},{20... | collective-permute-start | bytes 1572872 | tf_op jit(solution)/shard_map/ppermute | solution.py:480
  54.6 0.5 collective-permute-start.10
  55.1 0.1 collective-permute-start.9
  55.1 11.5 %collective-permute-done.7.refs_3_ = f32[4,32,1024]{2,1,0:T(8,128)S(1)} collective-permute-done((f32[4,32,1024]{2,1,0:T(8,128)}, f32[4,32,1024]{2,1,0:T(8,128)S(1)}, u32[]{:S(2)}, u32[]{:S(2)}) %collective-permute-start.7) | collective-permute-done | bytes 524320 | tf_op jit(solution)/shard_map/ppermute | solution.py:480
  66.7 1.9 %collective-permute-done.11.refs_7_ = f32[4,32,1024]{2,1,0:T(8,128)S(1)} collective-permute-done((f32[4,32,1024]{2,1,0:T(8,128)S(1)}, f32[4,32,1024]{2,1,0:T(8,128)S(1)}, u32[]{:S(2)}, u32[]{:S(2)}) %collective-permute-start.11) | collective-permute-done | bytes 524320 | tf_op jit(solution)/shard_map/ppermute | solution.py:477
  68.6 0.8 copy-done.17
  69.3 6.4 %up.1 = f32[8,2,128,128]{3,2,1,0:T(8,128)} custom-call(s32[3]{0:T(128)S(1)} %pad_add_fusion.ids_ref, f32[2,1024,128]{2,1,0:T(8,128)} %bitcast.25, f32[4,32,1024]{2,1,0:T(8,128)} %copy-done.10, f32[4,32,1024]{2,1,0:T(8,128)} %copy-done.12, f32[4,32,1024]{2,1,0:T(8,128)} %copy-done.11, f32[4,32,1024]{2,1,0:T(8,128)} %copy-done.13, f32[4,32,1024]{2,1,0:T(8,128)} %copy-done.14, ...), custom_call_target="tpu_custom_call" | custom-call | flops 1610612736 | bytes 6291456 | tf_op jit(solution)/shard_map/up/pallas_call | solution.py:296
  75.8 3.0 %all-to-all-done.1.va_ref.v_ref = f32[8,2,128,128]{3,2,1,0:T(8,128)S(1)} async-done(((f32[8,2,128,128]{3,2,1,0:T(8,128)}), f32[8,2,128,128]{3,2,1,0:T(8,128)S(1)}, u32[]{:S(2)}, u32[]{:S(2)}) %all-to-all-start.1) | async-done | bytes 1048608 | tf_op jit(solution)/shard_map/all_to_all | solution.py:486
  78.8 3.6 %all-to-all-start.2 = ((f32[8,2,128,128]{3,2,1,0:T(8,128)}), f32[8,2,128,128]{3,2,1,0:T(8,128)S(1)}, u32[]{:S(2)}, u32[]{:S(2)}) async-start(f32[8,2,128,128]{3,2,1,0:T(8,128)} %up.1), calls=%async_computation.2 | async-start | bytes 2097152 | tf_op jit(solution)/shard_map/all_to_all | solution.py:486
  82.4 0.0 collective-permute-start.12
  82.5 2.6 %collective-permute-done.12.vb_ref = f32[8,2,128,128]{3,2,1,0:T(8,128)S(1)} collective-permute-done((f32[8,2,128,128]{3,2,1,0:T(8,128)S(1)}, f32[8,2,128,128]{3,2,1,0:T(8,128)S(1)}, u32[]{:S(2)}, u32[]{:S(2)}) %collective-permute-start.12) | collective-permute-done | bytes 1048608 | tf_op jit(solution)/shard_map/ppermute | solution.py:477
  85.1 4.6 %first.1 = (f32[4,32,1024]{2,1,0:T(8,128)S(1)}, f32[4,32,1024]{2,1,0:T(8,128)}, f32[4,32,1024]{2,1,0:T(8,128)S(1)}, f32[4,32,1024]{2,1,0:T(8,128)}) custom-call(s32[3]{0:T(128)S(1)} %pad_add_fusion.ids_ref, f32[2,8,64,128]{3,2,1,0:T(8,128)} %get-tuple-element.44.ga_hbm, f32[2,8,64,128]{3,2,1,0:T(8,128)} %collective-permute-done.1.gb_hbm, ...), custom_call_target="tpu_custom_call" | custom-call | flops 1610612736 | bytes 6291456 | tf_op jit(solution)/shard_map/first/pallas_call | solution.py:425
  89.8 0.8 copy-done.1
  90.5 0.8 copy-done.3
  91.4 2.0 %collective-permute-start.14 = (f32[4,32,1024]{2,1,0:T(8,128)}, f32[4,32,1024]{2,1,0:T(8,128)}, u32[]{:S(2)}, u32[]{:S(2)}) collective-permute-start(f32[4,32,1024]{2,1,0:T(8,128)} %get-tuple-element.56), channel_id=1, source_target_pairs={{0,4},{2,6},{4,0},{6,2},{8,12},{10,14},{12,8},{14,10},{1,5},{3,7},... | collective-permute-start | bytes 1572872 | tf_op jit(solution)/shard_map/ppermute | solution.py:483
  93.4 1.5 collective-permute-start.13
  94.9 6.5 %mixed.1 = f32[2,1024,128]{2,1,0:T(8,128)} custom-call(s32[3]{0:T(128)S(1)} %pad_add_fusion.ids_ref, f32[8,2,128,128]{3,2,1,0:T(8,128)S(1)} %all-to-all-done.1.va_ref.v_ref, f32[2,1024,128]{2,1,0:T(8,128)} %bitcast.28, f32[4,32,1024]{2,1,0:T(8,128)} %copy-done.10, f32[4,32,1024]{2,1,0:T(8,128)} %copy-done.12, f32[4,32,1024]{2,1,0:T(8,128)} %copy-done.11, ...), custom_call_target="tpu_custom_call" | custom-call | flops 1610612736 | bytes 7340032 | tf_op jit(solution)/shard_map/mixed/pallas_call | solution.py:352
  101.3 7.2 %all-to-all-done.2 = f32[8,2,128,128]{3,2,1,0:T(8,128)S(1)} async-done(((f32[8,2,128,128]{3,2,1,0:T(8,128)}), f32[8,2,128,128]{3,2,1,0:T(8,128)S(1)}, u32[]{:S(2)}, u32[]{:S(2)}) %all-to-all-start.2) | async-done | bytes 1048608 | tf_op jit(solution)/shard_map/all_to_all | solution.py:486
  108.5 0.9 copy-done.9
  109.4 1.8 %mix_second.1 = (f32[2,136,128]{2,1,0:T(8,128)S(1)}, f32[2,136,128]{2,1,0:T(8,128)S(1)}, f32[2,136,128]{2,1,0:T(8,128)S(1)}, f32[2,136,128]{2,1,0:T(8,128)S(1)},...) custom-call(s32[3]{0:T(128)S(1)} %pad_add_fusion.ids_ref, ...), custom_call_target="tpu_custom_call" | custom-call | flops 805306368 | bytes 3145728 | tf_op jit(solution)/shard_map/mix_second/pallas_call | solution.py:202
  111.2 0.1 collective-permute-start.17
  111.3 2.2 %collective-permute-done.14.gb_ref = f32[4,32,1024]{2,1,0:T(8,128)} collective-permute-done((f32[4,32,1024]{2,1,0:T(8,128)}, f32[4,32,1024]{2,1,0:T(8,128)}, u32[]{:S(2)}, u32[]{:S(2)}) %collective-permute-start.14) | collective-permute-done | bytes 524320 | tf_op jit(solution)/shard_map/ppermute | solution.py:483
  113.5 1.3 sums.1
  114.8 1.3 collective-permute-start.15
  116.1 1.0 collective-permute-start.16
  117.2 2.6 %collective-permute-start.18 = (f32[2,136,128]{2,1,0:T(8,128)S(1)}, f32[2,136,128]{2,1,0:T(8,128)S(1)}, u32[]{:S(2)}, u32[]{:S(2)}) collective-permute-start(f32[2,136,128]{2,1,0:T(8,128)S(1)} %get-tuple-element.70), channel_id=1, source_target_pairs={{0,10},{2,8},{4,14},{6,12},{8,2},{10,0},{12,6},{14,4},{1,11},{3,9}... | collective-permute-start | bytes 417800 | tf_op jit(solution)/shard_map/ppermute | solution.py:483
  119.7 1.4 collective-permute-start.19
  121.1 3.3 %collective-permute-start.20 = (f32[2,136,128]{2,1,0:T(8,128)S(1)}, f32[2,136,128]{2,1,0:T(8,128)S(1)}, u32[]{:S(2)}, u32[]{:S(2)}) collective-permute-start(f32[2,136,128]{2,1,0:T(8,128)S(1)} %get-tuple-element.72), channel_id=1, source_target_pairs={{0,14},{2,12},{4,10},{6,8},{8,6},{10,4},{12,2},{14,0},{1,15},{3,13... | collective-permute-start | bytes 417800 | tf_op jit(solution)/shard_map/ppermute | solution.py:483
  124.5 9.3 %collective-permute-done.18.refs_5_ = f32[2,136,128]{2,1,0:T(8,128)S(1)} collective-permute-done((f32[2,136,128]{2,1,0:T(8,128)S(1)}, f32[2,136,128]{2,1,0:T(8,128)S(1)}, u32[]{:S(2)}, u32[]{:S(2)}) %collective-permute-start.18) | collective-permute-done | bytes 139296 | tf_op jit(solution)/shard_map/ppermute | solution.py:483
  133.8 0.8 collective-permute-start.21
  134.6 2.0 %collective-permute-start.22 = (f32[2,136,128]{2,1,0:T(8,128)S(1)}, f32[2,136,128]{2,1,0:T(8,128)S(1)}, u32[]{:S(2)}, u32[]{:S(2)}) collective-permute-start(f32[2,136,128]{2,1,0:T(8,128)S(1)} %get-tuple-element.79), channel_id=1, source_target_pairs={{0,4},{2,6},{4,0},{6,2},{8,12},{10,14},{12,8},{14,10},{1,5},{3,7},... | collective-permute-start | bytes 417800 | tf_op jit(solution)/shard_map/ppermute | solution.py:483
  136.6 2.5 %collective-permute-start.23 = (f32[2,136,128]{2,1,0:T(8,128)S(1)}, f32[2,136,128]{2,1,0:T(8,128)S(1)}, u32[]{:S(2)}, u32[]{:S(2)}) collective-permute-start(f32[2,136,128]{2,1,0:T(8,128)S(1)} %get-tuple-element.81), channel_id=1, source_target_pairs={{0,6},{2,4},{4,2},{6,0},{8,14},{10,12},{12,10},{14,8},{1,7},{3,5},... | collective-permute-start | bytes 417800 | tf_op jit(solution)/shard_map/ppermute | solution.py:483
  139.2 1.1 collective-permute-start.24
  140.4 0.2 collective-permute-done.22.refs_2_
  140.7 2.9 %collective-permute-done.23.refs_3_ = f32[2,136,128]{2,1,0:T(8,128)S(1)} collective-permute-done((f32[2,136,128]{2,1,0:T(8,128)S(1)}, f32[2,136,128]{2,1,0:T(8,128)S(1)}, u32[]{:S(2)}, u32[]{:S(2)}) %collective-permute-start.23) | collective-permute-done | bytes 139296 | tf_op jit(solution)/shard_map/ppermute | solution.py:483
  143.6 1.6 %finish.1 = (f32[2,1024,128]{2,1,0:T(8,128)}, f32[2,8,128]{2,1,0:T(8,128)S(1)}) custom-call(s32[3]{0:T(128)S(1)} %pad_add_fusion.ids_ref, f32[2,64,1024]{2,1,0:T(8,128)S(1)} %pad_maximum_fusion.ahead_ref, f32[2,136,128]{2,1,0:T(8,128)S(1)} %get-tuple-element.62.refs_0_, f32[2,136,128]{2,1,0:T(8,128)S(1)} %collective-permute-done.21.refs_1_, ...), custom_call_target="tpu_custom_call" | custom-call | bytes 2228224 | tf_op jit(solution)/shard_map/finish/pallas_call | solution.py:236
  145.1 0.1 collective-permute-start.25
  145.2 1.2 collective-permute-done.25
  146.4 0.6 fusion.5
  147.0 4.9 %collective-permute-done.24 = f32[1,64,1024]{2,1,0:T(8,128)S(1)} collective-permute-done((f32[1,64,1024]{2,1,0:T(8,128)S(1)}, f32[1,64,1024]{2,1,0:T(8,128)S(1)}, u32[]{:S(2)}, u32[]{:S(2)}) %collective-permute-start.24) | collective-permute-done | bytes 262176 | tf_op jit(solution)/shard_map/ppermute | solution.py:483
  151.9 0.7 fusion.3
  (57 shorter events, 0.3 us)
Async XLA Ops:
  0.6 1.0 copy-start
  0.6 11.0 %collective-permute-start = (f32[2048,128]{1,0:T(8,128)}, f32[2048,128]{1,0:T(8,128)S(1)}, u32[]{:S(2)}, u32[]{:S(2)}) collective-permute-start(f32[2048,128]{1,0:T(8,128)} %own_ref.1), channel_id=1, source_target_pairs={{0,1},{1,0},{2,3},{3,2},{4,5},{5,4},{6,7},{7,6},{8,9},{9,8},{10,11... | collective-permute-start | bytes 3145736 | tf_op jit(solution)/shard_map/ppermute | solution.py:477
  1.6 16.2 %collective-permute-start.4 = (f32[1,32,1024]{2,1,0:T(8,128)S(1)}, f32[1,32,1024]{2,1,0:T(8,128)S(1)}, u32[]{:S(2)}, u32[]{:S(2)}) collective-permute-start(f32[1,32,1024]{2,1,0:T(8,128)S(1)} %dynamic-slice_bitcast_fusion), channel_id=1, source_target_pairs={{0,12},{2,14},{4,8},{6,10},{8,4},{10,6},{12,0},{14,2},{1,13},{3,15... | collective-permute-start | bytes 393224 | tf_op jit(solution)/shard_map/ppermute | solution.py:483
  6.7 11.1 %collective-permute-start.3 = (f32[1,32,1024]{2,1,0:T(8,128)S(1)}, f32[1,32,1024]{2,1,0:T(8,128)S(1)}, u32[]{:S(2)}, u32[]{:S(2)}) collective-permute-start(f32[1,32,1024]{2,1,0:T(8,128)S(1)} %dynamic-slice_bitcast_fusion), channel_id=1, source_target_pairs={{0,8},{2,10},{4,12},{6,14},{8,0},{10,2},{12,4},{14,6},{1,9},{3,11}... | collective-permute-start | bytes 393224 | tf_op jit(solution)/shard_map/ppermute | solution.py:483
  6.7 9.6 %collective-permute-start.2 = (f32[1,32,1024]{2,1,0:T(8,128)S(1)}, f32[1,32,1024]{2,1,0:T(8,128)S(1)}, u32[]{:S(2)}, u32[]{:S(2)}) collective-permute-start(f32[1,32,1024]{2,1,0:T(8,128)S(1)} %dynamic-slice_bitcast_fusion), channel_id=1, source_target_pairs={{0,4},{2,6},{4,0},{6,2},{8,12},{10,14},{12,8},{14,10},{1,5},{3,7},... | collective-permute-start | bytes 393224 | tf_op jit(solution)/shard_map/ppermute | solution.py:483
  7.4 2.4 %copy-start.7 = (f32[16,16]{1,0:T(8,128)S(1)}, f32[16,16]{1,0:T(8,128)}, u32[]{:S(2)}) copy-start(f32[16,16]{1,0:T(8,128)} %w_ref.1) | copy-start | bytes 3076
  7.4 4.2 %copy-start.18 = (f32[256,256]{1,0:T(8,128)S(1)}, f32[256,256]{1,0:T(8,128)}, u32[]{:S(2)}) copy-start(f32[256,256]{1,0:T(8,128)} %param.11) | copy-start | bytes 786436
  17.8 36.7 %copy-start.10 = (f32[4,32,1024]{2,1,0:T(8,128)}, f32[4,32,1024]{2,1,0:T(8,128)S(1)}, u32[]{:S(2)}) copy-start(f32[4,32,1024]{2,1,0:T(8,128)S(1)} %constant_dynamic-update-slice_fusion.refs_0_) | copy-start | bytes 1572868
  17.8 30.0 %copy-start.5 = (bf16[256,256]{1,0:T(8,128)(2,1)S(1)}, bf16[256,256]{1,0:T(8,128)(2,1)}, u32[]{:S(2)}) copy-start(bf16[256,256]{1,0:T(8,128)(2,1)} %get-tuple-element.46.kh) | copy-start | bytes 393220
  17.9 30.0 %copy-start.6 = (bf16[256,256]{1,0:T(8,128)(2,1)S(1)}, bf16[256,256]{1,0:T(8,128)(2,1)}, u32[]{:S(2)}) copy-start(bf16[256,256]{1,0:T(8,128)(2,1)} %get-tuple-element.47.kl) | copy-start | bytes 393220
  17.9 30.0 %all-to-all-start = ((f32[8,2,128,128]{3,2,1,0:T(8,128)}), f32[8,2,128,128]{3,2,1,0:T(8,128)S(1)}, u32[]{:S(2)}, u32[]{:S(2)}) async-start(f32[8,2,128,128]{3,2,1,0:T(8,128)} %bitcast.21), calls=%async_computation | async-start | bytes 2097152 | tf_op jit(solution)/shard_map/all_to_all | solution.py:486
  22.7 12.5 %collective-permute-start.6 = (f32[4,32,1024]{2,1,0:T(8,128)S(1)}, f32[4,32,1024]{2,1,0:T(8,128)S(1)}, u32[]{:S(2)}, u32[]{:S(2)}) collective-permute-start(f32[4,32,1024]{2,1,0:T(8,128)S(1)} %constant_dynamic-update-slice_fusion.refs_0_), channel_id=1, source_target_pairs={{0,16},{16,0},{1,17},{17,1},{2,18},{18,2},{3,19},{19,3},{4,20},{20... | collective-permute-start | bytes 1572872 | tf_op jit(solution)/shard_map/ppermute | solution.py:480
  24.2 22.5 %collective-permute-start.5 = (f32[4,32,1024]{2,1,0:T(8,128)S(1)}, f32[4,32,1024]{2,1,0:T(8,128)S(1)}, u32[]{:S(2)}, u32[]{:S(2)}) collective-permute-start(f32[4,32,1024]{2,1,0:T(8,128)S(1)} %constant_dynamic-update-slice_fusion.refs_0_), channel_id=1, source_target_pairs={{0,2},{2,0},{4,6},{6,4},{8,10},{10,8},{12,14},{14,12},{1,3},{3,1},... | collective-permute-start | bytes 1572872 | tf_op jit(solution)/shard_map/ppermute | solution.py:483
  26.2 20.4 %collective-permute-start.1 = (f32[2,8,64,128]{3,2,1,0:T(8,128)}, f32[2,8,64,128]{3,2,1,0:T(8,128)}, u32[]{:S(2)}, u32[]{:S(2)}) collective-permute-start(f32[2,8,64,128]{3,2,1,0:T(8,128)} %get-tuple-element.45), channel_id=1, source_target_pairs={{0,1},{1,0},{2,3},{3,2},{4,5},{5,4},{6,7},{7,6},{8,9},{9,8},{10,11... | collective-permute-start | bytes 1572872 | tf_op jit(solution)/shard_map/ppermute | solution.py:477
  35.2 19.3 %copy-start.11 = (f32[4,32,1024]{2,1,0:T(8,128)}, f32[4,32,1024]{2,1,0:T(8,128)S(1)}, u32[]{:S(2)}) copy-start(f32[4,32,1024]{2,1,0:T(8,128)S(1)} %collective-permute-done.6.refs_2_) | copy-start | bytes 1572868
  46.7 2.7 %copy-start.12 = (f32[4,32,1024]{2,1,0:T(8,128)}, f32[4,32,1024]{2,1,0:T(8,128)S(1)}, u32[]{:S(2)}) copy-start(f32[4,32,1024]{2,1,0:T(8,128)S(1)} %collective-permute-done.5.refs_1_) | copy-start | bytes 1572868
  49.4 29.4 %all-to-all-start.1 = ((f32[8,2,128,128]{3,2,1,0:T(8,128)}), f32[8,2,128,128]{3,2,1,0:T(8,128)S(1)}, u32[]{:S(2)}, u32[]{:S(2)}) async-start(f32[8,2,128,128]{3,2,1,0:T(8,128)} %bitcast.7), calls=%async_computation.1 | async-start | bytes 2097152 | tf_op jit(solution)/shard_map/all_to_all | solution.py:486
  53.0 13.6 %collective-permute-start.7 = (f32[4,32,1024]{2,1,0:T(8,128)}, f32[4,32,1024]{2,1,0:T(8,128)S(1)}, u32[]{:S(2)}, u32[]{:S(2)}) collective-permute-start(f32[4,32,1024]{2,1,0:T(8,128)} %copy-done.12), channel_id=1, source_target_pairs={{0,16},{16,0},{1,17},{17,1},{2,18},{18,2},{3,19},{19,3},{4,20},{20... | collective-permute-start | bytes 1572872 | tf_op jit(solution)/shard_map/ppermute | solution.py:480
  54.5 12.1 %collective-permute-start.8 = (f32[4,32,1024]{2,1,0:T(8,128)S(1)}, f32[4,32,1024]{2,1,0:T(8,128)S(1)}, u32[]{:S(2)}, u32[]{:S(2)}) collective-permute-start(f32[4,32,1024]{2,1,0:T(8,128)S(1)} %constant_dynamic-update-slice_fusion.refs_0_), channel_id=1, source_target_pairs={{0,1},{1,0},{2,3},{3,2},{4,5},{5,4},{6,7},{7,6},{8,9},{9,8},{10,11... | collective-permute-start | bytes 1572872 | tf_op jit(solution)/shard_map/ppermute | solution.py:477
  54.6 12.1 %collective-permute-start.10 = (f32[4,32,1024]{2,1,0:T(8,128)S(1)}, f32[4,32,1024]{2,1,0:T(8,128)S(1)}, u32[]{:S(2)}, u32[]{:S(2)}) collective-permute-start(f32[4,32,1024]{2,1,0:T(8,128)S(1)} %collective-permute-done.6.refs_2_), channel_id=1, source_target_pairs={{0,1},{1,0},{2,3},{3,2},{4,5},{5,4},{6,7},{7,6},{8,9},{9,8},{10,11... | collective-permute-start | bytes 1572872 | tf_op jit(solution)/shard_map/ppermute | solution.py:477
  55.1 11.6 %collective-permute-start.9 = (f32[4,32,1024]{2,1,0:T(8,128)}, f32[4,32,1024]{2,1,0:T(8,128)S(1)}, u32[]{:S(2)}, u32[]{:S(2)}) collective-permute-start(f32[4,32,1024]{2,1,0:T(8,128)} %copy-done.12), channel_id=1, source_target_pairs={{0,1},{1,0},{2,3},{3,2},{4,5},{5,4},{6,7},{7,6},{8,9},{9,8},{10,11... | collective-permute-start | bytes 1572872 | tf_op jit(solution)/shard_map/ppermute | solution.py:477
  66.6 1.9 %copy-start.13 = (f32[4,32,1024]{2,1,0:T(8,128)}, f32[4,32,1024]{2,1,0:T(8,128)S(1)}, u32[]{:S(2)}) copy-start(f32[4,32,1024]{2,1,0:T(8,128)S(1)} %collective-permute-done.7.refs_3_) | copy-start | bytes 1572868
  66.6 1.9 %collective-permute-start.11 = (f32[4,32,1024]{2,1,0:T(8,128)S(1)}, f32[4,32,1024]{2,1,0:T(8,128)S(1)}, u32[]{:S(2)}, u32[]{:S(2)}) collective-permute-start(f32[4,32,1024]{2,1,0:T(8,128)S(1)} %collective-permute-done.7.refs_3_), channel_id=1, source_target_pairs={{0,1},{1,0},{2,3},{3,2},{4,5},{5,4},{6,7},{7,6},{8,9},{9,8},{10,11... | collective-permute-start | bytes 1572872 | tf_op jit(solution)/shard_map/ppermute | solution.py:477
  66.6 1.9 %copy-start.14 = (f32[4,32,1024]{2,1,0:T(8,128)}, f32[4,32,1024]{2,1,0:T(8,128)S(1)}, u32[]{:S(2)}) copy-start(f32[4,32,1024]{2,1,0:T(8,128)S(1)} %collective-permute-done.8.refs_4_) | copy-start | bytes 1572868
  66.7 1.9 %copy-start.15 = (f32[4,32,1024]{2,1,0:T(8,128)}, f32[4,32,1024]{2,1,0:T(8,128)S(1)}, u32[]{:S(2)}) copy-start(f32[4,32,1024]{2,1,0:T(8,128)S(1)} %collective-permute-done.10.refs_6_) | copy-start | bytes 1572868
  66.7 1.9 %copy-start.16 = (f32[4,32,1024]{2,1,0:T(8,128)}, f32[4,32,1024]{2,1,0:T(8,128)S(1)}, u32[]{:S(2)}) copy-start(f32[4,32,1024]{2,1,0:T(8,128)S(1)} %collective-permute-done.9.refs_5_) | copy-start | bytes 1572868
  68.5 0.8 copy-start.17
  78.8 29.7 %all-to-all-start.2 = ((f32[8,2,128,128]{3,2,1,0:T(8,128)}), f32[8,2,128,128]{3,2,1,0:T(8,128)S(1)}, u32[]{:S(2)}, u32[]{:S(2)}) async-start(f32[8,2,128,128]{3,2,1,0:T(8,128)} %up.1), calls=%async_computation.2 | async-start | bytes 2097152 | tf_op jit(solution)/shard_map/all_to_all | solution.py:486
  82.4 2.7 %collective-permute-start.12 = (f32[8,2,128,128]{3,2,1,0:T(8,128)S(1)}, f32[8,2,128,128]{3,2,1,0:T(8,128)S(1)}, u32[]{:S(2)}, u32[]{:S(2)}) collective-permute-start(f32[8,2,128,128]{3,2,1,0:T(8,128)S(1)} %all-to-all-done.1.va_ref.v_ref), channel_id=1, source_target_pairs={{0,1},{1,0},{2,3},{3,2},{4,5},{5,4},{6,7},{7,6},{8,9},{9,8},{10,11... | collective-permute-start | bytes 3145736 | tf_op jit(solution)/shard_map/ppermute | solution.py:477
  89.7 0.8 copy-start.1
  90.5 0.9 copy-start.3
  91.4 22.1 %collective-permute-start.14 = (f32[4,32,1024]{2,1,0:T(8,128)}, f32[4,32,1024]{2,1,0:T(8,128)}, u32[]{:S(2)}, u32[]{:S(2)}) collective-permute-start(f32[4,32,1024]{2,1,0:T(8,128)} %get-tuple-element.56), channel_id=1, source_target_pairs={{0,4},{2,6},{4,0},{6,2},{8,12},{10,14},{12,8},{14,10},{1,5},{3,7},... | collective-permute-start | bytes 1572872 | tf_op jit(solution)/shard_map/ppermute | solution.py:483
  93.4 20.1 %collective-permute-start.13 = (f32[4,32,1024]{2,1,0:T(8,128)}, f32[4,32,1024]{2,1,0:T(8,128)}, u32[]{:S(2)}, u32[]{:S(2)}) collective-permute-start(f32[4,32,1024]{2,1,0:T(8,128)} %get-tuple-element.55), channel_id=1, source_target_pairs={{0,2},{2,0},{4,6},{6,4},{8,10},{10,8},{12,14},{14,12},{1,3},{3,1},... | collective-permute-start | bytes 1572872 | tf_op jit(solution)/shard_map/ppermute | solution.py:483
  94.9 13.6 %copy-start.8 = (bf16[256,256]{1,0:T(8,128)(2,1)S(1)}, bf16[256,256]{1,0:T(8,128)(2,1)}, u32[]{:S(2)}) copy-start(bf16[256,256]{1,0:T(8,128)(2,1)} %get-tuple-element.57.kh) | copy-start | bytes 393220
  108.5 0.9 copy-start.9
  109.4 4.1 %copy-start.2 = (f32[4,32,1024]{2,1,0:T(8,128)S(1)}, f32[4,32,1024]{2,1,0:T(8,128)}, u32[]{:S(2)}) copy-start(f32[4,32,1024]{2,1,0:T(8,128)} %copy-done.1) | copy-start | bytes 1572868
  109.4 4.1 %copy-start.4 = (f32[4,32,1024]{2,1,0:T(8,128)S(1)}, f32[4,32,1024]{2,1,0:T(8,128)}, u32[]{:S(2)}) copy-start(f32[4,32,1024]{2,1,0:T(8,128)} %copy-done.3) | copy-start | bytes 1572868
  111.2 9.9 %collective-permute-start.17 = (f32[2,136,128]{2,1,0:T(8,128)S(1)}, f32[2,136,128]{2,1,0:T(8,128)S(1)}, u32[]{:S(2)}, u32[]{:S(2)}) collective-permute-start(f32[2,136,128]{2,1,0:T(8,128)S(1)} %get-tuple-element.69), channel_id=1, source_target_pairs={{0,8},{2,10},{4,12},{6,14},{8,0},{10,2},{12,4},{14,6},{1,9},{3,11}... | collective-permute-start | bytes 417800 | tf_op jit(solution)/shard_map/ppermute | solution.py:483
  114.8 24.3 %collective-permute-start.15 = (f32[2,32,1024]{2,1,0:T(8,128)S(1)}, f32[2,32,1024]{2,1,0:T(8,128)S(1)}, u32[]{:S(2)}, u32[]{:S(2)}) collective-permute-start(f32[2,32,1024]{2,1,0:T(8,128)S(1)} %get-tuple-element.67), channel_id=1, source_target_pairs={{0,4},{2,6},{4,0},{6,2},{8,12},{10,14},{12,8},{14,10},{1,5},{3,7},... | collective-permute-start | bytes 786440 | tf_op jit(solution)/shard_map/ppermute | solution.py:483
  116.1 23.0 %collective-permute-start.16 = (f32[2,32,1024]{2,1,0:T(8,128)S(1)}, f32[2,32,1024]{2,1,0:T(8,128)S(1)}, u32[]{:S(2)}, u32[]{:S(2)}) collective-permute-start(f32[2,32,1024]{2,1,0:T(8,128)S(1)} %get-tuple-element.68), channel_id=1, source_target_pairs={{0,2},{2,0},{4,6},{6,4},{8,10},{10,8},{12,14},{14,12},{1,3},{3,1},... | collective-permute-start | bytes 786440 | tf_op jit(solution)/shard_map/ppermute | solution.py:483
  117.2 16.7 %collective-permute-start.18 = (f32[2,136,128]{2,1,0:T(8,128)S(1)}, f32[2,136,128]{2,1,0:T(8,128)S(1)}, u32[]{:S(2)}, u32[]{:S(2)}) collective-permute-start(f32[2,136,128]{2,1,0:T(8,128)S(1)} %get-tuple-element.70), channel_id=1, source_target_pairs={{0,10},{2,8},{4,14},{6,12},{8,2},{10,0},{12,6},{14,4},{1,11},{3,9}... | collective-permute-start | bytes 417800 | tf_op jit(solution)/shard_map/ppermute | solution.py:483
  119.7 14.9 %collective-permute-start.19 = (f32[2,136,128]{2,1,0:T(8,128)S(1)}, f32[2,136,128]{2,1,0:T(8,128)S(1)}, u32[]{:S(2)}, u32[]{:S(2)}) collective-permute-start(f32[2,136,128]{2,1,0:T(8,128)S(1)} %get-tuple-element.71), channel_id=1, source_target_pairs={{0,12},{2,14},{4,8},{6,10},{8,4},{10,6},{12,0},{14,2},{1,13},{3,15... | collective-permute-start | bytes 417800 | tf_op jit(solution)/shard_map/ppermute | solution.py:483
  121.1 15.5 %collective-permute-start.20 = (f32[2,136,128]{2,1,0:T(8,128)S(1)}, f32[2,136,128]{2,1,0:T(8,128)S(1)}, u32[]{:S(2)}, u32[]{:S(2)}) collective-permute-start(f32[2,136,128]{2,1,0:T(8,128)S(1)} %get-tuple-element.72), channel_id=1, source_target_pairs={{0,14},{2,12},{4,10},{6,8},{8,6},{10,4},{12,2},{14,0},{1,15},{3,13... | collective-permute-start | bytes 417800 | tf_op jit(solution)/shard_map/ppermute | solution.py:483
  133.8 6.6 %collective-permute-start.21 = (f32[2,136,128]{2,1,0:T(8,128)S(1)}, f32[2,136,128]{2,1,0:T(8,128)S(1)}, u32[]{:S(2)}, u32[]{:S(2)}) collective-permute-start(f32[2,136,128]{2,1,0:T(8,128)S(1)} %get-tuple-element.77), channel_id=1, source_target_pairs={{0,2},{2,0},{4,6},{6,4},{8,10},{10,8},{12,14},{14,12},{1,3},{3,1},... | collective-permute-start | bytes 417800 | tf_op jit(solution)/shard_map/ppermute | solution.py:483
  134.6 6.0 %collective-permute-start.22 = (f32[2,136,128]{2,1,0:T(8,128)S(1)}, f32[2,136,128]{2,1,0:T(8,128)S(1)}, u32[]{:S(2)}, u32[]{:S(2)}) collective-permute-start(f32[2,136,128]{2,1,0:T(8,128)S(1)} %get-tuple-element.79), channel_id=1, source_target_pairs={{0,4},{2,6},{4,0},{6,2},{8,12},{10,14},{12,8},{14,10},{1,5},{3,7},... | collective-permute-start | bytes 417800 | tf_op jit(solution)/shard_map/ppermute | solution.py:483
  136.6 7.0 %collective-permute-start.23 = (f32[2,136,128]{2,1,0:T(8,128)S(1)}, f32[2,136,128]{2,1,0:T(8,128)S(1)}, u32[]{:S(2)}, u32[]{:S(2)}) collective-permute-start(f32[2,136,128]{2,1,0:T(8,128)S(1)} %get-tuple-element.81), channel_id=1, source_target_pairs={{0,6},{2,4},{4,2},{6,0},{8,14},{10,12},{12,10},{14,8},{1,7},{3,5},... | collective-permute-start | bytes 417800 | tf_op jit(solution)/shard_map/ppermute | solution.py:483
  139.2 12.6 %collective-permute-start.24 = (f32[1,64,1024]{2,1,0:T(8,128)S(1)}, f32[1,64,1024]{2,1,0:T(8,128)S(1)}, u32[]{:S(2)}, u32[]{:S(2)}) collective-permute-start(f32[1,64,1024]{2,1,0:T(8,128)S(1)} %fusion.4), channel_id=1, source_target_pairs={{0,8},{2,10},{4,12},{6,14},{8,0},{10,2},{12,4},{14,6},{1,9},{3,11}... | collective-permute-start | bytes 786440 | tf_op jit(solution)/shard_map/ppermute | solution.py:483
  145.1 1.2 collective-permute-start.25
